TPU v7x, 32 devices: a whole 2x2x4 slice. The times are simulated.
32 devices in a mesh: dir: 2 (over x), dp: 16 (over z, y, core).
Axes of the slice: x: 2, y: 2, z: 4, core: 2. Of those that a mesh axis runs over, the one named last changes fastest.
Arguments:
- tokens: bfloat16 [2048, 1536], P('dp'), may hold values from -6 to 6
- item_grids: int32 [32, 2], P('dp'), may hold values from 0 to 16, as said below
- norm_gain: bfloat16 [1536], P('dp'), may hold values from 0.099609375 to 1.8984375
- proj_in_x: bfloat16 [1536, 3072], P(None, 'dp'), may hold values from -0.15625 to 0.15625
- proj_in_z: bfloat16 [1536, 3072], P(None, 'dp'), may hold values from -0.15625 to 0.15625
- proj_out: bfloat16 [3072, 1536], P(None, 'dp'), may hold values from -0.109375 to 0.109375
- conv_weight: bfloat16 [2, 4, 3072], P('dir', None, 'dp'), may hold values from -3 to 3
- conv_bias: bfloat16 [2, 3072], P('dir', 'dp'), may hold values from -0.5 to 0.5
- proj_state: bfloat16 [2, 3072, 128], P('dir', 'dp'), may hold values from -0.109375 to 0.109375
- proj_step: bfloat16 [2, 96, 3072], P('dir', None, 'dp'), may hold values from -0.625 to 0.625
- step_bias: bfloat16 [2, 3072], P('dir', 'dp'), may hold values from -4 to -1
- decay_log: bfloat16 [2, 16, 3072], P('dir', None, 'dp'), may hold values from 0 to 2.796875
- skip_gain: bfloat16 [2, 3072], P('dir', 'dp'), may hold values from 0.5 to 1.5
- grad_out: bfloat16 [16, 2, 64, 1536], P('dp', 'dir'), may hold values from -6 to 6
Outputs:
- mixed: bfloat16 [16, 2, 64, 1536], P('dp', 'dir')
- grad_tokens: float32 [16, 2, 64, 1536], P('dp', 'dir')
- grad_norm_gain: float32 [1536], P(('dir', 'dp'))
- grad_proj_in_x: float32 [1536, 3072], P('dir', 'dp')
- grad_proj_in_z: float32 [1536, 3072], P('dir', 'dp')
- grad_proj_out: float32 [3072, 1536], P('dir', 'dp')
- grad_conv_weight: float32 [2, 4, 3072], P('dir', None, 'dp')
- grad_conv_bias: float32 [2, 3072], P('dir', 'dp')
- grad_proj_state: float32 [2, 3072, 128], P('dir', 'dp')
- grad_proj_step: float32 [2, 96, 3072], P('dir', None, 'dp')
- grad_step_bias: float32 [2, 3072], P('dir', 'dp')
- grad_decay_log: float32 [2, 16, 3072], P('dir', None, 'dp')
- grad_skip_gain: float32 [2, 3072], P('dir', 'dp')
Inputs may be any that keep to these rules, and one draw needn't show every extreme that they name: `item_grids`: rows 2p and 2p + 1 are the height and width of the items packed in order into the 128 token slots of index p of dp; an unused row is (0, 0); the lengths of a pack add up to at most 128, and some pack is filled completely.
All inputs are finite; a program needn't handle non-finite values.
Results may differ from a plain program's by a relative error of at most 0.013.
Values may be sent and summed in bfloat16 or wider, within the bound.
A program may use at most 320 MiB of HBM per device.

v0:
```python
from functools import partial

import jax
import jax.numpy as jnp
from jax import lax
from jax.sharding import PartitionSpec as P

DT_RANK = 96
BLOCK = 32


epsilon = 1e-05


def matmul(left, right):
    return jnp.dot(left, right, preferred_element_type=jnp.float32)


def inner_rows(left, right):
    return lax.dot_general(
        left, right, (((0,), (0,)), ((), ())), preferred_element_type=jnp.float32
    )


def outer_rows(left, right):
    return lax.dot_general(
        left, right, (((1,), (1,)), ((), ())), preferred_element_type=jnp.float32
    )


def segments(grid_rows, length):
    first_end = grid_rows[0, 0] * grid_rows[0, 1]
    second = first_end + grid_rows[1, 0] * grid_rows[1, 1]
    position = jnp.arange(length, dtype=jnp.int32)
    return (position >= first_end).astype(jnp.int32) + (position >= second).astype(jnp.int32)


def carry_mask(segment_ids, dtype):
    matching = (segment_ids[1:] == segment_ids[:-1]).astype(dtype)
    return jnp.concatenate([jnp.zeros((1,), dtype), matching], 0)


def conv_act(conv_in, kernel_rows, kernel_offset, segment_ids):
    kernel_len = kernel_rows.shape[0]
    length = conv_in.shape[0]
    summed = kernel_offset[None, :] + kernel_rows[kernel_len - 1][None, :] * conv_in
    for offset in range(1, kernel_len):
        shifted = jnp.concatenate(
            [jnp.zeros((offset, conv_in.shape[1]), conv_in.dtype), conv_in[: length - offset]], 0
        )
        earlier_ids = jnp.concatenate(
            [jnp.full((offset,), -1, jnp.int32), segment_ids[: length - offset]], 0
        )
        matching = (earlier_ids == segment_ids).astype(conv_in.dtype)
        summed = (
            summed + kernel_rows[kernel_len - 1 - offset][None, :] * shifted * matching[:, None]
        )
    return jax.nn.silu(summed)


def combine(earlier, latter):
    return (earlier[0] * latter[0], latter[0] * earlier[1] + latter[1])


def scan_block(decay_rate, state_in, block_data):
    step_size, values, state_io, keep_mask = block_data
    states = decay_rate.shape[0]
    factor = jnp.exp(step_size[:, None, :] * decay_rate[None]) * keep_mask[:, None, None]
    inject = (step_size * values)[:, None, :] * state_io[:, :states, None]
    total_a, total_b = lax.associative_scan(combine, (factor, inject), axis=0)
    hidden = total_a * state_in[None] + total_b
    readout = jnp.sum(hidden * state_io[:, states:, None], axis=1)
    return (hidden[-1], readout)


def mixer_scan(values, step_input, state_io, bias_row, log_rate, skip_row, keep_mask, block_len):
    step_size = jax.nn.softplus(step_input + bias_row[None, :])
    decay_rate = -jnp.exp(log_rate)
    length, channels = values.shape
    blocks = length // block_len
    shaped = (
        step_size.reshape(blocks, block_len, channels),
        values.reshape(blocks, block_len, channels),
        state_io.reshape(blocks, block_len, state_io.shape[1]),
        keep_mask.reshape(blocks, block_len),
    )
    initial = jnp.zeros(decay_rate.shape, values.dtype)
    _, readout = lax.scan(jax.checkpoint(partial(scan_block, decay_rate)), initial, shaped)
    return readout.reshape(length, channels) + skip_row[None, :] * values


def local(
    tokens,
    item_grids,
    norm_gain,
    proj_in_x,
    proj_in_z,
    proj_out,
    conv_weight,
    conv_bias,
    proj_state,
    proj_step,
    step_bias,
    decay_log,
    skip_gain,
    grad_out,
):
    length = tokens.shape[0]
    half_rows = length // 2
    direction = lax.axis_index("dir")
    flipped = direction == 1

    def orient(array):
        return jnp.where(flipped, jnp.flip(array, 0), array)

    gathered = (
        lax.all_gather(norm_gain, "dp", axis=0, tiled=True),
        lax.all_gather(proj_in_x, "dp", axis=1, tiled=True),
        lax.all_gather(proj_in_z, "dp", axis=1, tiled=True),
        lax.all_gather(proj_out, "dp", axis=1, tiled=True),
        lax.all_gather(conv_weight, "dp", axis=2, tiled=True),
        lax.all_gather(conv_bias, "dp", axis=1, tiled=True),
        lax.all_gather(proj_state, "dp", axis=1, tiled=True),
        lax.all_gather(proj_step, "dp", axis=2, tiled=True),
        lax.all_gather(step_bias, "dp", axis=1, tiled=True),
        lax.all_gather(decay_log, "dp", axis=2, tiled=True),
        lax.all_gather(skip_gain, "dp", axis=1, tiled=True),
    )
    (
        gain_full,
        weight_x,
        weight_z,
        weight_out,
        kernel,
        kernel_bias,
        weight_state,
        weight_step,
        bias_step,
        log_decay,
        skip_full,
    ) = gathered
    inputs = tokens.astype(jnp.float32)
    inv_rms = lax.rsqrt(jnp.mean(inputs * inputs, axis=1, keepdims=True) + epsilon)
    unit_rows = inputs * inv_rms
    gain_rows = gain_full.astype(jnp.float32)
    normed = (unit_rows * gain_rows[None, :]).astype(jnp.bfloat16)
    segment_ids = orient(segments(item_grids, length))
    keep_mask = carry_mask(segment_ids, jnp.float32)
    normed_dir = orient(normed)
    conv_input = matmul(normed_dir, weight_x)
    kernel_rows = kernel[0].astype(jnp.float32)
    kernel_offset = kernel_bias[0].astype(jnp.float32)

    def conv_piece(conv_in, taps, offsets):
        return conv_act(conv_in, taps, offsets, segment_ids)

    act_value, conv_back = jax.vjp(conv_piece, conv_input, kernel_rows, kernel_offset)
    conv_out = act_value.astype(jnp.bfloat16)
    projected = matmul(conv_out, weight_state[0])
    rank_input = projected[:, :DT_RANK].astype(jnp.bfloat16)
    state_io = projected[:, DT_RANK:]
    step_input = matmul(rank_input, weight_step[0])

    def scan_piece(values, step_in, io_rows, bias_row, log_rate, skip_row):
        return mixer_scan(values, step_in, io_rows, bias_row, log_rate, skip_row, keep_mask, BLOCK)

    scan_out, scan_back = jax.vjp(
        scan_piece,
        conv_out.astype(jnp.float32),
        step_input,
        state_io,
        bias_step[0].astype(jnp.float32),
        log_decay[0].astype(jnp.float32),
        skip_full[0].astype(jnp.float32),
    )
    summed = lax.psum_scatter(
        orient(scan_out).astype(jnp.bfloat16), "dir", scatter_dimension=0, tiled=True
    ).astype(jnp.float32)
    own_start = direction * half_rows
    normed_half = lax.dynamic_slice_in_dim(normed, own_start, half_rows, 0)
    inputs_half = lax.dynamic_slice_in_dim(inputs, own_start, half_rows, 0)
    unit_half = lax.dynamic_slice_in_dim(unit_rows, own_start, half_rows, 0)
    inv_half = lax.dynamic_slice_in_dim(inv_rms, own_start, half_rows, 0)
    gate_input = matmul(normed_half, weight_z)
    gate_sig = jax.nn.sigmoid(gate_input)
    gate_act = gate_input * gate_sig
    gated = (summed * gate_act).astype(jnp.bfloat16)
    mixed = (matmul(gated, weight_out) + inputs_half).astype(jnp.bfloat16)
    weight_x, weight_z, weight_out, weight_state, weight_step = (
        lax.all_gather(proj_in_x, "dp", axis=1, tiled=True),
        lax.all_gather(proj_in_z, "dp", axis=1, tiled=True),
        lax.all_gather(proj_out, "dp", axis=1, tiled=True),
        lax.all_gather(proj_state, "dp", axis=1, tiled=True),
        lax.all_gather(proj_step, "dp", axis=2, tiled=True),
    )
    cotangent = grad_out.reshape(half_rows, grad_out.shape[-1])
    grad_gated = outer_rows(cotangent, weight_out)
    grad_summed = grad_gated * gate_act
    grad_gate_in = (grad_gated * summed * gate_sig * (1.0 + gate_input * (1.0 - gate_sig))).astype(
        jnp.bfloat16
    )
    grad_normed_z = outer_rows(grad_gate_in, weight_z)
    grad_scan = orient(
        lax.all_gather(grad_summed.astype(jnp.bfloat16), "dir", axis=0, tiled=True).astype(
            grad_summed.dtype
        )
    )
    grad_values, grad_step_in, grad_state_io, grad_bias_step, grad_log_decay, grad_skip = scan_back(
        grad_scan
    )
    grad_step_low = grad_step_in.astype(jnp.bfloat16)
    grad_weight_step = inner_rows(rank_input, grad_step_low)
    grad_rank = outer_rows(grad_step_low, weight_step[0])
    grad_projected = jnp.concatenate([grad_rank, grad_state_io], axis=1).astype(jnp.bfloat16)
    grad_weight_state = inner_rows(conv_out, grad_projected)
    grad_conv_out = grad_values + outer_rows(grad_projected, weight_state[0])
    grad_conv_in, grad_kernel, grad_kernel_bias = conv_back(grad_conv_out)
    grad_conv_low = grad_conv_in.astype(jnp.bfloat16)
    grad_normed_x = orient(outer_rows(grad_conv_low, weight_x))
    grad_normed = (
        lax.psum_scatter(
            grad_normed_x.astype(jnp.bfloat16), "dir", scatter_dimension=0, tiled=True
        ).astype(jnp.float32)
        + grad_normed_z
    )
    grad_scaled = grad_normed * gain_rows[None, :]
    grad_inputs = inv_half * (
        grad_scaled - unit_half * jnp.mean(grad_scaled * unit_half, axis=1, keepdims=True)
    )
    grad_inputs = grad_inputs + cotangent.astype(jnp.float32)
    grad_gain = jnp.sum(grad_normed * unit_half, axis=0)
    gain_part = lax.psum_scatter(grad_gain, ("dir", "dp"), scatter_dimension=0, tiled=True)
    conv_slots = orient(grad_conv_low)
    both_conv, gated_full, gate_grad_full, cot_full = (
        lax.all_gather(conv_slots, "dir", axis=0, tiled=True),
        lax.all_gather(gated, "dir", axis=0, tiled=True),
        lax.all_gather(grad_gate_in, "dir", axis=0, tiled=True),
        lax.all_gather(cotangent, "dir", axis=0, tiled=True),
    )
    features = normed.shape[1]
    channels = gated.shape[1]
    feature_half = features // 2
    channel_half = channels // 2
    normed_cols = lax.dynamic_slice_in_dim(normed, direction * feature_half, feature_half, 1)
    gated_cols = lax.dynamic_slice_in_dim(gated_full, direction * channel_half, channel_half, 1)
    part_x = inner_rows(normed_cols, both_conv[:length]) + inner_rows(
        normed_cols, both_conv[length:]
    )
    part_z = inner_rows(normed_cols, gate_grad_full)
    part_out = inner_rows(gated_cols, cot_full)
    weight_x_part, weight_z_part, weight_out_part = (
        lax.psum_scatter(part_x, "dp", scatter_dimension=1, tiled=True),
        lax.psum_scatter(part_z, "dp", scatter_dimension=1, tiled=True),
        lax.psum_scatter(part_out, "dp", scatter_dimension=1, tiled=True),
    )
    owned = (
        lax.psum_scatter(grad_kernel[None], "dp", scatter_dimension=2, tiled=True),
        lax.psum_scatter(grad_kernel_bias[None], "dp", scatter_dimension=1, tiled=True),
        lax.psum_scatter(grad_weight_state[None], "dp", scatter_dimension=1, tiled=True),
        lax.psum_scatter(grad_weight_step[None], "dp", scatter_dimension=2, tiled=True),
        lax.psum_scatter(grad_bias_step[None], "dp", scatter_dimension=1, tiled=True),
        lax.psum_scatter(grad_log_decay[None], "dp", scatter_dimension=2, tiled=True),
        lax.psum_scatter(grad_skip[None], "dp", scatter_dimension=1, tiled=True),
    )
    width = tokens.shape[1]
    return (
        mixed.reshape(1, 1, half_rows, width),
        grad_inputs.reshape(1, 1, half_rows, width),
        gain_part,
        weight_x_part,
        weight_z_part,
        weight_out_part,
        owned[0],
        owned[1],
        owned[2],
        owned[3],
        owned[4],
        owned[5],
        owned[6],
    )


def solution(mesh):
    return jax.shard_map(
        local,
        mesh=mesh,
        in_specs=(
            P("dp", None),
            P("dp", None),
            P("dp"),
            P(None, "dp"),
            P(None, "dp"),
            P(None, "dp"),
            P("dir", None, "dp"),
            P("dir", "dp"),
            P("dir", "dp", None),
            P("dir", None, "dp"),
            P("dir", "dp"),
            P("dir", None, "dp"),
            P("dir", "dp"),
            P("dp", "dir", None, None),
        ),
        out_specs=(
            P("dp", "dir", None, None),
            P("dp", "dir", None, None),
            P(("dir", "dp")),
            P("dir", "dp"),
            P("dir", "dp"),
            P("dir", "dp"),
            P("dir", None, "dp"),
            P("dir", "dp"),
            P("dir", "dp", None),
            P("dir", None, "dp"),
            P("dir", "dp"),
            P("dir", None, "dp"),
            P("dir", "dp"),
        ),
        check_vma=False,
    )
```

profile of v0, /device:TPU:0, one launch (start us, length us, event | category | flops | bytes accessed | tf_op | source)
XLA Modules:
  0.0 3691.7 jit_solution(18437102797980498872)
XLA Ops:
  12.5 64.8 %all-reduce.104 = (bf16[3072]{0:T(1024)(128)(2,1)S(1)}, bf16[1536]{0:T(1024)(128)(2,1)S(1)}, bf16[3072]{0:T(1024)(128)(2,1)}, bf16[3072]{0:T(1024)(128)(2,1)S(1)}) all-reduce(bf16[3072]{0:T(1024)(128)(2,1)S(1)} %dynamic-update-slice.2, bf16[1536]{0:T(1024)(128)(2,1)S(1)} %dynamic-update-slice.1, ...), channel_id=1, replica_groups=mesh['dir'=2,'dp'=16] {'dp'}, use_global_device_ids=true, to_apply=%add.101 | all-reduce | flops 10752 | bytes 43008
  78.1 27.8 all_gather.58
  117.8 30.1 all_gather.54
  150.4 33.7 all_gather.60
  197.8 24.2 all_gather.57
  222.0 65.0 %slice_reduce_fusion.3 = (f32[3072]{0:T(1024)}, f32[3072]{0:T(1024)S(1)}, f32[3072]{0:T(1024)}, f32[3072]{0:T(1024)}) fusion(f32[1,4,3072]{1,0,2:T(1,128)S(1)} %convert_element_type.84), kind=kLoop, calls=%fused_computation.184 | loop fusion | bytes 98304 | tf_op jit(solution)/shard_map/jvp()/slice | solution.py:46
  330.6 690.1 %while.37 = (s32[]{:T(128)}, f32[16,3072]{1,0:T(8,128)S(1)}, f32[4,32,3072]{2,1,0:T(8,128)}, f32[4,16,3072]{2,1,0:T(8,128)}, f32[4,32,3072]{2,1,0:T(8,128)}, /*i...) while((s32[]{:T(128)}, f32[16,3072]{1,0:T(8,128)S(1)}, ...), condition=%wide.region_3.4_spmd, body=%wide.region_1.3_spmd.sunk | while | flops 31014912 | bytes 374756288 | solution.py:88
  428.6 12.4 pad.1295
  446.0 12.4 pad.1296
  463.2 12.5 pad.1297
  479.6 12.4 pad.1298
  601.1 12.4 pad.1295
  618.5 12.4 pad.1296
  635.6 12.5 pad.1297
  652.1 12.4 pad.1298
  773.5 12.4 pad.1295
  790.9 12.4 pad.1296
  808.1 12.5 pad.1297
  824.5 12.4 pad.1298
  945.9 12.4 pad.1295
  963.3 12.4 pad.1296
  980.5 12.5 pad.1297
  996.9 12.4 pad.1298
  1024.8 1800.9 %while.38 = (s32[]{:T(128)}, f32[16,3072]{1,0:T(8,128)}, f32[16,3072]{1,0:T(8,128)}, f32[4,32,3072]{2,1,0:T(8,128)}, f32[4,32,3072]{2,1,0:T(8,128)}, /*index=5*/...) while((s32[]{:T(128)}, f32[16,3072]{1,0:T(8,128)}, ...), condition=%wide.region_12.13_spmd.clone, body=%wide.region_5.12_spmd.clone.sunk | while | flops 96043008 | bytes 1115715712 | solution.py:88
  1312.7 12.1 multiply_add_fusion.21
  1328.7 13.0 pad.1383
  1374.0 12.9 pad.1386
  1390.9 13.0 pad.1387
  1405.7 13.0 pad.1388
  1422.6 12.4 pad.1389
  1445.3 13.0 pad.1390
  1755.4 12.1 multiply_add_fusion.21
  1771.4 13.0 pad.1383
  1792.6 11.9 pad.1385
  1817.6 12.9 pad.1386
  1834.5 13.0 pad.1387
  1849.3 13.0 pad.1388
  1866.2 12.4 pad.1389
  1888.9 13.0 pad.1390
  2199.0 12.1 multiply_add_fusion.21
  2215.0 13.0 pad.1383
  2261.2 12.9 pad.1386
  2278.1 13.0 pad.1387
  2292.9 13.0 pad.1388
  2309.8 12.4 pad.1389
  2332.5 13.0 pad.1390
  2642.6 12.1 multiply_add_fusion.21
  2658.6 13.0 pad.1383
  2704.8 12.9 pad.1386
  2721.7 13.0 pad.1387
  2736.5 13.0 pad.1388
  2753.4 12.4 pad.1389
  2776.1 13.0 pad.1390
  2924.6 22.3 reduce-scatter.39.cloned.1.call-done
  2948.4 60.7 %reduce-scatter.43.cloned.1.call-done = f32[192,1]{1,0:T(8,128)} async-done(((f32[3072,1]{1,0:T(8,128)}), f32[192,1]{1,0:T(8,128)}) %reduce-scatter.43.cloned.1.call-update) | async-done | bytes 784
  3010.6 61.1 %reduce-scatter.47.cloned.1.call-done = f32[192,1]{1,0:T(8,128)} async-done(((f32[3072,1]{1,0:T(8,128)}), f32[192,1]{1,0:T(8,128)}) %reduce-scatter.47.cloned.1.call-update) | async-done | bytes 784
  3073.2 60.7 %reduce-scatter.37.cloned.1.call-done = f32[192,4]{1,0:T(8,128)} async-done(((f32[3072,4]{1,0:T(8,128)}), f32[192,4]{1,0:T(8,128)}) %reduce-scatter.37.cloned.1.call-update) | async-done | bytes 3088
  3135.5 60.9 %reduce-scatter.45.cloned.1.call-done = f32[192,16]{1,0:T(8,128)} async-done(((f32[3072,16]{1,0:T(8,128)}), f32[192,16]{1,0:T(8,128)}) %reduce-scatter.45.cloned.1.call-update) | async-done | bytes 12304
  3197.9 13.4 reduce-scatter.27.cloned.1.call-done
  3216.9 40.0 %all-reduce.103 = f32[1536]{0:T(1024)S(1)} all-reduce(f32[1536]{0:T(1024)S(1)} %get-tuple-element.461), channel_id=5, replica_groups=mesh['dir'=2,'dp'=16] {'dir','dp'}, use_global_device_ids=true, to_apply=%region_16.17.clone | all-reduce | flops 1536 | bytes 12288
  3276.5 61.0 %reduce-scatter.35.cloned.1.call-done = f32[1,192,128]{2,1,0:T(8,128)} async-done(((f32[1,3072,128]{2,1,0:T(8,128)}), f32[1,192,128]{2,1,0:T(8,128)}) %reduce-scatter.35.cloned.1.call-update) | async-done | bytes 98320 | tf_op jit(solution)/shard_map/reduce_scatter | solution.py:259
  3337.5 115.6 %reduce-scatter.29.cloned.1.call-done = f32[768,192]{0,1:T(8,128)} async-done(((f32[768,3072]{0,1:T(8,128)}), f32[768,192]{0,1:T(8,128)}) %reduce-scatter.29.cloned.1.call-update) | async-done | bytes 589840 | tf_op jit(solution)/shard_map/reduce_scatter | solution.py:252
  3453.1 115.7 %reduce-scatter.31.cloned.1.call-done = f32[768,192]{0,1:T(8,128)} async-done(((f32[768,3072]{0,1:T(8,128)}), f32[768,192]{0,1:T(8,128)}) %reduce-scatter.31.cloned.1.call-update) | async-done | bytes 589840 | tf_op jit(solution)/shard_map/reduce_scatter | solution.py:253
  3568.8 116.2 %reduce-scatter.33.cloned.1.call-done = f32[1536,96]{0,1:T(8,128)} async-done(((f32[1536,1536]{0,1:T(8,128)}), f32[1536,96]{0,1:T(8,128)}) %reduce-scatter.33.cloned.1.call-update) | async-done | bytes 589840 | tf_op jit(solution)/shard_map/reduce_scatter | solution.py:254
  (1800 shorter events, 2099.6 us)
Async XLA Ops:
  7.2 70.7 %copy-start.137 = (bf16[1,96,192]{2,1,0:T(8,128)(2,1)S(1)}, bf16[1,96,192]{2,1,0:T(8,128)(2,1)}, u32[]{:S(2)}) copy-start(bf16[1,96,192]{2,1,0:T(8,128)(2,1)} %param.27) | copy-start | bytes 110596
  7.2 279.8 %all-gather.8.cloned.1.call-start = ((), (), s32[]{:S(2)}) async-start(), calls=%async_computation.14 | async-start | bytes 10027008 | tf_op jit(solution)/shard_map/all_gather | solution.py:119
  8.0 286.0 %all-gather.10.cloned.1.call-start = ((), (), s32[]{:S(2)}) async-start(), calls=%async_computation.15 | async-start | bytes 10027008 | tf_op jit(solution)/shard_map/all_gather | solution.py:120
  8.7 304.6 %all-gather.6.cloned.1.call-start = ((), (), s32[]{:S(2)}) async-start(), calls=%async_computation.12 | async-start | bytes 10027008 | tf_op jit(solution)/shard_map/all_gather | solution.py:118
  9.5 2856.9 %all-gather.12.cloned.1.call-start = ((), (), s32[]{:S(2)}) async-start(), calls=%async_computation.17 | async-start | bytes 2359296 | tf_op jit(solution)/shard_map/all_gather | solution.py:235
  77.3 35.4 copy-start.118
  78.1 30.6 copy-start.146
  78.1 34.4 copy-start.109
  113.7 199.6 %copy-start.91 = (bf16[128,1536]{1,0:T(8,128)(2,1)}, bf16[128,1536]{1,0:T(8,128)(2,1)S(1)}, u32[]{:S(2)}) copy-start(bf16[128,1536]{1,0:T(8,128)(2,1)S(1)} %get-tuple-element.645) | copy-start | bytes 1179652
  197.8 122.5 %copy-start.140 = (f32[128]{0:T(128)}, f32[128]{0:T(128)S(1)}, u32[]{:S(2)}) copy-start(f32[128]{0:T(128)S(1)} %get-tuple-element.650) | copy-start | bytes 1540
  222.0 102.0 %copy-start.93 = (bf16[1,3072,128]{2,1,0:T(8,128)(2,1)}, bf16[1,3072,128]{2,1,0:T(8,128)(2,1)S(1)}, u32[]{:S(2)}) copy-start(bf16[1,3072,128]{2,1,0:T(8,128)(2,1)S(1)} %all_gather.57) | copy-start | bytes 2359300
  287.0 33.2 copy-start.122
  1049.2 82.2 %copy-start.50 = (f32[32,3072]{1,0:T(8,128)}, f32[32,3072]{1,0:T(8,128)S(1)}, u32[]{:S(2)}) copy-start(f32[32,3072]{1,0:T(8,128)S(1)} %get-tuple-element.979) | copy-start | bytes 1179652 | tf_op jit(solution)/shard_map/transpose(jvp())/while
  1058.0 68.7 %copy-start.1 = (f32[16,16,3072]{2,1,0:T(8,128)}, f32[16,16,3072]{2,1,0:T(8,128)S(1)}, u32[]{:S(2)}) copy-start(f32[16,16,3072]{2,1,0:T(8,128)S(1)} %get-tuple-element.957) | copy-start | bytes 9437188 | tf_op jit(solution)/shard_map/transpose(jvp())/while
  1152.1 21.8 slice-start
  1159.2 14.6 slice-start.1
  1306.0 18.8 slice-start.2
  1328.7 13.0 copy-start.27
  1390.9 13.0 slice-start.4
  1390.9 13.0 copy-start.28
  1405.7 13.0 copy-start.10
  1445.3 13.0 copy-start.7
  1491.8 82.2 %copy-start.50 = (f32[32,3072]{1,0:T(8,128)}, f32[32,3072]{1,0:T(8,128)S(1)}, u32[]{:S(2)}) copy-start(f32[32,3072]{1,0:T(8,128)S(1)} %get-tuple-element.979) | copy-start | bytes 1179652 | tf_op jit(solution)/shard_map/transpose(jvp())/while
  1500.7 68.7 %copy-start.1 = (f32[16,16,3072]{2,1,0:T(8,128)}, f32[16,16,3072]{2,1,0:T(8,128)S(1)}, u32[]{:S(2)}) copy-start(f32[16,16,3072]{2,1,0:T(8,128)S(1)} %get-tuple-element.957) | copy-start | bytes 9437188 | tf_op jit(solution)/shard_map/transpose(jvp())/while
  1594.7 21.8 slice-start
  1601.9 14.6 slice-start.1
  1748.6 18.8 slice-start.2
  1771.4 13.0 copy-start.27
  1834.5 13.0 slice-start.4
  1834.5 13.0 copy-start.28
  1849.3 13.0 copy-start.10
  1888.9 13.0 copy-start.7
  1935.5 82.2 %copy-start.50 = (f32[32,3072]{1,0:T(8,128)}, f32[32,3072]{1,0:T(8,128)S(1)}, u32[]{:S(2)}) copy-start(f32[32,3072]{1,0:T(8,128)S(1)} %get-tuple-element.979) | copy-start | bytes 1179652 | tf_op jit(solution)/shard_map/transpose(jvp())/while
  1944.3 68.7 %copy-start.1 = (f32[16,16,3072]{2,1,0:T(8,128)}, f32[16,16,3072]{2,1,0:T(8,128)S(1)}, u32[]{:S(2)}) copy-start(f32[16,16,3072]{2,1,0:T(8,128)S(1)} %get-tuple-element.957) | copy-start | bytes 9437188 | tf_op jit(solution)/shard_map/transpose(jvp())/while
  2038.3 21.8 slice-start
  2045.5 14.6 slice-start.1
  2192.2 18.8 slice-start.2
  2215.0 13.0 copy-start.27
  2278.1 13.0 slice-start.4
  2278.1 13.0 copy-start.28
  2379.1 82.2 %copy-start.50 = (f32[32,3072]{1,0:T(8,128)}, f32[32,3072]{1,0:T(8,128)S(1)}, u32[]{:S(2)}) copy-start(f32[32,3072]{1,0:T(8,128)S(1)} %get-tuple-element.979) | copy-start | bytes 1179652 | tf_op jit(solution)/shard_map/transpose(jvp())/while
  2387.9 68.7 %copy-start.1 = (f32[16,16,3072]{2,1,0:T(8,128)}, f32[16,16,3072]{2,1,0:T(8,128)S(1)}, u32[]{:S(2)}) copy-start(f32[16,16,3072]{2,1,0:T(8,128)S(1)} %get-tuple-element.957) | copy-start | bytes 9437188 | tf_op jit(solution)/shard_map/transpose(jvp())/while
  2481.9 21.8 slice-start
  2489.1 14.6 slice-start.1
  2635.8 18.8 slice-start.2
  2658.6 13.0 copy-start.27
  2721.7 13.0 slice-start.4
  2721.7 13.0 copy-start.28
  2736.5 13.0 copy-start.10
  2776.1 13.0 copy-start.7
  2839.2 44.3 %reduce-scatter.25.cloned.1.call-start = ((), (), s32[]{:S(2)}) async-start(), calls=%async_computation.13 | async-start | bytes 1179648 | tf_op jit(solution)/shard_map/reduce_scatter | solution.py:176
  2843.2 103.7 %reduce-scatter.39.cloned.1.call-start = ((), (), s32[]{:S(2)}) async-start(), calls=%async_computation.23 | async-start | bytes 1671168
  2844.9 164.2 %reduce-scatter.43.cloned.1.call-start = ((), (), s32[]{:S(2)}) async-start(), calls=%async_computation.25 | async-start | bytes 1671168
  2848.4 223.3 %reduce-scatter.47.cloned.1.call-start = ((), (), s32[]{:S(2)}) async-start(), calls=%async_computation.27 | async-start | bytes 1671168
  2853.0 281.0 %reduce-scatter.37.cloned.1.call-start = ((), (), s32[]{:S(2)}) async-start(), calls=%async_computation.22 | async-start | bytes 1671168
  2855.9 340.5 %reduce-scatter.45.cloned.1.call-start = ((), (), s32[]{:S(2)}) async-start(), calls=%async_computation.26 | async-start | bytes 1671168
  2861.5 349.9 %reduce-scatter.27.cloned.1.call-start = ((), (), s32[]{:S(2)}) async-start(), calls=%async_computation.16 | async-start | bytes 589824 | tf_op jit(solution)/shard_map/reduce_scatter | solution.py:221
  2862.4 412.5 %reduce-scatter.41.cloned.1.call-start = ((), (), s32[]{:S(2)}) async-start(), calls=%async_computation.24 | async-start | bytes 1671168
  2864.4 473.1 %reduce-scatter.35.cloned.1.call-start = ((), (), s32[]{:S(2)}) async-start(), calls=%async_computation.21 | async-start | bytes 1671168 | tf_op jit(solution)/shard_map/reduce_scatter | solution.py:259
  2866.1 587.1 %reduce-scatter.29.cloned.1.call-start = ((), (), s32[]{:S(2)}) async-start(), calls=%async_computation.18 | async-start | bytes 10027008 | tf_op jit(solution)/shard_map/reduce_scatter | solution.py:252
  2874.2 694.5 %reduce-scatter.31.cloned.1.call-start = ((), (), s32[]{:S(2)}) async-start(), calls=%async_computation.19 | async-start | bytes 10027008 | tf_op jit(solution)/shard_map/reduce_scatter | solution.py:253
  2901.4 783.6 %reduce-scatter.33.cloned.1.call-start = ((), (), s32[]{:S(2)}) async-start(), calls=%async_computation.20 | async-start | bytes 10027008 | tf_op jit(solution)/shard_map/reduce_scatter | solution.py:254
  2924.4 287.0 %copy-start.112 = (f32[128,1536]{1,0:T(8,128)S(1)}, f32[128,1536]{1,0:T(8,128)}, u32[]{:S(2)}) copy-start(f32[128,1536]{1,0:T(8,128)} %get-tuple-element.644) | copy-start | bytes 2359300
  2924.4 287.0 %copy-start.119 = (f32[1536]{0:T(1024)S(1)}, f32[1536]{0:T(1024)}, u32[]{:S(2)}) copy-start(f32[1536]{0:T(1024)} %copy-done.118) | copy-start | bytes 18436
  (440 other events, 2001.5 us)
Sparse Core Ops, SparseCore 0:
  10.4 90.9 all-gather.7
  103.6 104.9 all-gather.9
  210.9 79.7 all-gather.5
  2839.3 24.5 all-gather.11
  2866.0 17.4 reduce-scatter.24
  2887.4 59.4 reduce-scatter.38
  2950.6 58.5 reduce-scatter.42
  3013.2 58.4 reduce-scatter.46
  3075.4 58.5 reduce-scatter.36
  3137.9 58.4 reduce-scatter.44
  3199.2 12.1 reduce-scatter.26
  3215.3 59.5 reduce-scatter.40
  3279.1 58.3 reduce-scatter.34
  3342.6 110.4 reduce-scatter.28
  3457.6 111.0 reduce-scatter.30
  3573.8 111.0 reduce-scatter.32
where the time goes:
time: 3720 us; the launch traced here: 3690 us
  local copies, waits for them, and re-layouts  1730 us (47%)
  other arithmetic  872 us (23%)
  waiting for transfers between devices  708 us (19%)
  blocking collectives  260 us (7%)
  matrix products  64.6 us (2%)
    pad x248, local copies, waits for them, and re-layouts, scan_block(): total_a, total_b = lax.associative_scan(combine, (factor, inject), axis=0)  1410 us
    unnamed x22, waiting for transfers between devices  277 us
    mul x80, other arithmetic, combine(): return (earlier[0] * latter[0], latter[0] * earlier[1] + latter[1])  270 us
    add x64, other arithmetic, scan_block(): total_a, total_b = lax.associative_scan(combine, (factor, inject), axis=0)  142 us
    reduce_scatter x1, waiting for transfers between devices, local(): lax.psum_scatter(part_out, 'dp', scatter_dimension=1, tiled=True)  116 us
    reduce_scatter x1, waiting for transfers between devices, local(): lax.psum_scatter(part_z, 'dp', scatter_dimension=1, tiled=True)  116 us
    reduce_scatter x1, waiting for transfers between devices, local(): lax.psum_scatter(part_x, 'dp', scatter_dimension=1, tiled=True)  116 us
    unnamed x2, blocking collectives  105 us
  transfers between devices with their start and end apart: 16, of which 12 were waited for; matrix products, arithmetic and copies ran while one was open for 5% of the time, Pallas kernels for 0%

commit v1 on v0

v1 whole, which is shorter than its diff:
```python
from functools import partial

import jax
import jax.numpy as jnp
from jax import lax
from jax.experimental import pallas as pl
from jax.experimental.pallas import tpu as pltpu
from jax.sharding import PartitionSpec as P

f32 = jnp.float32
bf16 = jnp.bfloat16
EPS = 1e-05
DT_RANK = 96
STATE = 16
TAPS = 4
TP = 8
PACK = 128
CHUNK = 16
NSTEP = 4
LOG2E = 1.4426950408889634
LN2 = 0.6931471805599453
BIG = 1e9
PAD = 24


def mm(left, right):
    return jnp.dot(left, right, preferred_element_type=f32)


def mm_nt(left, right):
    return lax.dot_general(left, right, (((1,), (1,)), ((), ())), preferred_element_type=f32)


def mm_tn(left, right):
    return lax.dot_general(left, right, (((0,), (0,)), ((), ())), preferred_element_type=f32)


def segment_of(t, ends):
    return (t >= ends[0]).astype(jnp.int32) + (t >= ends[1]).astype(jnp.int32)


def rows8(t):
    return pl.ds(pl.multiple_of(t * 8, 8), 8)


def sigmoid(v):
    return 1.0 / (1.0 + jnp.exp(-v))


def call(kernel, outs, args, **kw):
    params = dict(vmem_limit_bytes=60 << 20)
    return pl.pallas_call(
        kernel,
        out_shape=outs,
        compiler_params=pltpu.CompilerParams(**params),
        **kw,
    )(*args)


def spaces(args, scalars):
    return [
        pl.BlockSpec(memory_space=pltpu.SMEM if n in scalars else pltpu.VMEM)
        for n in range(len(args))
    ]


def front_kernel(
    dir_ref, ends_ref, tokens, gain, wx, wz, wstate, taps,
    normed, conv_in, conv_pre, conv_out, gate_in, proj,
):
    s = dir_ref[0]
    half = PACK // 2
    sgn = 1 - 2 * s
    conv_in[0:PAD, :] = jnp.zeros((PAD, conv_in.shape[1]), f32)
    conv_in[PAD + 8 * PACK :, :] = jnp.zeros((PAD, conv_in.shape[1]), f32)

    def norm_pack(p, carry):
        rows = pl.ds(pl.multiple_of(p * PACK, PACK), PACK)
        x = tokens[rows, :].astype(f32)
        inv = lax.rsqrt(jnp.mean(x * x, axis=1, keepdims=True) + EPS)
        normed[rows, :] = (x * inv * gain[...]).astype(bf16)
        mine = pl.ds(pl.multiple_of(p * PACK + s * half, half), half)
        gate_in[pl.ds(pl.multiple_of(p * half, half), half), :] = mm(normed[mine, :], wz[...])
        return carry

    lax.fori_loop(0, 8, norm_pack, 0)

    def in_rows(b, carry):
        span = 32
        parts = [normed[pl.ds(pl.multiple_of(p * PACK + b * span, span), span), :] for p in range(8)]
        x = mm(jnp.concatenate(parts, axis=0), wx[...])
        x = jnp.swapaxes(x.reshape(8, span, x.shape[1]), 0, 1).reshape(8 * span, x.shape[1])
        conv_in[pl.ds(pl.multiple_of(PAD + b * span * 8, 8), 8 * span), :] = x
        return carry

    lax.fori_loop(0, PACK // 32, in_rows, 0)
    ends = (ends_ref[0], ends_ref[1])

    def conv_step(t, carry):
        seg = segment_of(t, ends)
        total = taps[4:5, :] + taps[3:4, :] * conv_in[rows8(t + 3), :]
        for j in range(1, TAPS):
            there = t - j * sgn
            same = (segment_of(there, ends) == seg).astype(f32)[:, 0:1]
            total = total + taps[3 - j : 4 - j, :] * (conv_in[rows8(there + 3), :] * same)
        conv_pre[rows8(t), :] = total
        act = total * sigmoid(total)
        conv_out[rows8(t), :] = act.astype(bf16).astype(f32)
        return carry

    lax.fori_loop(0, PACK, conv_step, 0, unroll=2)
    proj[...] = mm(conv_out[...].astype(bf16), wstate[...])


def front(s, ends, tokens, gain, wx, wz, wstate, taps):
    rows, width = tokens.shape
    ch = wx.shape[1]
    args = (s, ends, tokens, gain, wx, wz, wstate, taps)
    outs = (
        jax.ShapeDtypeStruct((rows, width), bf16),
        jax.ShapeDtypeStruct((rows + 2 * PAD, ch), f32),
        jax.ShapeDtypeStruct((rows, ch), f32),
        jax.ShapeDtypeStruct((rows, ch), f32),
        jax.ShapeDtypeStruct((rows // 2, ch), f32),
        jax.ShapeDtypeStruct((rows, 128), f32),
    )
    return call(front_kernel, outs, args, in_specs=spaces(args, (0,)))


def softplus(v):
    return jnp.maximum(v, 0.0) + jnp.log1p(jnp.exp(-jnp.abs(v)))


def scan_kernel(dir_ref, ends_ref, proj, conv_out, wstep, small, decay, y, hprev, step, decay_step, u, state):
    c = pl.program_id(0)
    s = dir_ref[0]
    sgn = 1 - 2 * s
    block = c + s * (pl.num_programs(0) - 1 - 2 * c)
    ch = conv_out.shape[1]
    pre = mm(proj[...].astype(bf16), wstep[...])
    step_all = softplus(pre + small[0:1, :])
    step[...] = step_all
    u[...] = step_all * conv_out[...]
    y[...] = small[1:2, :] * conv_out[...]
    ends = (ends_ref[0], ends_ref[1])

    @pl.when(c == 0)
    def _():
        state[...] = jnp.zeros_like(state)

    for k in range(CHUNK):
        t = block * CHUNK + k
        fresh = (segment_of(t, ends) != segment_of(t - sgn, ends))[:, 0:1]
        decay_step[8 * k : 8 * k + 8, :] = jnp.where(fresh, BIG, step_all[8 * k : 8 * k + 8, :])

    for n0 in range(0, STATE, NSTEP):
        rate = [jnp.broadcast_to(decay[n : n + 1, :], (8, ch)) for n in range(n0, n0 + NSTEP)]

        def body(k, hs):
            r = s * (CHUNK - 1 - k) + (1 - s) * k
            rows = rows8(r)
            pv = proj[rows, :]
            st = decay_step[rows, :]
            uv = u[rows, :]
            acc = y[rows, :]
            new = []
            for m in range(NSTEP):
                n = n0 + m
                hprev[r, n] = hs[m]
                a = jnp.exp2(st * rate[m])
                h = a * hs[m] + uv * pv[:, DT_RANK + n : DT_RANK + n + 1]
                acc = acc + h * pv[:, DT_RANK + STATE + n : DT_RANK + STATE + n + 1]
                new.append(h)
            y[rows, :] = acc
            return tuple(new)

        hs = tuple(state[n] for n in range(n0, n0 + NSTEP))
        hs = lax.fori_loop(0, CHUNK, body, hs, unroll=2)
        for m in range(NSTEP):
            state[n0 + m] = hs[m]


def scan_forward(s, ends, proj, conv_out, wstep, small, decay):
    rows, ch = conv_out.shape
    span = CHUNK * 8
    blocks = rows // span

    def at(c, d):
        return c + d[0] * (blocks - 1 - 2 * c)

    def rowspec(width):
        return pl.BlockSpec((span, width), lambda c, d: (at(c, d), 0))

    def whole(shape):
        return pl.BlockSpec(shape, lambda c, d: (0,) * len(shape))

    return pl.pallas_call(
        scan_kernel,
        grid_spec=pltpu.PrefetchScalarGridSpec(
            num_scalar_prefetch=1,
            grid=(blocks,),
            in_specs=[
                whole(ends.shape), rowspec(128), rowspec(ch), whole(wstep.shape), whole(small.shape), whole(decay.shape),
            ],
            out_specs=(
                rowspec(ch),
                pl.BlockSpec((CHUNK, STATE, 8, ch), lambda c, d: (at(c, d), 0, 0, 0)),
            ),
            scratch_shapes=[
                pltpu.VMEM((span, ch), f32),
                pltpu.VMEM((span, ch), f32),
                pltpu.VMEM((span, ch), f32),
                pltpu.VMEM((STATE, 8, ch), f32),
            ],
        ),
        out_shape=(
            jax.ShapeDtypeStruct((rows, ch), f32),
            jax.ShapeDtypeStruct((rows // 8, STATE, 8, ch), f32),
        ),
        compiler_params=pltpu.CompilerParams(vmem_limit_bytes=60 << 20),
    )(s, ends, proj, conv_out, wstep, small, decay)


def gate_kernel(dir_ref, y, y_other, gate_in, wout, cot, gated, mixed, grad_sum, grad_gate, both, other):
    s = dir_ref[0]
    half = y_other.shape[0]
    steps = half // 8
    ch = y.shape[1]
    both[...] = y[pl.ds(pl.multiple_of(s * half, half), half), :] + y_other[...].astype(f32)
    summed = jnp.swapaxes(both[...].reshape(steps, 8, ch), 0, 1).reshape(half, ch)
    gate = gate_in[...]
    sig = sigmoid(gate)
    act = gate * sig
    g = (summed * act).astype(bf16)
    gated[...] = g
    mixed[...] = mm(g, wout[...]).astype(bf16)
    grad_gated = mm_nt(cot[...], wout[...])
    grad_gate[...] = (grad_gated * summed * sig * (1.0 + gate * (1.0 - sig))).astype(bf16)
    back = grad_gated * act
    other[...] = jnp.swapaxes(back.reshape(8, steps, ch), 0, 1).reshape(half, ch)
    grad_sum[...] = other[...].astype(bf16)


def gate(s, y, y_other, gate_in, wout, cot):
    half, ch = gate_in.shape
    args = (s, y, y_other, gate_in, wout, cot)
    outs = (
        jax.ShapeDtypeStruct((half, ch), bf16),
        jax.ShapeDtypeStruct((half, wout.shape[1]), bf16),
        jax.ShapeDtypeStruct((half, ch), bf16),
        jax.ShapeDtypeStruct((half, ch), bf16),
    )
    return call(
        gate_kernel, outs, args, in_specs=spaces(args, (0,)),
        scratch_shapes=[pltpu.VMEM((half, ch), f32), pltpu.VMEM((half, ch), f32)],
    )


def back_kernel(
    dir_ref, ends_ref, g_low, proj, conv_out, hprev, wstep, small, decay, ones,
    grad_values, grad_proj, grad_wstep, grad_rows, grad_decay,
    g, step, decay_step, u, s1, s2, pb, pc, carry_ref, acc_ref, bias_acc, skip_acc,
):
    c = pl.program_id(0)
    last = pl.num_programs(0) - 1
    s = dir_ref[0]
    sgn = 1 - 2 * s
    block = (last - c) + s * (2 * c - last)
    ch = conv_out.shape[1]
    rank = proj[...].astype(bf16)
    pre = mm(rank, wstep[...]) + small[0:1, :]
    step_all = softplus(pre)
    step[...] = step_all
    g[...] = g_low[...].astype(f32)
    u[...] = step_all * conv_out[...]
    ends = (ends_ref[0], ends_ref[1])

    @pl.when(c == 0)
    def _():
        carry_ref[...] = jnp.zeros_like(carry_ref)
        acc_ref[...] = jnp.zeros_like(acc_ref)
        bias_acc[...] = jnp.zeros_like(bias_acc)
        skip_acc[...] = jnp.zeros_like(skip_acc)
        grad_wstep[...] = jnp.zeros_like(grad_wstep)

    for k in range(CHUNK):
        t = block * CHUNK + k
        fresh = (segment_of(t, ends) != segment_of(t - sgn, ends))[:, 0:1]
        decay_step[8 * k : 8 * k + 8, :] = jnp.where(fresh, BIG, step_all[8 * k : 8 * k + 8, :])
    s1[...] = jnp.zeros_like(s1)
    s2[...] = jnp.zeros_like(s2)

    def tiles(v):
        total = v[:, 0:128]
        for w in range(128, ch, 128):
            total = total + v[:, w : w + 128]
        return total

    for n0 in range(0, STATE, NSTEP):
        rate = [jnp.broadcast_to(decay[n : n + 1, :], (8, ch)) for n in range(n0, n0 + NSTEP)]

        def body(k, state):
            carry, acc = state
            r = s * k + (1 - s) * (CHUNK - 1 - k)
            rows = rows8(r)
            pv = proj[rows, :]
            gv = g[rows, :]
            uv = u[rows, :]
            stv = step[rows, :]
            st = decay_step[rows, :]
            one = s1[rows, :]
            two = s2[rows, :]
            new_carry, new_acc = [], []
            for m in range(NSTEP):
                n = n0 + m
                a = jnp.exp2(st * rate[m])
                ah = a * hprev[r, n]
                lam = gv * pv[:, DT_RANK + STATE + n : DT_RANK + STATE + n + 1] + carry[m]
                w = lam * ah
                new_carry.append(a * lam)
                two = two + rate[m] * w
                new_acc.append(acc[m] + stv * w)
                one = one + lam * pv[:, DT_RANK + n : DT_RANK + n + 1]
                pb[rows, 128 * n : 128 * n + 128] = tiles(lam * uv)
                pc[rows, 128 * n : 128 * n + 128] = tiles(gv * ah)
            s1[rows, :] = one
            s2[rows, :] = two
            return tuple(new_carry), tuple(new_acc)

        first = (
            tuple(carry_ref[n] for n in range(n0, n0 + NSTEP)),
            tuple(acc_ref[n] for n in range(n0, n0 + NSTEP)),
        )
        carry, acc = lax.fori_loop(0, CHUNK, body, first, unroll=2)
        for m in range(NSTEP):
            carry_ref[n0 + m] = carry[m]
            acc_ref[n0 + m] = acc[m]

    values = conv_out[...]
    gv = g[...]
    one = s1[...]
    grad_values[...] = gv * small[1:2, :] + step[...] * one
    q = (LN2 * s2[...] + values * one) * sigmoid(pre)
    low = q.astype(bf16)
    bias_acc[...] += jnp.sum(q.reshape(CHUNK, 8, ch), axis=0)
    skip_acc[...] += jnp.sum((gv * values).reshape(CHUNK, 8, ch), axis=0)
    grad_wstep[...] += mm_tn(rank, low)
    gu = jnp.sum(gv * u[...], axis=1, keepdims=True)
    lane = lax.broadcasted_iota(jnp.int32, (CHUNK * 8, 128), 1)
    inject = jnp.where(lane >= DT_RANK + STATE, pltpu.roll(proj[...], STATE, 1), 0.0)
    grad_proj[...] = (
        mm_nt(low, wstep[...])
        + mm(pb[...].astype(bf16), ones[0])
        + mm(pc[...].astype(bf16), ones[1])
        + gu * inject
    )

    @pl.when(c == last)
    def _():
        grad_rows[0:1, :] = jnp.sum(bias_acc[...], axis=0, keepdims=True)
        grad_rows[1:2, :] = jnp.sum(skip_acc[...], axis=0, keepdims=True)
        for n in range(STATE):
            grad_decay[n : n + 1, :] = jnp.sum(acc_ref[n], axis=0, keepdims=True) * decay[n : n + 1, :] * LN2


def scan_backward(s, ends, g, proj, conv_out, hprev, wstep, small, decay):
    rows, ch = conv_out.shape
    span = CHUNK * 8
    blocks = rows // span

    def at(c, d):
        return (blocks - 1 - c) + d[0] * (2 * c - blocks + 1)

    def rowspec(width):
        return pl.BlockSpec((span, width), lambda c, d: (at(c, d), 0))

    def whole(shape):
        return pl.BlockSpec(shape, lambda c, d: (0,) * len(shape))

    source = lax.broadcasted_iota(jnp.int32, (2, STATE * 128, 128), 1) // 128
    which = lax.broadcasted_iota(jnp.int32, (2, STATE * 128, 128), 0)
    target = lax.broadcasted_iota(jnp.int32, (2, STATE * 128, 128), 2)
    ones = (target == DT_RANK + which * STATE + source).astype(bf16)
    big = pltpu.VMEM((span, ch), f32)
    return pl.pallas_call(
        back_kernel,
        grid_spec=pltpu.PrefetchScalarGridSpec(
            num_scalar_prefetch=1,
            grid=(blocks,),
            in_specs=[
                whole(ends.shape), rowspec(ch), rowspec(128), rowspec(ch),
                pl.BlockSpec((CHUNK, STATE, 8, ch), lambda c, d: (at(c, d), 0, 0, 0)),
                whole(wstep.shape), whole(small.shape), whole(decay.shape), whole(ones.shape),
            ],
            out_specs=(rowspec(ch), rowspec(128), whole((128, ch)), whole((2, ch)), whole((STATE, ch))),
            scratch_shapes=[big] * 6
            + [
                pltpu.VMEM((span, STATE * 128), f32),
                pltpu.VMEM((span, STATE * 128), f32),
                pltpu.VMEM((STATE, 8, ch), f32),
                pltpu.VMEM((STATE, 8, ch), f32),
                pltpu.VMEM((8, ch), f32),
                pltpu.VMEM((8, ch), f32),
            ],
        ),
        out_shape=(
            jax.ShapeDtypeStruct((rows, ch), f32),
            jax.ShapeDtypeStruct((rows, 128), f32),
            jax.ShapeDtypeStruct((128, ch), f32),
            jax.ShapeDtypeStruct((2, ch), f32),
            jax.ShapeDtypeStruct((STATE, ch), f32),
        ),
        compiler_params=pltpu.CompilerParams(vmem_limit_bytes=60 << 20),
    )(s, ends, g, proj, conv_out, hprev, wstep, small, decay, ones)


def conv_back_kernel(
    dir_ref, ends_ref, grad_values, grad_proj, conv_out, conv_pre, conv_in, wstate, taps,
    grad_in, grad_state, grad_taps, w, slots, sums,
):
    s = dir_ref[0]
    sgn = 1 - 2 * s
    ch = conv_out.shape[1]
    low = grad_proj[...].astype(bf16)
    w[0:PAD, :] = jnp.zeros((PAD, ch), f32)
    w[PAD + 8 * PACK :, :] = jnp.zeros((PAD, ch), f32)
    c = conv_pre[...]
    sig = sigmoid(c)
    w[PAD : PAD + 8 * PACK, :] = (grad_values[...] + mm_nt(low, wstate[...])) * (sig * (1.0 + c * (1.0 - sig)))
    grad_state[...] = mm_tn(conv_out[...].astype(bf16), low)
    sums[...] = jnp.zeros_like(sums)
    ends = (ends_ref[0], ends_ref[1])

    def step(t, carry):
        seg = segment_of(t, ends)
        here = w[rows8(t + 3), :]
        total = taps[3:4, :] * here
        sums[3] += here * conv_in[rows8(t + 3), :]
        sums[4] += here
        for j in range(1, TAPS):
            back = t - j * sgn
            ahead = t + j * sgn
            same_back = (segment_of(back, ends) == seg).astype(f32)[:, 0:1]
            same_ahead = (segment_of(ahead, ends) == seg).astype(f32)[:, 0:1]
            sums[3 - j] += here * (conv_in[rows8(back + 3), :] * same_back)
            total = total + taps[3 - j : 4 - j, :] * (w[rows8(ahead + 3), :] * same_ahead)
        slots[rows8(t), :] = total
        return carry

    lax.fori_loop(0, PACK, step, 0, unroll=2)
    for n in range(5):
        grad_taps[n : n + 1, :] = jnp.sum(sums[n], axis=0, keepdims=True)

    def out_rows(b, carry):
        span = 32
        x = slots[pl.ds(pl.multiple_of(b * span * 8, 8), 8 * span), :]
        x = jnp.swapaxes(x.reshape(span, 8, ch), 0, 1).astype(bf16)
        for p in range(8):
            grad_in[pl.ds(pl.multiple_of(p * PACK + b * span, span), span), :] = x[p]
        return carry

    lax.fori_loop(0, PACK // 32, out_rows, 0)


def conv_backward(s, ends, grad_values, grad_proj, conv_out, conv_pre, conv_in, wstate, taps):
    rows, ch = conv_out.shape
    args = (s, ends, grad_values, grad_proj, conv_out, conv_pre, conv_in, wstate, taps)
    outs = (
        jax.ShapeDtypeStruct((rows, ch), bf16),
        jax.ShapeDtypeStruct((ch, 128), f32),
        jax.ShapeDtypeStruct((5, ch), f32),
    )
    return call(
        conv_back_kernel, outs, args, in_specs=spaces(args, (0,)),
        scratch_shapes=[
            pltpu.VMEM((rows + 2 * PAD, ch), f32),
            pltpu.VMEM((rows, ch), f32),
            pltpu.VMEM((5, 8, ch), f32),
        ],
    )


def normed_grad_kernel(grad_x0, grad_x1, grad_z, wx, wz, out):
    rows = out.shape[0] // 4

    def body(b, carry):
        r = pl.ds(pl.multiple_of(b * rows, rows), rows)
        out[r, :] = (
            mm_nt(grad_x0[r, :], wx[...]) + mm_nt(grad_x1[r, :], wx[...]) + mm_nt(grad_z[r, :], wz[...])
        ).astype(bf16)
        return carry

    lax.fori_loop(0, 4, body, 0)


def tail_kernel(dir_ref, mixed_parts, grad_parts, tokens, cot, gain, mixed, grad_tokens, grad_gain):
    half = cot.shape[0]
    x = tokens[pl.ds(pl.multiple_of(dir_ref[0] * half, half), half), :].astype(f32)
    inv = lax.rsqrt(jnp.mean(x * x, axis=1, keepdims=True) + EPS)
    unit = x * inv
    total = x
    grad = jnp.zeros_like(x)
    for j in range(TP):
        total = total + mixed_parts[j].astype(f32)
        grad = grad + grad_parts[j].astype(f32)
    mixed[...] = total.astype(bf16)
    scaled = grad * gain[...]
    mean = jnp.mean(scaled * unit, axis=1, keepdims=True)
    grad_tokens[...] = inv * (scaled - unit * mean) + cot[...].astype(f32)
    grad_gain[...] = jnp.sum(grad * unit, axis=0, keepdims=True)


def local(
    reps, tokens, item_grids, norm_gain, proj_in_x, proj_in_z, proj_out, conv_weight, conv_bias,
    proj_state, proj_step, step_bias, decay_log, skip_gain, grad_out,
):
    share = [[(z * reps + y) * 2 + i for z in range(4) for i in range(2)] for y in range(reps)]
    same = [[(z * reps + y) * 2 + i for y in range(reps)] for z in range(4) for i in range(2)]
    direction = lax.axis_index("dir")
    s = direction.reshape(1).astype(jnp.int32)
    length, width = tokens.shape
    half = length // 2
    cols = proj_in_x.shape[1]
    ch = reps * cols
    outs_dev = proj_out.shape[1]

    def gather(x, groups, axis):
        return lax.all_gather(x, "dp", axis=axis, tiled=True, axis_index_groups=groups)

    def spread(x, groups):
        return lax.all_to_all(x, "dp", 0, 0, axis_index_groups=groups, tiled=False)

    tokens_all = gather(tokens, share, 0)
    grids = gather(item_grids.reshape(1, 2, 2), share, 0)
    gain = lax.all_gather(norm_gain, "dp", axis=0, tiled=True).astype(f32).reshape(1, width)
    lengths = grids[:, :, 0] * grids[:, :, 1]
    ends = jnp.stack([lengths[:, 0], lengths[:, 0] + lengths[:, 1]])
    ends = jnp.broadcast_to(ends[:, :, None], (2, TP, 128))
    wx = gather(proj_in_x, same, 1)
    wz = gather(proj_in_z, same, 1)
    small = jnp.concatenate(
        [conv_weight[0], conv_bias, step_bias, skip_gain, decay_log[0], proj_step[0]], axis=0
    )
    small = gather(small, same, 1)
    wstate = gather(proj_state[0], same, 0)
    taps = small[0:5].astype(f32)
    rows_small = small[5:7].astype(f32)
    decay = -LOG2E * jnp.exp(small[7 : 7 + STATE].astype(f32))
    wstep = jnp.concatenate([small[7 + STATE :], jnp.zeros((128 - DT_RANK, ch), bf16)], axis=0)
    wout = proj_out.reshape(4, reps, 2, cols, outs_dev).transpose(0, 2, 1, 3, 4).reshape(TP, ch, outs_dev)
    wout = spread(wout, share)
    wout = lax.all_gather(wout, "dp", axis=0, axis_index_groups=same)
    wout = wout.reshape(reps, 4, 2, ch, outs_dev).transpose(3, 1, 0, 2, 4).reshape(ch, width)
    cot_own = grad_out.reshape(half, width)
    cot = gather(cot_own, share, 0)

    normed, conv_in, conv_pre, conv_out, gate_in, proj_part = front(
        s, ends, tokens_all, gain, wx, wz, wstate, taps
    )
    proj = lax.psum(proj_part, "dp", axis_index_groups=share)
    y, hprev = scan_forward(s, ends, proj, conv_out, wstep, rows_small, decay)
    swap = [(0, 1), (1, 0)]
    rows_half = y.shape[0] // 2
    y_send = lax.dynamic_slice_in_dim(y, (1 - direction) * rows_half, rows_half, 0).astype(bf16)
    y_other = lax.ppermute(y_send, "dir", swap)
    gated, mixed_part, grad_sum, grad_gate = gate(s, y, y_other, gate_in, wout, cot)
    mixed_parts = spread(mixed_part.reshape(TP, half, width), share)
    grad_sum_other = lax.ppermute(grad_sum, "dir", swap)

    def in_order(own, other):
        first = jnp.where(direction == 0, own, other)
        second = jnp.where(direction == 0, other, own)
        return first, second

    g = jnp.concatenate(in_order(grad_sum, grad_sum_other), axis=0)
    grad_values, grad_proj_part, grad_wstep, grad_rows, grad_decay = scan_backward(
        s, ends, g, proj, conv_out, hprev, wstep, rows_small, decay
    )
    grad_proj = lax.psum(grad_proj_part, "dp", axis_index_groups=share)
    grad_in, grad_state, grad_taps = conv_backward(
        s, ends, grad_values, grad_proj, conv_out, conv_pre, conv_in, wstate, taps
    )
    grad_in_other = lax.ppermute(grad_in, "dir", swap)

    def own_half(x):
        x = x.reshape(TP, length, x.shape[1])
        return lax.dynamic_slice_in_dim(x, direction * half, half, 1).reshape(TP * half, x.shape[2])

    args = (own_half(grad_in), own_half(grad_in_other), grad_gate, wx, wz)
    grad_normed_part = call(
        normed_grad_kernel, jax.ShapeDtypeStruct((TP * half, width), bf16), args, in_specs=spaces(args, ())
    )
    grad_parts = spread(grad_normed_part.reshape(TP, half, width), share)

    grad_gate_other = lax.ppermute(grad_gate, "dir", swap)
    first, second = in_order(grad_gate.reshape(TP, half, ch), grad_gate_other.reshape(TP, half, ch))
    gate_all = jnp.concatenate([first, second], axis=1).reshape(TP * length, ch)
    own_cols = lax.dynamic_slice_in_dim(normed, direction * (width // 2), width // 2, 1)
    part_x = mm_tn(own_cols, grad_in) + mm_tn(own_cols, grad_in_other)
    part_z = mm_tn(own_cols, gate_all)

    def reduce_same(x, axis):
        x = jnp.moveaxis(x.reshape(x.shape[:axis] + (reps, cols) + x.shape[axis + 1 :]), axis, 0)
        return jnp.sum(spread(x, same).astype(f32), axis=0)

    grad_x = reduce_same(part_x.astype(bf16), 1)
    grad_z = reduce_same(part_z.astype(bf16), 1)
    part_out = mm_tn(gated, cot).astype(bf16)
    part_out = part_out.reshape(ch, 4, reps, 2, outs_dev).transpose(2, 1, 3, 0, 4)
    part_out = jnp.sum(spread(part_out, same).astype(f32), axis=0).astype(bf16)
    part_out = spread(part_out.reshape(TP, ch, outs_dev), share)
    part_out = lax.all_to_all(part_out.reshape(2, 4, ch, outs_dev), "dir", 0, 0, tiled=False)
    part_out = jnp.sum(part_out.astype(f32), axis=0)
    grad_out_w = (
        part_out.reshape(2, 2, reps, cols, outs_dev).transpose(0, 2, 1, 3, 4).reshape(4 * ch, outs_dev)
    )
    rows_grad = jnp.concatenate([grad_taps, grad_rows, grad_decay, grad_wstep[:DT_RANK]], axis=0)
    rows_grad = reduce_same(rows_grad, 1)
    state_grad = reduce_same(grad_state, 0)

    args = (s, mixed_parts, grad_parts, tokens, cot_own, gain)
    mixed, grad_tokens, grad_gain = call(
        tail_kernel,
        (
            jax.ShapeDtypeStruct((half, width), bf16),
            jax.ShapeDtypeStruct((half, width), f32),
            jax.ShapeDtypeStruct((1, width), f32),
        ),
        args,
        in_specs=spaces(args, (0,)),
    )
    gain_part = lax.psum_scatter(grad_gain[0], ("dir", "dp"), scatter_dimension=0, tiled=True)
    return (
        mixed.reshape(1, 1, half, width),
        grad_tokens.reshape(1, 1, half, width),
        gain_part,
        grad_x,
        grad_z,
        grad_out_w,
        rows_grad[None, 0:4],
        rows_grad[4:5],
        state_grad[None],
        rows_grad[None, 7 + STATE :],
        rows_grad[5:6],
        rows_grad[None, 7 : 7 + STATE],
        rows_grad[6:7],
    )


def solution(mesh):
    reps = mesh.shape["dp"] // TP
    return jax.shard_map(
        partial(local, reps),
        mesh=mesh,
        in_specs=(
            P("dp", None),
            P("dp", None),
            P("dp"),
            P(None, "dp"),
            P(None, "dp"),
            P(None, "dp"),
            P("dir", None, "dp"),
            P("dir", "dp"),
            P("dir", "dp", None),
            P("dir", None, "dp"),
            P("dir", "dp"),
            P("dir", None, "dp"),
            P("dir", "dp"),
            P("dp", "dir", None, None),
        ),
        out_specs=(
            P("dp", "dir", None, None),
            P("dp", "dir", None, None),
            P(("dir", "dp")),
            P("dir", "dp"),
            P("dir", "dp"),
            P("dir", "dp"),
            P("dir", None, "dp"),
            P("dir", "dp"),
            P("dir", "dp", None),
            P("dir", None, "dp"),
            P("dir", "dp"),
            P("dir", None, "dp"),
            P("dir", "dp"),
        ),
        check_vma=False,
    )
```

time: 3720 us -> 549 us (0.15)
  local copies, waits for them, and re-layouts: 1730 us -> 34.1 us
  other arithmetic: 872 us -> 12.2 us
  waiting for transfers between devices: 708 us -> 197 us
  blocking collectives: 260 us -> 128 us
  Pallas kernels: 0 us -> 119 us
  matrix products: 64.6 us -> 7.84 us
    pad x248 -> x0, local copies, waits for them, and re-layouts: 1410 us -> none  [scan_block(): total_a, total_b = lax.associative_scan(combine, (factor, inject), axis=0)]
    reduce_scatter x6 -> x0, waiting for transfers between devices: 431 us -> none  [the longest x1 116 us: local(): lax.psum_scatter(part_out, 'dp', scatter_dimension=1, tiled=True)]
    mul x109 -> x2, other arithmetic: 309 us -> 0.69 us  [the longest x1 0.62 us: local(): decay = -LOG2E * jnp.exp(small[7:7 + STATE].astype(f32))]
    unnamed x22 -> x7, waiting for transfers between devices: 277 us -> 2.63 us
    reduce_sum x20 -> x6, other arithmetic: 159 us -> 4.9 us  [the longest x4 3.65 us: reduce_same(): return jnp.sum(spread(x, same).astype(f32), axis=0)]
    add x84 -> x2, other arithmetic: 153 us -> 0.01 us  [the longest x1 0.01 us: local(): ends = jnp.stack([lengths[:, 0], lengths[:, 0] + lengths[:, 1]])]
    slice x99 -> x5, local copies, waits for them, and re-layouts: 130 us -> 0.42 us  [the longest x1 0.13 us: local(): rows_grad[6:7]]
    all_gather x8 -> x3, blocking collectives: 155 us -> 26.9 us  [gather(): lax.all_gather(x, 'dp', axis=axis, tiled=True, axis_index_groups=groups)]
  transfers between devices with their start and end apart: 16 -> 18, of which waited for: 12 -> 9; matrix products, arithmetic and copies ran while one was open for 5% -> 9% of each run, Pallas kernels for 0% -> 20%
where the time goes in v1:
time: 549 us; the launch traced here: 547 us
  waiting for transfers between devices  197 us (36%)
  blocking collectives  128 us (23%)
  Pallas kernels  119 us (22%)
  local copies, waits for them, and re-layouts  34.1 us (6%)
  starting transfers between devices  33.4 us (6%)
  between operations  15.4 us (3%)
  other arithmetic  12.2 us (2%)
  matrix products  7.84 us (1%)
    unnamed x2, blocking collectives  70.6 us
    all_to_all x7, waiting for transfers between devices, spread(): return lax.all_to_all(x, 'dp', 0, 0, axis_index_groups=groups, tiled=False)  62.5 us
    psum x1, waiting for transfers between devices, local(): proj = lax.psum(proj_part, 'dp', axis_index_groups=share)  51.2 us
    psum x1, waiting for transfers between devices, local(): grad_proj = lax.psum(grad_proj_part, 'dp', axis_index_groups=share)  49 us
    pallas_call x5, Pallas kernels, call(): pl.pallas_call(kernel, out_shape=outs, compiler_params=pltpu.CompilerPara...  47.5 us
    pallas_call x1, Pallas kernels, scan_backward(): pl.pallas_call(back_kernel, grid_spec=pltpu.PrefetchScalarGridSpec(num_sc...  40.8 us
    pallas_call x1, Pallas kernels, scan_forward(): pl.pallas_call(scan_kernel, grid_spec=pltpu.PrefetchScalarGridSpec(num_sc...  30.7 us
    all_to_all x7, starting transfers between devices, spread(): return lax.all_to_all(x, 'dp', 0, 0, axis_index_groups=groups, tiled=False)  27.8 us
  transfers between devices with their start and end apart: 18, of which 9 were waited for; matrix products, arithmetic and copies ran while one was open for 9% of the time, Pallas kernels for 20%

profile of v1, /device:TPU:0, one launch (start us, length us, event | category | flops | bytes accessed | tf_op | source)
XLA Modules:
  0.0 546.9 jit_solution(7672952299835159942)
XLA Ops:
  8.0 0.7 all-gather.15.cloned.1.call-update
  9.4 0.9 reshape.135
  11.1 1.2 reshape.136
  12.3 6.3 %all-to-all-start = ((bf16[8,384,96]{1,2,0:T(8,128)(2,1)}), bf16[8,384,96]{1,2,0:T(8,128)(2,1)S(1)}, u32[]{:S(2)}, u32[]{:S(2)}) async-start(bf16[8,384,96]{1,2,0:T(8,128)(2,1)} %reshape.136), calls=%async_computation | async-start | bytes 1179648 | tf_op jit(solution)/shard_map/all_to_all | solution.py:531
  18.7 17.2 %all-gather.4 = s32[8,2,2]{2,1,0:T(2,128)S(1)} all-gather(s32[1,2,2]{2,1,0:T(2,128)S(1)} %bitcast.98), channel_id=2, replica_groups={{0,1,4,5,8,9,12,13},{2,3,6,7,10,11,14,15},{16,17,20,21,24,25,28,29},{18..., dimensions={0}, use_global_device_ids=true | all-gather | bytes 144 | tf_op jit(solution)/shard_map/all_gather | solution.py:528
  37.2 4.8 all_gather.36
  44.2 33.6 %all-reduce.1 = bf16[1536]{0:T(1024)(128)(2,1)S(1)} all-reduce(bf16[1536]{0:T(1024)(128)(2,1)S(1)} %dynamic-update-slice), channel_id=1, replica_groups=mesh['dir'=2,'dp'=16] {'dp'}, use_global_device_ids=true, to_apply=%add.1 | all-reduce | flops 1536 | bytes 6144
  78.4 4.9 all-gather.1
  83.3 2.4 copy.55.wx
  85.7 2.4 copy.56.wz
  88.1 11.7 %all-gather.11.cloned.1.call-done.tokens = bf16[1024,1536]{1,0:T(8,128)(2,1)} async-done(((bf16[128,1536]{1,0:T(8,128)(2,1)}), bf16[1024,1536]{1,0:T(8,128)(2,1)}) %all-gather.11.cloned.1.call-update) | async-done | bytes 3145744 | tf_op jit(solution)/shard_map/all_gather | solution.py:528
  100.5 19.1 %shard_map.237 = (bf16[1024,1536]{1,0:T(8,128)(2,1)}, f32[1072,384]{1,0:T(8,128)}, f32[1024,384]{1,0:T(8,128)}, f32[1024,384]{1,0:T(8,128)}, f32[512,384]{1,0:T(8,128)}, /*index=5*/f32[1024,128]{1,0:T(8,128)}) custom-call(s32[1]{0:T(128)} %bitcast.dir_ref, s32[2,8,128]{2,1,0:T(8,128)} %broadcast_in_dim.19.ends_ref, ...), custom_call_target="tpu_custom_call" | custom-call | tf_op jit(solution)/shard_map/pallas_call | solution.py:52
  119.7 0.8 copy-done.2
  123.5 51.2 %all-reduce.6.cloned.1.call-done.proj = f32[1024,128]{1,0:T(8,128)} async-done(((f32[1024,128]{1,0:T(8,128)}), f32[1024,128]{1,0:T(8,128)}) %all-reduce.6.cloned.1.call-update) | async-done | bytes 524304 | tf_op jit(solution)/shard_map/psum | solution.py:560
  174.8 30.7 %shard_map.238 = (f32[1024,384]{1,0:T(8,128)}, f32[128,16,8,384]{3,2,1,0:T(8,128)}) custom-call(s32[1]{0:T(128)} %bitcast.dir_ref, s32[2,8,128]{2,1,0:T(8,128)} %broadcast_in_dim.19.ends_ref, f32[1024,128]{1,0:T(8,128)} %all-reduce.6.cloned.1.call-done.proj, f32[1024,384]{1,0:T(8,128)} %get-tuple-element.37.conv_out, bf16[128,384]{1,0:T(8,128)(2,1)} %concatenate.16.wstep, ...), custom_call_target="tpu_custom_call" | custom-call | tf_op jit(solution)/shard_map/pallas_call | solution.py:197
  205.5 1.2 dynamic-slice_convert_fusion
  206.7 1.5 collective-permute-start
  208.2 1.4 copy.61
  209.6 1.5 copy.62.wout
  211.1 14.3 %all-gather.19.cloned.1.call-done = bf16[1,1,512,1536]{3,2,1,0:T(8,128)(2,1)} async-done(((bf16[1,1,64,1536]{3,2,1,0:T(8,128)(2,1)}), bf16[1,1,512,1536]{3,2,1,0:T(8,128)(2,1)}) %all-gather.19.cloned.1.call-update) | async-done | bytes 1572880 | tf_op jit(solution)/shard_map/all_gather | solution.py:528
  225.4 0.7 copy-done.9
  226.2 5.8 %shard_map.239 = (bf16[512,384]{1,0:T(8,128)(2,1)}, bf16[512,1536]{1,0:T(8,128)(2,1)}, bf16[512,384]{1,0:T(8,128)(2,1)}, bf16[512,384]{1,0:T(8,128)(2,1)}) custom-call(s32[1]{0:T(128)} %bitcast.dir_ref, f32[1024,384]{1,0:T(8,128)} %get-tuple-element.38.y, bf16[512,384]{1,0:T(8,128)(2,1)} %copy-done.9, f32[512,384]{1,0:T(8,128)} %get-tuple-element.39.gate_in, ...), custom_call_target="tpu_custom_call" | custom-call | tf_op jit(solution)/shard_map/pallas_call | solution.py:52
  231.9 1.5 collective-permute-start.1
  233.4 2.7 fusion.ones
  236.6 1.8 convolution_convert_fusion
  238.4 0.7 copy.65
  239.2 1.2 copy.66
  240.4 3.7 all-to-all-start.5
  244.5 1.0 pad_maximum_fusion.g_low
  245.5 40.8 %shard_map.240 = (f32[1024,384]{1,0:T(8,128)}, f32[1024,128]{1,0:T(8,128)}, f32[128,384]{1,0:T(8,128)}, f32[2,384]{1,0:T(2,128)}, f32[16,384]{1,0:T(8,128)}) custom-call(s32[1]{0:T(128)} %bitcast.dir_ref, s32[2,8,128]{2,1,0:T(8,128)} %broadcast_in_dim.19.ends_ref, bf16[1024,384]{1,0:T(8,128)(2,1)} %pad_maximum_fusion.g_low, ...), custom_call_target="tpu_custom_call" | custom-call | tf_op jit(solution)/shard_map/pallas_call | solution.py:385
  286.5 1.7 copy-done.24
  288.2 1.7 convolution_convert_fusion.1
  289.9 3.5 all-to-all-start.4
  293.4 49.0 %all-reduce.8.cloned.1.call-done.grad_proj = f32[1024,128]{1,0:T(8,128)} async-done(((f32[1024,128]{1,0:T(8,128)}), f32[1024,128]{1,0:T(8,128)}) %all-reduce.8.cloned.1.call-update) | async-done | bytes 524304 | tf_op jit(solution)/shard_map/psum | solution.py:579
  342.4 11.2 %shard_map.241 = (bf16[1024,384]{1,0:T(8,128)(2,1)}, f32[384,128]{1,0:T(8,128)}, f32[5,384]{1,0:T(8,128)}) custom-call(s32[1]{0:T(128)} %bitcast.dir_ref, s32[2,8,128]{2,1,0:T(8,128)} %broadcast_in_dim.19.ends_ref, f32[1024,384]{1,0:T(8,128)} %get-tuple-element.43.grad_values, f32[1024,128]{1,0:T(8,128)} %all-reduce.8.cloned.1.call-done.grad_proj, ...), custom_call_target="tpu_custom_call" | custom-call | tf_op jit(solution)/shard_map/pallas_call | solution.py:52
  353.6 0.7 pad_maximum_fusion.2
  354.5 7.4 %all_to_all.50 = f32[2,119,192]{1,2,0:T(8,128)S(1)} all-to-all(f32[2,119,192]{1,2,0:T(8,128)S(1)} %bitcast.90), channel_id=1, replica_groups={{0,2},{1,3},{4,6},{5,7},{8,10},{9,11},{12,14},{13,15},{16,18},{17,19},{..., dimensions={0} | all-to-all | bytes 365568 | tf_op jit(solution)/shard_map/all_to_all | solution.py:531
  361.9 3.4 all-to-all-start.9
  365.3 1.6 collective-permute-start.2
  366.9 1.2 reduce_sum.59
  368.1 2.1 all-to-all-done.9
  370.1 3.5 all-to-all-start.6
  373.7 2.4 fusion.4
  376.1 5.8 %collective-permute-done.2 = bf16[1024,384]{1,0:T(8,128)(2,1)} collective-permute-done((bf16[1024,384]{1,0:T(8,128)(2,1)}, bf16[1024,384]{1,0:T(8,128)(2,1)}, u32[]{:S(2)}, u32[]{:S(2)}) %collective-permute-start.2) | collective-permute-done | bytes 786464 | tf_op jit(solution)/shard_map/ppermute | solution.py:583
  381.9 2.0 fusion.1
  383.9 6.4 %all-to-all-done.6 = bf16[8,384,96]{1,2,0:T(8,128)(2,1)S(1)} async-done(((bf16[8,384,96]{1,2,0:T(8,128)(2,1)}), bf16[8,384,96]{1,2,0:T(8,128)(2,1)S(1)}, u32[]{:S(2)}, u32[]{:S(2)}) %all-to-all-start.6) | async-done | bytes 589856 | tf_op jit(solution)/shard_map/all_to_all | solution.py:531
  390.4 11.9 %all_to_all.51 = bf16[2,768,192]{1,2,0:T(8,128)(2,1)} all-to-all(bf16[2,768,192]{1,2,0:T(8,128)(2,1)S(1)} %bitcast.91), channel_id=1, replica_groups={{0,2},{1,3},{4,6},{5,7},{8,10},{9,11},{12,14},{13,15},{16,18},{17,19},{..., dimensions={0} | all-to-all | bytes 1179648 | tf_op jit(solution)/shard_map/all_to_all | solution.py:531
  402.3 11.0 %all_to_all.52 = bf16[2,4,384,96]{2,3,1,0:T(8,128)(2,1)} all-to-all(bf16[2,4,384,96]{2,3,1,0:T(8,128)(2,1)S(1)} %bitcast.78), channel_id=1, replica_groups=mesh['dir'=2,'dp'=16] {'dir'}, dimensions={0} | all-to-all | bytes 1179648 | tf_op jit(solution)/shard_map/all_to_all | solution.py:612
  413.2 3.7 all-to-all-start.1
  417.0 0.8 constant_dynamic-slice_fusion.1
  417.8 1.8 constant_dynamic-slice_fusion
  419.6 8.0 %shard_map.242 = bf16[512,1536]{1,0:T(8,128)(2,1)} custom-call(bf16[512,384]{1,0:T(8,128)(2,1)} %bitcast.80, bf16[512,384]{1,0:T(8,128)(2,1)} %bitcast.81, bf16[512,384]{1,0:T(8,128)(2,1)} %get-tuple-element.48.grad_z, bf16[1536,384]{1,0:T(8,128)(2,1)} %copy.55.wx, bf16[1536,384]{1,0:T(8,128)(2,1)} %copy.56.wz), custom_call_target="tpu_custom_call" | custom-call | tf_op jit(solution)/shard_map/pallas_call | solution.py:52
  427.6 27.2 %all-to-all-done.1.mixed_parts = bf16[8,64,1536]{2,1,0:T(8,128)(2,1)S(1)} async-done(((bf16[8,64,1536]{2,1,0:T(8,128)(2,1)}), bf16[8,64,1536]{2,1,0:T(8,128)(2,1)S(1)}, u32[]{:S(2)}, u32[]{:S(2)}) %all-to-all-start.1) | async-done | bytes 1572896 | tf_op jit(solution)/shard_map/all_to_all | solution.py:531
  454.7 1.2 copy-done
  455.9 3.6 all-to-all-start.2
  459.5 2.1 convert_reduce_fusion.1
  463.8 0.7 copy.72
  466.6 0.9 convert_reduce_fusion.2
  468.8 1.6 reshape.155
  470.4 26.8 %all-to-all-done.2.grad_parts = bf16[8,64,1536]{2,1,0:T(8,128)(2,1)S(1)} async-done(((bf16[8,64,1536]{2,1,0:T(8,128)(2,1)}), bf16[8,64,1536]{2,1,0:T(8,128)(2,1)S(1)}, u32[]{:S(2)}, u32[]{:S(2)}) %all-to-all-start.2) | async-done | bytes 1572896 | tf_op jit(solution)/shard_map/all_to_all | solution.py:531
  497.2 1.2 copy-done.1
  498.4 3.4 shard_map.243
  501.8 0.7 reduce.1
  502.5 37.0 %all-reduce.2 = f32[1536]{0:T(1024)S(1)} all-reduce(f32[1536]{0:T(1024)S(1)} %reduce.1), channel_id=6, replica_groups=mesh['dir'=2,'dp'=16] {'dir','dp'}, use_global_device_ids=true, to_apply=%region_2.3.clone | all-reduce | flops 1536 | bytes 12288
  (126 shorter events, 16.7 us)
Async XLA Ops:
  7.2 2.2 copy-start.8
  7.2 76.1 %all-gather.13.cloned.1.call-start = ((), (), s32[]{:S(2)}) async-start(), calls=%async_computation.11 | async-start | bytes 1769472 | tf_op jit(solution)/shard_map/all_gather | solution.py:528
  7.9 77.8 %all-gather.15.cloned.1.call-start = ((), (), s32[]{:S(2)}) async-start(), calls=%async_computation.12 | async-start | bytes 1769472 | tf_op jit(solution)/shard_map/all_gather | solution.py:528
  8.7 91.1 %all-gather.11.cloned.1.call-start = ((), (), s32[]{:S(2)}) async-start(), calls=%async_computation.10 | async-start | bytes 3538944 | tf_op jit(solution)/shard_map/all_gather | solution.py:528
  11.0 7.7 %copy-start.20 = (s32[2,2]{1,0:T(2,128)S(1)}, s32[2,2]{1,0:T(2,128)}, u32[]{:S(2)}) copy-start(s32[2,2]{1,0:T(2,128)} %param.15) | copy-start | bytes 52
  11.0 25.1 %copy-start.19 = (bf16[1,4,192]{2,1,0:T(4,128)(2,1)S(1)}, bf16[1,4,192]{2,1,0:T(4,128)(2,1)}, u32[]{:S(2)}) copy-start(bf16[1,4,192]{2,1,0:T(4,128)(2,1)} %param.20) | copy-start | bytes 4612
  11.0 25.3 %copy-start.17 = (bf16[1,16,192]{2,1,0:T(8,128)(2,1)S(1)}, bf16[1,16,192]{2,1,0:T(8,128)(2,1)}, u32[]{:S(2)}) copy-start(bf16[1,16,192]{2,1,0:T(8,128)(2,1)} %param.25) | copy-start | bytes 18436
  11.0 25.4 %copy-start.14 = (bf16[1,96,192]{2,1,0:T(8,128)(2,1)S(1)}, bf16[1,96,192]{2,1,0:T(8,128)(2,1)}, u32[]{:S(2)}) copy-start(bf16[1,96,192]{2,1,0:T(8,128)(2,1)} %param.23) | copy-start | bytes 110596
  11.0 25.5 %copy-start.21 = (bf16[1,192]{1,0:T(2,128)(2,1)S(1)}, bf16[1,192]{1,0:T(2,128)(2,1)}, u32[]{:S(2)}) copy-start(bf16[1,192]{1,0:T(2,128)(2,1)} %param.21) | copy-start | bytes 1156
  11.0 25.6 %copy-start.22 = (bf16[1,192]{1,0:T(2,128)(2,1)S(1)}, bf16[1,192]{1,0:T(2,128)(2,1)}, u32[]{:S(2)}) copy-start(bf16[1,192]{1,0:T(2,128)(2,1)} %param.24) | copy-start | bytes 1156
  11.1 25.8 %copy-start.23 = (bf16[1,192]{1,0:T(2,128)(2,1)S(1)}, bf16[1,192]{1,0:T(2,128)(2,1)}, u32[]{:S(2)}) copy-start(bf16[1,192]{1,0:T(2,128)(2,1)} %param.26) | copy-start | bytes 1156
  11.1 31.6 %copy-start.27 = (u32[32]{0:T(128)S(1)}, u32[32]{0:T(128)}, u32[]{:S(2)}) copy-start(u32[32]{0:T(128)} %constant.63) | copy-start | bytes 388
  11.1 32.9 %copy-start.26 = (bf16[96]{0:T(256)(128)(2,1)S(1)}, bf16[96]{0:T(256)(128)(2,1)}, u32[]{:S(2)}) copy-start(bf16[96]{0:T(256)(128)(2,1)} %param.16) | copy-start | bytes 580
  11.1 67.3 %copy-start.15 = (bf16[1,192,128]{2,1,0:T(8,128)(2,1)S(1)}, bf16[1,192,128]{2,1,0:T(8,128)(2,1)}, u32[]{:S(2)}) copy-start(bf16[1,192,128]{2,1,0:T(8,128)(2,1)} %param.22) | copy-start | bytes 147460
  12.3 107.3 %all-to-all-start = ((bf16[8,384,96]{1,2,0:T(8,128)(2,1)}), bf16[8,384,96]{1,2,0:T(8,128)(2,1)S(1)}, u32[]{:S(2)}, u32[]{:S(2)}) async-start(bf16[8,384,96]{1,2,0:T(8,128)(2,1)} %reshape.136), calls=%async_computation | async-start | bytes 1179648 | tf_op jit(solution)/shard_map/all_to_all | solution.py:531
  18.7 156.1 %all-reduce.6.cloned.1.call-start = ((), (), s32[]{:S(2)}) async-start(), calls=%async_computation.13 | async-start | bytes 1048576 | tf_op jit(solution)/shard_map/psum | solution.py:560
  119.6 88.6 %all-gather.17.cloned.1.call-start = ((), (), s32[]{:S(2)}) async-start(), calls=%async_computation.15 | async-start | bytes 1769472 | tf_op jit(solution)/shard_map/all_gather | solution.py:552
  119.7 0.8 copy-start.2
  120.5 104.9 %all-gather.19.cloned.1.call-start = ((), (), s32[]{:S(2)}) async-start(), calls=%async_computation.16 | async-start | bytes 1769472 | tf_op jit(solution)/shard_map/all_gather | solution.py:528
  206.7 18.7 %collective-permute-start = (bf16[512,384]{1,0:T(8,128)(2,1)S(1)}, bf16[512,384]{1,0:T(8,128)(2,1)S(1)}, u32[]{:S(2)}, u32[]{:S(2)}) collective-permute-start(bf16[512,384]{1,0:T(8,128)(2,1)S(1)} %dynamic-slice_convert_fusion), channel_id=1, source_target_pairs={{0,16},{16,0},{1,17},{17,1},{2,18},{18,2},{3,19},{19,3},{4,20},{20... | collective-permute-start | bytes 1179656 | tf_op jit(solution)/shard_map/ppermute | solution.py:565
  225.4 0.7 copy-start.9
  226.2 10.5 %copy-start.7 = (bf16[1,1,512,1536]{3,2,1,0:T(8,128)(2,1)S(1)}, bf16[1,1,512,1536]{3,2,1,0:T(8,128)(2,1)}, u32[]{:S(2)}) copy-start(bf16[1,1,512,1536]{3,2,1,0:T(8,128)(2,1)} %all-gather.19.cloned.1.call-done) | copy-start | bytes 4718596
  231.9 12.5 %collective-permute-start.1 = (bf16[512,384]{1,0:T(8,128)(2,1)}, bf16[512,384]{1,0:T(8,128)(2,1)S(1)}, u32[]{:S(2)}, u32[]{:S(2)}) collective-permute-start(bf16[512,384]{1,0:T(8,128)(2,1)} %get-tuple-element.41), channel_id=1, source_target_pairs={{0,16},{16,0},{1,17},{17,1},{2,18},{18,2},{3,19},{19,3},{4,20},{20... | collective-permute-start | bytes 1179656 | tf_op jit(solution)/shard_map/ppermute | solution.py:568
  236.1 50.2 %collective-permute-start.3 = (bf16[512,384]{1,0:T(8,128)(2,1)}, bf16[512,384]{1,0:T(8,128)(2,1)S(1)}, u32[]{:S(2)}, u32[]{:S(2)}) collective-permute-start(bf16[512,384]{1,0:T(8,128)(2,1)} %get-tuple-element.48.grad_z), channel_id=1, source_target_pairs={{0,16},{16,0},{1,17},{17,1},{2,18},{18,2},{3,19},{19,3},{4,20},{20... | collective-permute-start | bytes 1179656 | tf_op jit(solution)/shard_map/ppermute | solution.py:595
  240.4 4.0 copy-start.10
  240.4 49.5 %all-to-all-start.5 = ((bf16[2,4,2,384,96]{3,4,2,1,0:T(8,128)(2,1)}), bf16[2,4,2,384,96]{3,4,2,1,0:T(8,128)(2,1)S(1)}, u32[]{:S(2)}, u32[]{:S(2)}) async-start(bf16[2,4,2,384,96]{3,4,2,1,0:T(8,128)(2,1)} %copy.66), calls=%async_computation.5 | async-start | bytes 2359296 | tf_op jit(solution)/shard_map/all_to_all | solution.py:531
  244.1 98.3 %all-reduce.8.cloned.1.call-start = ((), (), s32[]{:S(2)}) async-start(), calls=%async_computation.14 | async-start | bytes 1048576 | tf_op jit(solution)/shard_map/psum | solution.py:579
  245.5 40.9 %copy-start.6 = (bf16[512,384]{1,0:T(8,128)(2,1)S(1)}, bf16[512,384]{1,0:T(8,128)(2,1)}, u32[]{:S(2)}) copy-start(bf16[512,384]{1,0:T(8,128)(2,1)} %get-tuple-element.48.grad_z) | copy-start | bytes 1179652
  286.3 1.9 copy-start.24
  288.2 5.2 copy-start.13
  289.9 64.6 %all-to-all-start.4 = ((bf16[2,768,192]{1,2,0:T(8,128)(2,1)}), bf16[2,768,192]{1,2,0:T(8,128)(2,1)S(1)}, u32[]{:S(2)}, u32[]{:S(2)}) async-start(bf16[2,768,192]{1,2,0:T(8,128)(2,1)} %bitcast.30), calls=%async_computation.4 | async-start | bytes 1179648 | tf_op jit(solution)/shard_map/all_to_all | solution.py:531
  342.4 11.2 %copy-start.16 = (f32[16,384]{1,0:T(8,128)S(1)}, f32[16,384]{1,0:T(8,128)}, u32[]{:S(2)}) copy-start(f32[16,384]{1,0:T(8,128)} %get-tuple-element.56) | copy-start | bytes 73732
  342.4 11.2 %copy-start.18 = (f32[2,384]{1,0:T(2,128)S(1)}, f32[2,384]{1,0:T(2,128)}, u32[]{:S(2)}) copy-start(f32[2,384]{1,0:T(2,128)} %get-tuple-element.55) | copy-start | bytes 9220
  354.5 15.6 %copy-start.3 = (bf16[2,768,192]{1,2,0:T(8,128)(2,1)}, bf16[2,768,192]{1,2,0:T(8,128)(2,1)S(1)}, u32[]{:S(2)}) copy-start(bf16[2,768,192]{1,2,0:T(8,128)(2,1)S(1)} %all-to-all-done.4) | copy-start | bytes 1769476
  361.9 8.2 %all-to-all-start.9 = ((f32[2,192,128]{2,1,0:T(8,128)}), f32[2,192,128]{2,1,0:T(8,128)S(1)}, u32[]{:S(2)}, u32[]{:S(2)}) async-start(f32[2,192,128]{2,1,0:T(8,128)} %bitcast.92), calls=%async_computation.9 | async-start | bytes 393216 | tf_op jit(solution)/shard_map/all_to_all | solution.py:531
  365.3 8.4 %copy-start.11 = (bf16[1024,384]{1,0:T(8,128)(2,1)S(1)}, bf16[1024,384]{1,0:T(8,128)(2,1)}, u32[]{:S(2)}) copy-start(bf16[1024,384]{1,0:T(8,128)(2,1)} %get-tuple-element.47) | copy-start | bytes 2359300
  365.3 16.6 %collective-permute-start.2 = (bf16[1024,384]{1,0:T(8,128)(2,1)}, bf16[1024,384]{1,0:T(8,128)(2,1)}, u32[]{:S(2)}, u32[]{:S(2)}) collective-permute-start(bf16[1024,384]{1,0:T(8,128)(2,1)} %get-tuple-element.47), channel_id=1, source_target_pairs={{0,16},{16,0},{1,17},{17,1},{2,18},{18,2},{3,19},{19,3},{4,20},{20... | collective-permute-start | bytes 2359304 | tf_op jit(solution)/shard_map/ppermute | solution.py:583
  370.1 20.2 %all-to-all-start.6 = ((bf16[8,384,96]{1,2,0:T(8,128)(2,1)}), bf16[8,384,96]{1,2,0:T(8,128)(2,1)S(1)}, u32[]{:S(2)}, u32[]{:S(2)}) async-start(bf16[8,384,96]{1,2,0:T(8,128)(2,1)} %bitcast.33), calls=%async_computation.6 | async-start | bytes 1179648 | tf_op jit(solution)/shard_map/all_to_all | solution.py:531
  373.7 8.2 %copy-start.25 = (bf16[1024,1536]{1,0:T(8,128)(2,1)S(1)}, bf16[1024,1536]{1,0:T(8,128)(2,1)}, u32[]{:S(2)}) copy-start(bf16[1024,1536]{1,0:T(8,128)(2,1)} %get-tuple-element.52) | copy-start | bytes 9437188
  413.2 3.7 copy-start.12
  413.2 41.5 %all-to-all-start.1 = ((bf16[8,64,1536]{2,1,0:T(8,128)(2,1)}), bf16[8,64,1536]{2,1,0:T(8,128)(2,1)S(1)}, u32[]{:S(2)}, u32[]{:S(2)}) async-start(bf16[8,64,1536]{2,1,0:T(8,128)(2,1)} %bitcast.79), calls=%async_computation.1 | async-start | bytes 3145728 | tf_op jit(solution)/shard_map/all_to_all | solution.py:531
  454.7 1.2 copy-start
  455.9 41.3 %all-to-all-start.2 = ((bf16[8,64,1536]{2,1,0:T(8,128)(2,1)}), bf16[8,64,1536]{2,1,0:T(8,128)(2,1)S(1)}, u32[]{:S(2)}, u32[]{:S(2)}) async-start(bf16[8,64,1536]{2,1,0:T(8,128)(2,1)} %bitcast.72), calls=%async_computation.2 | async-start | bytes 3145728 | tf_op jit(solution)/shard_map/all_to_all | solution.py:531
  459.5 7.1 %copy-start.4 = (bf16[2,768,192]{1,2,0:T(8,128)(2,1)S(1)}, bf16[2,768,192]{1,2,0:T(8,128)(2,1)}, u32[]{:S(2)}) copy-start(bf16[2,768,192]{1,2,0:T(8,128)(2,1)} %all_to_all.51) | copy-start | bytes 1769476
  461.6 5.9 %copy-start.5 = (bf16[2,4,384,96]{2,3,1,0:T(8,128)(2,1)S(1)}, bf16[2,4,384,96]{2,3,1,0:T(8,128)(2,1)}, u32[]{:S(2)}) copy-start(bf16[2,4,384,96]{2,3,1,0:T(8,128)(2,1)} %all_to_all.52) | copy-start | bytes 1769476
  497.2 1.2 copy-start.1
Sparse Core Ops, SparseCore 0:
  9.6 25.4 all-gather.12
  36.6 23.1 all-gather.14
  61.4 38.3 all-gather.10
  119.7 55.0 all-reduce.5
  176.8 21.7 all-gather.16
  200.3 25.0 all-gather.18
  286.4 55.9 all-reduce.7

commit v2 on v0

v2 whole, which is shorter than its diff:
```python
from functools import partial

import jax
import jax.numpy as jnp
from jax import lax
from jax.experimental import pallas as pl
from jax.experimental.pallas import tpu as pltpu
from jax.sharding import PartitionSpec as P

f32 = jnp.float32
bf16 = jnp.bfloat16
EPS = 1e-05
DT_RANK = 96
STATE = 16
TAPS = 4
ZS = 4
TP = 8
PACK = 128
HALF = 64
CHUNK = 16
NSTEP = 4
LOG2E = 1.4426950408889634
LN2 = 0.6931471805599453
BIG = 1e9
PAD = 24
TAP_ROW, BIAS_ROW, STEP_ROW, SKIP_ROW, DECAY_ROW, SMALL_ROWS = 96, 100, 101, 102, 103, 128


def mm(left, right):
    return jnp.dot(left, right, preferred_element_type=f32)


def mm_nt(left, right):
    return lax.dot_general(left, right, (((1,), (1,)), ((), ())), preferred_element_type=f32)


def mm_tn(left, right):
    return lax.dot_general(left, right, (((0,), (0,)), ((), ())), preferred_element_type=f32)


def segment_of(t, ends):
    t = t.astype(f32) if hasattr(t, "astype") else float(t)
    return (t >= ends[0]).astype(f32) + (t >= ends[1]).astype(f32)


def rows8(t):
    return pl.ds(pl.multiple_of(t * 8, 8), 8)


def span(start, size):
    return pl.ds(pl.multiple_of(start * size, size), size)


def sigmoid(v):
    return 1.0 / (1.0 + jnp.exp(-v))


def softplus(v):
    return jnp.maximum(v, 0.0) + jnp.log1p(jnp.exp(-jnp.abs(v)))


def wide(mask, ch):
    return jnp.concatenate([mask] * (ch // 128), axis=1)


def tiles(v):
    total = v[:, 0:128]
    for at in range(128, v.shape[1], 128):
        total = total + v[:, at : at + 128]
    return total


class Net:
    def __init__(self, reps, send, recv, local):
        self.reps, self.send, self.recv, self.local = reps, send, recv, local
        self.s = lax.axis_index("dir")
        p = lax.axis_index("dp")
        self.i = lax.rem(p, 2)
        self.y = lax.rem(p // 2, reps)
        self.z = p // (2 * reps)
        self.used = 0
        self.moved = 0
        self.copies = []
        self.saves = []

    def place(self, s, z, y, i):
        return (s, (z * self.reps + y) * 2 + i)

    def flip(self, m):
        if m == 1:
            return self.z + 1 - 2 * lax.rem(self.z, 2)
        if m == 2:
            return lax.rem(self.z + 2, ZS)
        return ZS - 1 - self.z

    def over_x(self):
        return self.place(1 - self.s, self.z, self.y, self.i)

    def sibling(self):
        return self.place(self.s, self.z, self.y, 1 - self.i)

    def along_z(self, m):
        return self.place(self.s, self.flip(m), self.y, self.i)

    def shared(self, m):
        z = self.flip(m // 2) if m // 2 else self.z
        i = 1 - self.i if m % 2 else self.i
        return z, i

    def to_shared(self, m):
        z, i = self.shared(m)
        return self.place(self.s, z, self.y, i)

    def y_at(self, d):
        return lax.rem(self.y + d, self.reps)

    def along_y(self, d):
        return self.place(self.s, self.z, self.y_at(d), self.i)

    def greet(self):
        peers = [self.over_x()] + [self.to_shared(m) for m in range(1, TP)]
        peers += [self.along_y(d) for d in range(1, self.reps)]
        barrier = pltpu.get_barrier_semaphore()
        for peer in peers:
            pl.semaphore_signal(barrier, inc=1, device_id=peer, device_id_type=pl.DeviceIdType.MESH)
        pl.semaphore_wait(barrier, len(peers))

    def copy(self, source, target, peer):
        k = self.used
        self.used += 1
        c = pltpu.make_async_remote_copy(
            src_ref=source,
            dst_ref=target,
            send_sem=self.send.at[k],
            recv_sem=self.recv.at[k],
            device_id=peer,
            device_id_type=pl.DeviceIdType.MESH,
        )
        c.start()
        self.copies.append(c)
        return c

    def load(self, source, target):
        c = pltpu.make_async_copy(source, target, self.local.at[self.moved])
        self.moved += 1
        c.start()
        return c

    def save(self, source, target):
        self.saves.append(self.load(source, target))

    def finish(self):
        for c in self.copies:
            c.wait_send()
        for c in self.saves:
            c.wait()


class Reduce:
    def __init__(self, net, part, fold, out_low, in_low, total):
        self.net, self.part, self.fold, self.out_low, self.in_low, self.total = (
            net, part, fold, out_low, in_low, total,
        )
        self.rows = part.shape[0] // 2
        self.block = self.rows // ZS
        self.first = net.copy(part.at[span(1 - net.i, self.rows)], fold, net.sibling())

    def across_z(self):
        net, fold = self.net, self.fold
        self.first.wait_recv()
        fold[...] = self.part[span(net.i, self.rows), :] + fold[...]
        self.out_low[...] = fold[...].astype(bf16).reshape(ZS, self.block, 128)
        self.cs = [
            net.copy(self.out_low.at[net.flip(m)], self.in_low.at[m - 1], net.along_z(m))
            for m in range(1, ZS)
        ]

    def give(self):
        net, total = self.net, self.total
        mine = span(net.i * ZS + net.z, self.block)
        value = self.fold[span(net.z, self.block), :]
        for m in range(1, ZS):
            self.cs[m - 1].wait_recv()
            value = value + self.in_low[m - 1].astype(f32)
        total[mine, :] = value.astype(bf16)
        self.cs = [net.copy(total.at[mine], total.at[mine], net.along_z(m)) for m in range(1, ZS)]
        self.ds = [net.copy(total.at[mine], total.at[mine], net.sibling())]

    def end(self):
        net, total = self.net, self.total
        for m in range(1, ZS):
            self.cs[m - 1].wait_recv()
            there = span(net.i * ZS + net.flip(m), self.block)
            self.ds.append(net.copy(total.at[there], total.at[there], net.sibling()))
        for d in self.ds:
            d.wait_recv()


REDUCE_SCRATCH = (
    pltpu.VMEM((TP * PACK // 2, 128), f32),
    pltpu.VMEM((ZS, PACK, 128), bf16),
    pltpu.VMEM((ZS - 1, PACK, 128), bf16),
)


def fused(kernel, name_id, copies, moves, outs, args, scratch):
    return pl.pallas_call(
        kernel,
        out_shape=tuple(o for o, _ in outs),
        in_specs=[pl.BlockSpec(memory_space=m) for _, m in args],
        out_specs=tuple(pl.BlockSpec(memory_space=m) for _, m in outs),
        scratch_shapes=list(scratch)
        + [pltpu.SemaphoreType.DMA((n,)) for n in (copies, copies, moves)],
        compiler_params=pltpu.CompilerParams(
            collective_id=name_id, has_side_effects=True, vmem_limit_bytes=63 << 20
        ),
    )(*(a for a, _ in args))


def front_kernel(
    reps,
    grids, tokens, gain_own, wx_own, wz_own, wstep, taps_own, bias_own, step_own, skip_own, decay_own,
    wstate_own, wout_own, cot_own,
    normed_out, conv_in_out, conv_pre_out, conv_out_out, gate_out, tok_out, wx_out, wz_out,
    wout_out, cot_out, proj, gain, ends_out, small, wstate,
    tok_all, normed, wx_all, wz_all, wx, wz, small_all, wstate_all, wout_send, wout_in, meta_all, raw,
    conv_in, conv_pre, conv_out, gate_in, part,
    fold, out_low, in_low, send, recv, local,
):
    net = Net(reps, send, recv, local)
    s, z, y, i = net.s, net.z, net.y, net.i
    j = z * 2 + i
    cols, width = wx_own.shape
    ch = reps * cols
    piece = wout_own.shape[0]
    mine = span(j, PACK)
    mine_half = pl.ds(pl.multiple_of(j * PACK + s * HALF, HALF), HALF)
    tok_all[mine, :] = tokens[...]
    first_end = (grids[0, 0] * grids[0, 1]).astype(f32)
    second_end = first_end + (grids[1, 0] * grids[1, 1]).astype(f32)
    row = lax.broadcasted_iota(jnp.int32, (16, 128), 0)
    gain_row = jnp.concatenate([gain_own[...].astype(f32), jnp.zeros((1, 128 - piece), f32)], axis=1)
    meta = jnp.where(row == 0, gain_row, jnp.where(row == 1, first_end, second_end))
    meta_all[y, j] = meta.astype(bf16)
    wx_all[y] = wx_own[...]
    wz_all[y] = wz_own[...]
    small_rows = [wstep, taps_own, bias_own, step_own, skip_own, decay_own]
    small_rows = [ref[...].astype(f32) for ref in small_rows]
    small_rows.append(jnp.zeros((SMALL_ROWS - DECAY_ROW - STATE, cols), f32))
    small_all[y] = jnp.concatenate(small_rows, axis=0).astype(bf16)
    wstate_all[y] = wstate_own[...]
    net.greet()
    from_z = [net.copy(tok_all.at[mine_half], tok_all.at[mine_half], net.along_z(m)) for m in range(1, ZS)]
    from_core = [net.copy(tok_all.at[mine], tok_all.at[mine], net.sibling())]
    metas = [net.copy(meta_all.at[y, j], meta_all.at[y, j], net.to_shared(m)) for m in range(1, TP)]
    first_y = []
    for d in range(1, reps):
        for ref in (wx_all, small_all, wstate_all):
            first_y.append(net.copy(ref.at[y], ref.at[y], net.along_y(d)))
    cot_x = net.copy(cot_own, cot_out, net.over_x())
    for c in metas:
        c.wait_recv()
    meta_y = [net.copy(meta_all.at[y], meta_all.at[y], net.along_y(d)) for d in range(1, reps)]
    late_y = [net.copy(wz_all.at[y], wz_all.at[y], net.along_y(d)) for d in range(1, reps)]

    conv_in[0:PAD, :] = jnp.zeros((PAD, ch), f32)
    conv_in[PAD + 8 * PACK :, :] = jnp.zeros((PAD, ch), f32)
    for b in range(TP):
        both = meta_all[y, b].astype(f32)
        ends_out[0, b : b + 1, :] = both[1:2, :]
        ends_out[1, b : b + 1, :] = both[2:3, :]
    for p in range(TP * reps):
        zp, yp, ip = p // (2 * reps), (p // 2) % reps, p % 2
        wout_send[zp * 2 + ip, yp] = wout_own[:, p * cols : (p + 1) * cols]

    from_x = []
    for m in range(1, ZS):
        from_z[m - 1].wait_recv()
        rows = pl.ds(pl.multiple_of((net.flip(m) * 2 + i) * PACK + s * HALF, HALF), HALF)
        from_x.append(net.copy(tok_all.at[rows], tok_all.at[rows], net.over_x()))
        from_core.append(net.copy(tok_all.at[rows], tok_all.at[rows], net.sibling()))
    wout_in[j] = wout_send[j]
    wout_z = []
    for m in range(1, TP):
        zm, im = net.shared(m)
        wout_z.append(net.copy(wout_send.at[zm * 2 + im], wout_in.at[j], net.to_shared(m)))

    for c in meta_y + first_y:
        c.wait_recv()
    for p in range(TP * reps):
        zp, yp, ip = p // (2 * reps), (p // 2) % reps, p % 2
        gain[:, p * piece : (p + 1) * piece] = meta_all[yp, zp * 2 + ip].astype(f32)[0:1, 0:piece]
    for r in range(reps):
        wx[r * cols : (r + 1) * cols, :] = wx_all[r]
        small[:, r * cols : (r + 1) * cols] = small_all[r]
        wstate[r * cols : (r + 1) * cols, :] = wstate_all[r]
    net.save(wx, wx_out)

    def take(block):
        rows = span(block, PACK)
        x = tok_all[rows, :].astype(f32)
        inv = lax.rsqrt(jnp.mean(x * x, axis=1, keepdims=True) + EPS)
        low = (x * inv * gain[...]).astype(bf16)
        for h in range(2):
            normed[h, span(block, HALF), :] = low[h * HALF : (h + 1) * HALF]
        raw[rows, :] = mm_nt(low, wx[...])

    from_core[0].wait_recv()

    def take_pair(k, carry):
        take(z * 2 + k)
        return carry

    lax.fori_loop(0, 2, take_pair, 0)
    for m in range(1, ZS):
        from_x[m - 1].wait_recv()
        rows = pl.ds(pl.multiple_of((net.flip(m) * 2 + i) * PACK + (1 - s) * HALF, HALF), HALF)
        from_core.append(net.copy(tok_all.at[rows], tok_all.at[rows], net.sibling()))
    for m in range(1, ZS):
        from_core[m].wait_recv()
        from_core[m + ZS - 1].wait_recv()

        def take_far(k, carry, m=m):
            take(net.flip(m) * 2 + k)
            return carry

        lax.fori_loop(0, 2, take_far, 0)
    net.save(normed, normed_out)
    net.save(tok_all, tok_out)

    def in_order(b, carry):
        size = 32
        parts = [raw[pl.ds(pl.multiple_of(p * PACK + b * size, size), size), :] for p in range(8)]
        x = jnp.stack(parts, axis=1).reshape(8 * size, ch)
        conv_in[pl.ds(pl.multiple_of(PAD + b * size * 8, 8), 8 * size), :] = x
        return carry

    lax.fori_loop(0, PACK // 32, in_order, 0)
    ends = (ends_out[0], ends_out[1])
    sgn = 1 - 2 * s
    taps = small[TAP_ROW : TAP_ROW + 16, :].astype(f32)

    def conv_step(t, carry):
        seg = segment_of(t, ends)
        total = taps[4:5, :] + taps[3:4, :] * conv_in[rows8(t + 3), :]
        for k in range(1, TAPS):
            there = t - k * sgn
            same = wide((segment_of(there, ends) == seg).astype(f32), ch)
            total = total + taps[3 - k : 4 - k, :] * (conv_in[rows8(there + 3), :] * same)
        conv_pre[rows8(t), :] = total
        act = total * sigmoid(total)
        conv_out[rows8(t), :] = act.astype(bf16).astype(f32)
        return carry

    lax.fori_loop(0, PACK, conv_step, 0, unroll=2)
    part[...] = mm(conv_out[...].astype(bf16), wstate[...])
    sum_proj = Reduce(net, part, fold, out_low, in_low, proj)
    net.save(conv_in, conv_in_out)
    net.save(conv_pre, conv_pre_out)
    net.save(conv_out, conv_out_out)
    sum_proj.across_z()
    for c in late_y:
        c.wait_recv()
    for r in range(reps):
        wz[r * cols : (r + 1) * cols, :] = wz_all[r]
    net.save(wz, wz_out)
    gate_in[...] = mm_nt(normed[1 - s], wz[...])
    net.save(gate_in, gate_out)
    sum_proj.give()
    for c in wout_z:
        c.wait_recv()
    net.save(wout_in, wout_out)
    cot_x.wait_recv()
    sum_proj.end()
    net.finish()


def front(reps, grids, tokens, gain, wx, wz, wstep, taps, bias, step, skip, decay, wstate, wout, cot):
    cols, width = wx.shape
    ch = reps * cols
    rows = TP * PACK
    half = rows // 2
    piece = wout.shape[0]
    sds = jax.ShapeDtypeStruct
    V, H = pltpu.VMEM, pl.ANY
    args = [(grids, pltpu.SMEM), (tokens, V), (gain, V), (wx, V), (wz, V), (wstep, V), (taps, V), (bias, V)]
    args += [(step, V), (skip, V), (decay, V), (wstate, V), (wout, V), (cot, H)]
    outs = (
        (sds((2, half, width), bf16), H),
        (sds((rows + 2 * PAD, ch), f32), H),
        (sds((rows, ch), f32), H),
        (sds((rows, ch), f32), H),
        (sds((half, ch), f32), H),
        (sds((rows, width), bf16), H),
        (sds((ch, width), bf16), H),
        (sds((ch, width), bf16), H),
        (sds((TP, reps, piece, cols), bf16), H),
        (sds((HALF, width), bf16), H),
        (sds((rows, 128), bf16), V),
        (sds((1, width), f32), V),
        (sds((2, 8, 128), f32), V),
        (sds((SMALL_ROWS, ch), bf16), V),
        (sds((ch, 128), bf16), V),
    )
    scratch = (
        V((rows, width), bf16),
        V((2, half, width), bf16),
        V((reps, cols, width), bf16),
        V((reps, cols, width), bf16),
        V((ch, width), bf16),
        V((ch, width), bf16),
        V((reps, SMALL_ROWS, cols), bf16),
        V((reps, cols, 128), bf16),
        V((TP, reps, piece, cols), bf16),
        V((TP, reps, piece, cols), bf16),
        V((reps, TP, 16, 128), bf16),
        V((rows, ch), f32),
        V((rows + 2 * PAD, ch), f32),
        V((rows, ch), f32),
        V((rows, ch), f32),
        V((half, ch), f32),
        V((rows, 128), f32),
    ) + REDUCE_SCRATCH
    copies = 3 + 1 + 7 + 1 + 6 + 7 + 3 + 11 + 5 * (reps - 1)
    return fused(partial(front_kernel, reps), 1, copies, 9, outs, args, scratch)


def core_kernel(
    reps,
    proj_low, conv_out, small, ends_in, tokens, gate_hbm, wout_hbm, cot_hbm, normed_hbm,
    grad_values, grad_proj, gate_both, mixed, rows_grad, grad_wout, grad_wz,
    gate_in, wout_all, wout, cot, normed, ones, hprev, proj, step, decay_step, u, state, acc_ref, rate_ref, y_send, y_in,
    gated, mixed_part, mixed_core, mixed_low, mixed_z, mixed_sum, g, g_send, g_in,
    s1, s2, pb, pc, bias_acc, skip_acc, part,
    out_send, out_y, out_low, out_all, out_x, wz_low, wz_in,
    fold, low_out, low_in, send, recv, local,
):
    net = Net(reps, send, recv, local)
    s, z, yi, i = net.s, net.z, net.y, net.i
    sgn = 1 - 2 * s
    gh = 1 - s
    ch = conv_out.shape[1]
    cols = ch // reps
    half = TP * HALF
    rounds = HALF // CHUNK
    size = CHUNK * 8
    piece = out_all.shape[1]
    width = tokens.shape[1]
    y = grad_values
    loads = [
        net.load(gate_hbm, gate_in),
        net.load(normed_hbm, normed),
        net.load(wout_hbm, wout_all.at[yi]),
        net.load(cot_hbm, cot.at[span(z * 2 + i, HALF)]),
    ]
    net.greet()
    cot_mine = span(z * 2 + i, HALF)
    cot_z = [net.copy(cot_hbm, cot.at[cot_mine], net.along_z(m)) for m in range(1, ZS)]
    cot_core = [net.copy(cot_hbm, cot.at[cot_mine], net.sibling())]
    wout_y = [net.copy(wout_hbm, wout_all.at[yi], net.along_y(d)) for d in range(1, reps)]
    for k in range(2):
        source = lax.broadcasted_iota(jnp.int32, (STATE * 128, 128), 0) // 128
        target = lax.broadcasted_iota(jnp.int32, (STATE * 128, 128), 1)
        ones[k] = (target == DT_RANK + k * STATE + source).astype(f32).astype(bf16)
    proj[...] = proj_low[...].astype(f32)
    wstep = jnp.where(lax.broadcasted_iota(jnp.int32, (128, ch), 0) < DT_RANK, small[...], 0.0).astype(bf16)
    rows_grad[...] = jnp.zeros_like(rows_grad)
    rate_ref[...] = -LOG2E * jnp.exp(small[DT_RANK:, :].astype(f32)[DECAY_ROW - DT_RANK : DECAY_ROW - DT_RANK + STATE, :])
    vectors = small[DT_RANK : DT_RANK + 16, :].astype(f32)
    step_bias = vectors[STEP_ROW - DT_RANK : STEP_ROW - DT_RANK + 1, :]
    skip = vectors[SKIP_ROW - DT_RANK : SKIP_ROW - DT_RANK + 1, :]
    ends = (ends_in[0], ends_in[1])

    def prepare(block):
        rows = span(block, size)
        pre = mm(proj[rows, :].astype(bf16), wstep) + step_bias
        step_all = softplus(pre)
        values = conv_out[rows, :]
        step[...] = step_all
        u[...] = step_all * values
        for k in range(CHUNK):
            t = block * CHUNK + k
            fresh = segment_of(t, ends) != segment_of(t - sgn, ends)
            decay_step[8 * k : 8 * k + 8, :] = jnp.where(
                wide(fresh, ch), BIG, step_all[8 * k : 8 * k + 8, :]
            )
        return rows, pre, values

    def rates(n0):
        return [jnp.broadcast_to(rate_ref[n : n + 1, :], (8, ch)) for n in range(n0, n0 + NSTEP)]

    state[...] = jnp.zeros_like(state)

    def forward(c, carry):
        block = c + s * (2 * rounds - 1 - 2 * c)
        rows, _, values = prepare(block)
        y[rows, :] = skip * values
        for n0 in range(0, STATE, NSTEP):
            rate = rates(n0)

            def body(k, hs):
                r = s * (CHUNK - 1 - k) + (1 - s) * k
                t = block * CHUNK + r
                pv = proj[rows8(t), :]
                st = decay_step[rows8(r), :]
                uv = u[rows8(r), :]
                total = y[rows8(t), :]
                new = []
                for m in range(NSTEP):
                    n = n0 + m
                    hprev[t, n] = hs[m]
                    h = jnp.exp2(st * rate[m]) * hs[m] + uv * pv[:, DT_RANK + n : DT_RANK + n + 1]
                    total = total + h * pv[:, DT_RANK + STATE + n : DT_RANK + STATE + n + 1]
                    new.append(h)
                y[rows8(t), :] = total
                return tuple(new)

            hs = lax.fori_loop(0, CHUNK, body, tuple(state[n] for n in range(n0, n0 + NSTEP)), unroll=2)
            for m in range(NSTEP):
                state[n0 + m] = hs[m]
        return carry

    lax.fori_loop(0, rounds, forward, 0)
    y_send[...] = y[span(s, half), :].astype(bf16)
    y_copy = net.copy(y_send, y_in, net.over_x())
    lax.fori_loop(rounds, 2 * rounds - 1, forward, 0)
    for m in range(1, ZS):
        cot_z[m - 1].wait_recv()
        rows = span(net.flip(m) * 2 + i, HALF)
        cot_core.append(net.copy(cot.at[rows], cot.at[rows], net.sibling()))
    lax.fori_loop(2 * rounds - 1, 2 * rounds, forward, 0)
    for c in loads:
        c.wait()
    for c in wout_y:
        c.wait_recv()
    for p in range(TP * reps):
        zp, yp, ip = p // (2 * reps), (p // 2) % reps, p % 2
        for r in range(reps):
            wout[p * piece : (p + 1) * piece, r * cols : (r + 1) * cols] = wout_all[yp, zp * 2 + ip, r]
    for c in cot_core:
        c.wait_recv()
    y_copy.wait_recv()

    y_own = y[span(gh, half), :] + y_in[...].astype(f32)
    summed = jnp.swapaxes(y_own.reshape(HALF, 8, ch), 0, 1).reshape(half, ch)
    gate = gate_in[...]
    sig = sigmoid(gate)
    act = gate * sig
    grad_gated = mm(cot[...], wout[...])
    back = grad_gated * act
    back = jnp.swapaxes(back.reshape(8, HALF, ch), 0, 1).reshape(half, ch)
    g[span(gh, half), :] = back
    g_send[...] = back.astype(bf16)
    g_copy = net.copy(g_send, g_in, net.over_x())
    gate_both[gh] = (grad_gated * summed * sig * (1.0 + gate * (1.0 - sig))).astype(bf16)
    gate_copy = net.copy(gate_both.at[gh], gate_both.at[gh], net.over_x())
    low = (summed * act).astype(bf16)
    gated[...] = low
    mixed_part[...] = mm_nt(low, wout[...]).astype(bf16).reshape(mixed_part.shape)
    mixed_copy = net.copy(mixed_part.at[:, 1 - i], mixed_core, net.sibling())
    part_out = mm_tn(cot[...], gated[...]).astype(bf16)
    for q in range(ZS):
        for r in range(reps):
            at = (q * reps + r) * 2 * piece
            out_send[r, q * 2 * piece : (q + 1) * 2 * piece, :] = part_out[at : at + 2 * piece, :]
    out_copies = [
        net.copy(out_send.at[net.y_at(d)], out_y.at[d - 1], net.along_y(d)) for d in range(1, reps)
    ]

    state[...] = jnp.zeros_like(state)
    acc_ref[...] = jnp.zeros_like(acc_ref)
    bias_acc[...] = jnp.zeros_like(bias_acc)
    skip_acc[...] = jnp.zeros_like(skip_acc)

    def backward(c, carry):
        block = (1 - s) * (2 * rounds - 1 - c) + s * c
        rows, pre, values = prepare(block)
        s1[...] = jnp.zeros_like(s1)
        s2[...] = jnp.zeros_like(s2)
        for n0 in range(0, STATE, NSTEP):
            rate = rates(n0)

            def body(k, both):
                lams, accs = both
                r = s * k + (1 - s) * (CHUNK - 1 - k)
                t = block * CHUNK + r
                here = rows8(r)
                pv = proj[rows8(t), :]
                gv = g[rows8(t), :]
                uv = u[here, :]
                stv = step[here, :]
                st = decay_step[here, :]
                one = s1[here, :]
                two = s2[here, :]
                new_lams, new_accs = [], []
                for m in range(NSTEP):
                    n = n0 + m
                    a = jnp.exp2(st * rate[m])
                    ah = a * hprev[t, n]
                    lam = gv * pv[:, DT_RANK + STATE + n : DT_RANK + STATE + n + 1] + lams[m]
                    w = lam * ah
                    new_lams.append(a * lam)
                    two = two + rate[m] * w
                    new_accs.append(accs[m] + stv * w)
                    one = one + lam * pv[:, DT_RANK + n : DT_RANK + n + 1]
                    pb[here, 128 * n : 128 * n + 128] = tiles(lam * uv)
                    pc[here, 128 * n : 128 * n + 128] = tiles(gv * ah)
                s1[here, :] = one
                s2[here, :] = two
                return tuple(new_lams), tuple(new_accs)

            first = (
                tuple(state[n] for n in range(n0, n0 + NSTEP)),
                tuple(acc_ref[n] for n in range(n0, n0 + NSTEP)),
            )
            lams, accs = lax.fori_loop(0, CHUNK, body, first, unroll=2)
            for m in range(NSTEP):
                state[n0 + m] = lams[m]
                acc_ref[n0 + m] = accs[m]
        gv = g[rows, :]
        one = s1[...]
        grad_values[rows, :] = gv * skip + step[...] * one
        q = (LN2 * s2[...] + values * one) * sigmoid(pre)
        q_low = q.astype(bf16)
        bias_acc[...] += jnp.sum(q.reshape(CHUNK, 8, ch), axis=0)
        skip_acc[...] += jnp.sum((gv * values).reshape(CHUNK, 8, ch), axis=0)
        rank = proj_low[rows, :]
        rows_grad[0:DT_RANK, :] += mm_tn(rank, q_low)[0:DT_RANK, :]
        gu = jnp.sum(gv * u[...], axis=1, keepdims=True)
        lane = lax.broadcasted_iota(jnp.int32, (size, 128), 1)
        inject = jnp.where(lane >= DT_RANK + STATE, pltpu.roll(proj[rows, :], STATE, 1), 0.0)
        part[rows, :] = (
            mm_nt(q_low, wstep)
            + mm(pb[...].astype(bf16), ones[0])
            + mm(pc[...].astype(bf16), ones[1])
            + gu * inject
        )
        return carry

    lax.fori_loop(0, 1, backward, 0)
    mixed_copy.wait_recv()
    for q in range(ZS):
        mixed_low[q] = (mixed_part[q, i].astype(f32) + mixed_core[q].astype(f32)).astype(bf16)
    mixed_zs = [net.copy(mixed_low.at[net.flip(m)], mixed_z.at[m - 1], net.along_z(m)) for m in range(1, ZS)]
    lax.fori_loop(1, 2, backward, 0)
    for c in out_copies:
        c.wait_recv()
    total = out_send[yi].astype(f32)
    for d in range(1, reps):
        total = total + out_y[d - 1].astype(f32)
    total = total.astype(bf16)
    for q in range(TP):
        out_low[q] = total[q * piece : (q + 1) * piece]
    out_zs = []
    for m in range(1, TP):
        zm, im = net.shared(m)
        out_zs.append(net.copy(out_low.at[zm * 2 + im], out_all.at[z * 2 + i], net.to_shared(m)))
    out_all[z * 2 + i] = out_low[z * 2 + i]
    lax.fori_loop(2, rounds, backward, 0)
    g_copy.wait_recv()
    g[span(s, half), :] = g_in[...].astype(f32)
    lax.fori_loop(rounds, 2 * rounds, backward, 0)

    sum_proj = Reduce(net, part, fold, low_out, low_in, grad_proj)
    rows_grad[STEP_ROW : STEP_ROW + 1, :] = jnp.sum(bias_acc[...], axis=0, keepdims=True)
    rows_grad[SKIP_ROW : SKIP_ROW + 1, :] = jnp.sum(skip_acc[...], axis=0, keepdims=True)
    for n in range(STATE):
        rows_grad[DECAY_ROW + n : DECAY_ROW + n + 1, :] = (
            jnp.sum(acc_ref[n], axis=0, keepdims=True) * rate_ref[n : n + 1, :] * LN2
        )
    sum_proj.across_z()
    for c in mixed_zs:
        c.wait_recv()
    total = mixed_part[z, i].astype(f32) + mixed_core[z].astype(f32)
    for m in range(1, ZS):
        total = total + mixed_z[m - 1].astype(f32)
    mixed_sum[...] = (total + tokens[span(gh, HALF), :].astype(f32)).astype(bf16)
    mixed_home = net.copy(mixed_sum, mixed, net.over_x())
    gate_copy.wait_recv()
    own = pl.ds(pl.multiple_of(s * (width // 2), 128), width // 2)
    part_z = mm_tn(gate_both[0], normed[0, :, own]) + mm_tn(gate_both[1], normed[1, :, own])
    for r in range(reps):
        wz_low[r] = part_z[r * cols : (r + 1) * cols].astype(bf16)
    wz_copies = [
        net.copy(wz_low.at[net.y_at(d)], wz_in.at[d - 1], net.along_y(d)) for d in range(1, reps)
    ]
    sum_proj.give()
    for c in out_zs:
        c.wait_recv()
    out_home = net.copy(out_all.at[pl.ds((1 - s) * ZS, ZS)], out_x, net.over_x())
    sum_proj.end()
    total = wz_low[yi].astype(f32)
    for d in range(1, reps):
        wz_copies[d - 1].wait_recv()
        total = total + wz_in[d - 1].astype(f32)
    grad_wz[...] = total
    out_home.wait_recv()
    for q in range(ZS):
        total = out_all[s * ZS + q].astype(f32) + out_x[q].astype(f32)
        for r in range(reps):
            at = ((q // 2) * reps + r) * 2 + q % 2
            grad_wout[:, at * cols : (at + 1) * cols] = total[:, r * cols : (r + 1) * cols]
    mixed_home.wait_recv()
    net.finish()


def core(reps, proj, conv_out, small, ends, tokens, gate_in, wout, cot, normed):
    rows, ch = conv_out.shape
    half = rows // 2
    cols = ch // reps
    width = tokens.shape[1]
    piece = width // (TP * reps)
    V, H = pltpu.VMEM, pl.ANY
    args = [(proj, V), (conv_out, V), (small, V), (ends, V), (tokens, V)]
    args += [(gate_in, H), (wout, H), (cot, H), (normed, H)]
    sds = jax.ShapeDtypeStruct
    outs = (
        (sds((rows, ch), f32), V),
        (sds((rows, 128), bf16), V),
        (sds((2, half, ch), bf16), V),
        (sds((HALF, width), bf16), V),
        (sds((SMALL_ROWS, ch), f32), V),
        (sds((piece, ZS * ch), f32), V),
        (sds((cols, width // 2), f32), V),
    )
    size = CHUNK * 8
    scratch = (
        V((half, ch), f32),
        V((reps, TP, reps, piece, cols), bf16),
        V((width, ch), bf16),
        V((half, width), bf16),
        V((2, half, width), bf16),
        V((2, STATE * 128, 128), bf16),
        V((PACK, STATE, 8, ch), f32),
        V((rows, 128), f32),
        V((size, ch), f32),
        V((size, ch), f32),
        V((size, ch), f32),
        V((STATE, 8, ch), f32),
        V((STATE, 8, ch), f32),
        V((STATE, ch), f32),
        V((half, ch), bf16),
        V((half, ch), bf16),
        V((half, ch), bf16),
        V((ZS, 2, HALF, width), bf16),
        V((ZS, HALF, width), bf16),
        V((ZS, HALF, width), bf16),
        V((ZS - 1, HALF, width), bf16),
        V((HALF, width), bf16),
        V((rows, ch), f32),
        V((half, ch), bf16),
        V((half, ch), bf16),
        V((size, ch), f32),
        V((size, ch), f32),
        V((size, STATE * 128), f32),
        V((size, STATE * 128), f32),
        V((8, ch), f32),
        V((8, ch), f32),
        V((rows, 128), f32),
        V((reps, TP * piece, ch), bf16),
        V((reps - 1, TP * piece, ch), bf16),
        V((TP, piece, ch), bf16),
        V((TP, piece, ch), bf16),
        V((ZS, piece, ch), bf16),
        V((reps, cols, width // 2), bf16),
        V((reps - 1, cols, width // 2), bf16),
    ) + REDUCE_SCRATCH
    copies = 7 + 27 + 3 * (reps - 1)
    return fused(partial(core_kernel, reps), 2, copies, 4, outs, args, scratch)


def back_kernel(
    reps,
    grad_values, grad_proj, conv_pre, small, wstate, ends_in, gate_both, tokens, cot, gain, rows_in,
    conv_in_hbm, conv_out_hbm, wx_hbm, wz_hbm, normed_hbm, tok_hbm,
    grad_tokens, grad_gain, grad_wx, grad_taps, grad_bias, grad_step, grad_skip, grad_decay, grad_wstep, grad_wstate,
    conv_in, conv_out, wx, wz, normed, tok_all, w, slots, sums, gx, gx_in, part, core_in, low, z_in, gain_acc, gain_in,
    wx_low, wx_in, rows_part, rows_recv, state_part, state_in, send, recv, local,
):
    net = Net(reps, send, recv, local)
    s, z, yi, i = net.s, net.z, net.y, net.i
    sgn = 1 - 2 * s
    ch = conv_out.shape[1]
    cols = ch // reps
    width = tokens.shape[1]
    half = TP * HALF
    load_conv_in = net.load(conv_in_hbm, conv_in)
    load_w = [net.load(wx_hbm, wx), net.load(wz_hbm, wz)]
    load_tok = net.load(tok_hbm, tok_all)
    load_rest = [net.load(conv_out_hbm, conv_out), net.load(normed_hbm, normed)]
    net.greet()
    w[0:PAD, :] = jnp.zeros((PAD, ch), f32)
    w[PAD + 8 * PACK :, :] = jnp.zeros((PAD, ch), f32)

    def pull(b, carry):
        rows = span(b, 256)
        c = conv_pre[rows, :]
        sig = sigmoid(c)
        w[pl.ds(pl.multiple_of(PAD + b * 256, 8), 256), :] = (
            grad_values[rows, :] + mm_nt(grad_proj[rows, :], wstate[...])
        ) * (sig * (1.0 + c * (1.0 - sig)))
        return carry

    lax.fori_loop(0, 4, pull, 0)
    sums[...] = jnp.zeros_like(sums)
    ends = (ends_in[0], ends_in[1])
    taps = small[TAP_ROW : TAP_ROW + 16, :].astype(f32)

    def conv_step(t, carry):
        seg = segment_of(t, ends)
        here = w[rows8(t + 3), :]
        total = taps[3:4, :] * here
        sums[3] += here * conv_in[rows8(t + 3), :]
        sums[4] += here
        for k in range(1, TAPS):
            back = t - k * sgn
            ahead = t + k * sgn
            same_back = wide((segment_of(back, ends) == seg).astype(f32), ch)
            same_ahead = wide((segment_of(ahead, ends) == seg).astype(f32), ch)
            sums[3 - k] += here * (conv_in[rows8(back + 3), :] * same_back)
            total = total + taps[3 - k : 4 - k, :] * (w[rows8(ahead + 3), :] * same_ahead)
        slots[rows8(t), :] = total
        return carry

    gx_copies = []
    load_conv_in.wait()
    for h in (1 - s, s):
        lax.fori_loop(h * HALF, (h + 1) * HALF, conv_step, 0)
        x = slots[span(h, half), :]
        gx[h] = jnp.swapaxes(x.reshape(HALF, 8, ch), 0, 1).reshape(half, ch).astype(bf16)
        gx_copies.append(net.copy(gx.at[h], gx_in.at[h], net.over_x()))

    def rows_of(b, carry):
        rows = span(b, 2 * HALF)
        value = (
            mm(gx[s, rows, :], wx[...])
            + mm(gx_in[s, rows, :], wx[...])
            + mm(gate_both[s, rows, :], wz[...])
        )
        part[b] = value.astype(bf16).reshape(2, HALF, width)
        return carry

    for c in load_w:
        c.wait()
    gx_copies[0].wait_recv()
    lax.fori_loop(0, ZS, rows_of, 0)
    to_core = net.copy(part.at[:, 1 - i], core_in, net.sibling())

    gain_acc[0] = jnp.zeros(gain_acc.shape[1:], f32)

    def gain_terms(b, carry):
        rows = pl.ds(pl.multiple_of(b * PACK + s * HALF, HALF), HALF)
        x = tok_all[rows, :].astype(f32)
        inv = lax.rsqrt(jnp.mean(x * x, axis=1, keepdims=True) + EPS)
        terms = part[b // 2, lax.rem(b, 2)].astype(f32) * (x * inv)
        gain_acc[0] += jnp.sum(terms.reshape(HALF // 8, 8, width), axis=0)
        return carry

    to_core.wait_recv()
    for q in range(ZS):
        low[q] = (part[q, i].astype(f32) + core_in[q].astype(f32)).astype(bf16)
    to_z = [net.copy(low.at[net.flip(m)], z_in.at[m - 1], net.along_z(m)) for m in range(1, ZS)]
    load_tok.wait()
    lax.fori_loop(0, TP, gain_terms, 0)
    stages = [
        [net.sibling()],
        [net.over_x()],
        [net.along_y(d) for d in range(1, reps)],
        [net.along_z(1)],
        [net.along_z(2)],
    ]
    slot = [0]

    def gain_start(k):
        cs = []
        for peer in stages[k]:
            cs.append((slot[0], net.copy(gain_acc.at[k], gain_in.at[slot[0]], peer)))
            slot[0] += 1
        return cs

    def gain_end(k, cs):
        total = gain_acc[k]
        for at, c in cs:
            c.wait_recv()
            total = total + gain_in[at]
        gain_acc[k + 1] = total

    cs = gain_start(0)
    for c in load_rest:
        c.wait()
    state_all = mm_tn(conv_out[...].astype(bf16), grad_proj[...])
    for r in range(reps):
        state_part[r] = state_all[r * cols : (r + 1) * cols, :]
        rows_part[r] = rows_in[:, r * cols : (r + 1) * cols]
        for n in range(TAPS + 1):
            row = jnp.sum(sums[n], axis=0, keepdims=True)
            rows_part[r, TAP_ROW + n : TAP_ROW + n + 1, :] = row[:, r * cols : (r + 1) * cols]
    state_copies = [
        net.copy(state_part.at[net.y_at(d)], state_in.at[d - 1], net.along_y(d)) for d in range(1, reps)
    ]
    rows_copies = [
        net.copy(rows_part.at[net.y_at(d)], rows_recv.at[d - 1], net.along_y(d)) for d in range(1, reps)
    ]
    gain_end(0, cs)
    cs = gain_start(1)
    own = pl.ds(pl.multiple_of(s * (width // 2), 128), width // 2)
    gx_copies[1].wait_recv()
    part_x = mm_tn(gx[0], normed[0, :, own]) + mm_tn(gx[1], normed[1, :, own])
    part_x = part_x + mm_tn(gx_in[0], normed[0, :, own]) + mm_tn(gx_in[1], normed[1, :, own])
    for r in range(reps):
        wx_low[r] = part_x[r * cols : (r + 1) * cols].astype(bf16)
    wx_copies = [
        net.copy(wx_low.at[net.y_at(d)], wx_in.at[d - 1], net.along_y(d)) for d in range(1, reps)
    ]
    gain_end(1, cs)
    cs = gain_start(2)
    gain_end(2, cs)
    cs = gain_start(3)
    x = tokens[span(s, HALF), :].astype(f32)
    inv = lax.rsqrt(jnp.mean(x * x, axis=1, keepdims=True) + EPS)
    unit = x * inv
    gain_end(3, cs)
    cs = gain_start(4)
    grad = part[z, i].astype(f32) + core_in[z].astype(f32)
    for m in range(1, ZS):
        to_z[m - 1].wait_recv()
        grad = grad + z_in[m - 1].astype(f32)
    scaled = grad * gain[...]
    mean = jnp.mean(scaled * unit, axis=1, keepdims=True)
    grad_tokens[...] = inv * (scaled - unit * mean) + cot[...].astype(f32)
    gain_end(4, cs)
    grad_gain[...] = jnp.sum(gain_acc[5], axis=0, keepdims=True)
    total = rows_part[yi]
    for d in range(1, reps):
        rows_copies[d - 1].wait_recv()
        total = total + rows_recv[d - 1]
    grad_wstep[...] = total[0:DT_RANK]
    grad_taps[...] = total[TAP_ROW : TAP_ROW + TAPS]
    grad_bias[...] = total[BIAS_ROW : BIAS_ROW + 1]
    grad_step[...] = total[STEP_ROW : STEP_ROW + 1]
    grad_skip[...] = total[SKIP_ROW : SKIP_ROW + 1]
    grad_decay[...] = total[DECAY_ROW : DECAY_ROW + STATE]
    total = state_part[yi]
    for d in range(1, reps):
        state_copies[d - 1].wait_recv()
        total = total + state_in[d - 1]
    grad_wstate[...] = total
    total = wx_low[yi].astype(f32)
    for d in range(1, reps):
        wx_copies[d - 1].wait_recv()
        total = total + wx_in[d - 1].astype(f32)
    grad_wx[...] = total
    net.finish()


def backward(
    reps, grad_values, grad_proj, conv_pre, small, wstate, ends, gate_both, tokens, cot, gain, rows_in,
    conv_in, conv_out, wx, wz, normed, tok_all,
):
    rows, ch = conv_out.shape
    half = rows // 2
    cols = ch // reps
    width = tokens.shape[1]
    V, H = pltpu.VMEM, pl.ANY
    near = (grad_values, grad_proj, conv_pre, small, wstate, ends, gate_both, tokens, cot, gain, rows_in)
    far = (conv_in, conv_out, wx, wz, normed, tok_all)
    args = [(a, V) for a in near] + [(a, H) for a in far]
    sds = jax.ShapeDtypeStruct
    outs = (
        sds((HALF, width), f32),
        sds((1, width), f32),
        sds((cols, width // 2), f32),
        sds((TAPS, cols), f32),
        sds((1, cols), f32),
        sds((1, cols), f32),
        sds((1, cols), f32),
        sds((STATE, cols), f32),
        sds((DT_RANK, cols), f32),
        sds((cols, 128), f32),
    )
    scratch = tuple(V(a.shape, a.dtype) for a in far) + (
        V((rows + 2 * PAD, ch), f32),
        V((rows, ch), f32),
        V((TAPS + 1, 8, ch), f32),
        V((2, half, ch), bf16),
        V((2, half, ch), bf16),
        V((ZS, 2, HALF, width), bf16),
        V((ZS, HALF, width), bf16),
        V((ZS, HALF, width), bf16),
        V((ZS - 1, HALF, width), bf16),
        V((6, 8, width), f32),
        V((3 + reps, 8, width), f32),
        V((reps, cols, width // 2), bf16),
        V((reps - 1, cols, width // 2), bf16),
        V((reps, SMALL_ROWS, cols), f32),
        V((reps - 1, SMALL_ROWS, cols), f32),
        V((reps, cols, 128), f32),
        V((reps - 1, cols, 128), f32),
    )
    copies = 2 + 1 + 3 + 4 + 4 * (reps - 1)
    return fused(partial(back_kernel, reps), 3, copies, 6, [(o, V) for o in outs], args, scratch)


def place_kernel(index, gain, *refs):
    count = (len(refs) - 1) // 2
    for source, target in zip(refs[:count], refs[count : 2 * count]):
        target[...] = source[...]
    gain_out = refs[-1]
    width, n = gain.shape[1], gain_out.shape[1]
    moved = pltpu.roll(jnp.broadcast_to(gain[...], (8, width)), width - index[0] * n, 1)
    gain_out[...] = moved[0:1, 0:n]


def place(index, gain, n, *results):
    V = pl.BlockSpec(memory_space=pltpu.VMEM)
    return pl.pallas_call(
        place_kernel,
        out_shape=tuple(jax.ShapeDtypeStruct(r.shape, r.dtype) for r in results)
        + (jax.ShapeDtypeStruct((1, n), f32),),
        in_specs=[pl.BlockSpec(memory_space=pltpu.SMEM), V] + [V] * len(results),
        out_specs=tuple([V] * (len(results) + 1)),
    )(index, gain, *results)

def local(
    reps, tokens, item_grids, norm_gain, proj_in_x, proj_in_z, proj_out, conv_weight, conv_bias,
    proj_state, proj_step, step_bias, decay_log, skip_gain, grad_out,
):
    width = tokens.shape[1]
    cot = grad_out.reshape(HALF, width)
    (
        normed, conv_in, conv_pre, conv_out, gate_in, tok_all, wx, wz, wout, cot_other,
        proj, gain, ends, small, wstate,
    ) = front(
        reps, item_grids, tokens, norm_gain[None], proj_in_x.T, proj_in_z.T, proj_step[0], conv_weight[0],
        conv_bias, step_bias, skip_gain, decay_log[0], proj_state[0], proj_out.T, cot,
    )
    grad_values, grad_proj, gate_both, mixed, rows_grad, grad_wout, grad_wz = core(
        reps, proj, conv_out, small, ends, tokens, gate_in, wout, cot_other, normed
    )
    (
        grad_tokens, grad_gain, grad_wx, grad_taps, grad_bias, grad_step, grad_skip, grad_decay,
        grad_wstep, grad_wstate,
    ) = backward(
        reps, grad_values, grad_proj, conv_pre, small, wstate, ends, gate_both, tokens, cot, gain, rows_grad,
        conv_in, conv_out, wx, wz, normed, tok_all,
    )
    index = (lax.axis_index("dir") * lax.axis_size("dp") + lax.axis_index("dp")).astype(jnp.int32)
    (
        mixed, grad_tokens, grad_wx, grad_wz, grad_wout, grad_taps, grad_bias, grad_wstate, grad_wstep,
        grad_step, grad_decay, grad_skip, grad_gain,
    ) = place(
        index.reshape(1), grad_gain, width // (2 * TP * reps),
        mixed, grad_tokens, grad_wx, grad_wz, grad_wout, grad_taps, grad_bias, grad_wstate, grad_wstep,
        grad_step, grad_decay, grad_skip,
    )
    return (
        mixed.reshape(1, 1, HALF, width),
        grad_tokens.reshape(1, 1, HALF, width),
        grad_gain[0],
        grad_wx.T,
        grad_wz.T,
        grad_wout.T,
        grad_taps[None],
        grad_bias,
        grad_wstate[None],
        grad_wstep[None],
        grad_step,
        grad_decay[None],
        grad_skip,
    )


def solution(mesh):
    reps = mesh.shape["dp"] // TP
    return jax.shard_map(
        partial(local, reps),
        mesh=mesh,
        in_specs=(
            P("dp", None),
            P("dp", None),
            P("dp"),
            P(None, "dp"),
            P(None, "dp"),
            P(None, "dp"),
            P("dir", None, "dp"),
            P("dir", "dp"),
            P("dir", "dp", None),
            P("dir", None, "dp"),
            P("dir", "dp"),
            P("dir", None, "dp"),
            P("dir", "dp"),
            P("dp", "dir", None, None),
        ),
        out_specs=(
            P("dp", "dir", None, None),
            P("dp", "dir", None, None),
            P(("dir", "dp")),
            P("dir", "dp"),
            P("dir", "dp"),
            P("dir", "dp"),
            P("dir", None, "dp"),
            P("dir", "dp"),
            P("dir", "dp", None),
            P("dir", None, "dp"),
            P("dir", "dp"),
            P("dir", None, "dp"),
            P("dir", "dp"),
        ),
        check_vma=False,
    )
```

time: 3720 us -> 209 us (0.06)
  local copies, waits for them, and re-layouts: 1730 us -> 0 us
  other arithmetic: 872 us -> 0 us
  waiting for transfers between devices: 708 us -> 0 us
  blocking collectives: 260 us -> 0 us
  Pallas kernels: 0 us -> 208 us
  matrix products: 64.6 us -> 0 us
    pad x248 -> x0, local copies, waits for them, and re-layouts: 1410 us -> none  [scan_block(): total_a, total_b = lax.associative_scan(combine, (factor, inject), axis=0)]
    reduce_scatter x6 -> x0, waiting for transfers between devices: 431 us -> none  [the longest x1 116 us: local(): lax.psum_scatter(part_out, 'dp', scatter_dimension=1, tiled=True)]
    mul x109 -> x0, other arithmetic: 309 us -> none  [the longest x80 270 us: combine(): return (earlier[0] * latter[0], latter[0] * earlier[1] + latter[1])]
    unnamed x22 -> x0, waiting for transfers between devices: 277 us -> none
    pallas_call x0 -> x4, Pallas kernels: none -> 208 us  [the longest x3 204 us: fused(): pl.pallas_call(kernel, out_shape=tuple((o for o, _ in outs)), in_specs=[p...]
    reduce_sum x20 -> x0, other arithmetic: 159 us -> none  [the longest x8 83.4 us: scan_block(): readout = jnp.sum(hidden * state_io[:, states:, None], axis=1)]
    all_gather x8 -> x0, blocking collectives: 155 us -> none  [the longest x1 33.7 us: local(): lax.all_gather(decay_log, 'dp', axis=2, tiled=True)]
    add x84 -> x0, other arithmetic: 153 us -> none  [the longest x64 142 us: scan_block(): total_a, total_b = lax.associative_scan(combine, (factor, inject), axis=0)]
  transfers between devices with their start and end apart: 16 -> 0, of which waited for: 12 -> 0; matrix products, arithmetic and copies ran while one was open for 5% -> 0% of each run, Pallas kernels for 0% -> 0%
where the time goes in v2:
time: 209 us; the launch traced here: 208 us
  Pallas kernels  208 us (100%)
    pallas_call x3, Pallas kernels, fused(): pl.pallas_call(kernel, out_shape=tuple((o for o, _ in outs)), in_specs=[p...  204 us

profile of v2, /device:TPU:0, one launch (start us, length us, event | category | flops | bytes accessed | tf_op | source)
XLA Modules:
  0.0 208.4 jit_solution(13663440278379857363)
XLA Ops:
  0.6 62.2 %shard_map.237 = (bf16[2,512,1536]{2,1,0:T(8,128)(2,1)}, f32[1072,384]{1,0:T(8,128)}, f32[1024,384]{1,0:T(8,128)}, f32[1024,384]{1,0:T(8,128)}, f32[512,384]{1,0...) custom-call(s32[2,2]{1,0:T(2,128)} %grids.1, ...), custom_call_target="tpu_custom_call" | custom-call | tf_op jit(solution)/shard_map/pallas_call | solution.py:207
  62.9 94.5 %shard_map.238 = (f32[1024,384]{1,0:T(8,128)}, bf16[1024,128]{1,0:T(8,128)(2,1)}, bf16[2,512,384]{2,1,0:T(8,128)(2,1)}, bf16[64,1536]{1,0:T(8,128)(2,1)}, f32[12...) custom-call(bf16[1024,128]{1,0:T(8,128)(2,1)} %get-tuple-element.58.proj_low, ...), custom_call_target="tpu_custom_call" | custom-call | tf_op jit(solution)/shard_map/pallas_call | solution.py:207
  157.4 47.6 %shard_map.239 = (f32[64,1536]{1,0:T(8,128)}, f32[1,1536]{1,0:T(1,128)}, f32[192,768]{1,0:T(8,128)}, f32[4,192]{1,0:T(4,128)}, f32[1,192]{1,0:T(1,128)}, /*index...) custom-call(f32[1024,384]{1,0:T(8,128)} %get-tuple-element.66.grad_values, ...), custom_call_target="tpu_custom_call" | custom-call | tf_op jit(solution)/shard_map/pallas_call | solution.py:207
  205.0 3.2 %shard_map.240 = (bf16[64,1536]{1,0:T(8,128)(2,1)}, f32[64,1536]{1,0:T(8,128)}, f32[192,768]{1,0:T(8,128)}, f32[192,768]{1,0:T(8,128)}, f32[96,1536]{1,0:T(8,128...) custom-call(s32[1]{0:T(128)} %bitcast.index, ...), custom_call_target="tpu_custom_call" | custom-call | tf_op jit(solution)/shard_map/pallas_call | solution.py:1016

commit v3 on v2

--- a/solution.py
+++ b/solution.py
@@ -430,7 +430,7 @@
     proj_low, conv_out, small, ends_in, tokens, gate_hbm, wout_hbm, cot_hbm, normed_hbm,
     grad_values, grad_proj, gate_both, mixed, rows_grad, grad_wout, grad_wz,
     gate_in, wout_all, wout, cot, normed, ones, hprev, proj, step, decay_step, u, state, acc_ref, rate_ref, y_send, y_in,
-    gated, mixed_part, mixed_core, mixed_low, mixed_z, mixed_sum, g, g_send, g_in,
+    gated, mixed_part, mixed_core, mixed_low, mixed_z, mixed_sum, g_send, g_in,
     s1, s2, pb, pc, bias_acc, skip_acc, part,
     out_send, out_y, out_low, out_all, out_x, wz_low, wz_in,
     fold, low_out, low_in, send, recv, local,
@@ -446,10 +446,11 @@
     size = CHUNK * 8
     piece = out_all.shape[1]
     width = tokens.shape[1]
-    y = grad_values
+    y = g = grad_values
+    own = pl.ds(pl.multiple_of(s * (width // 2), 128), width // 2)
     loads = [
         net.load(gate_hbm, gate_in),
-        net.load(normed_hbm, normed),
+        net.load(normed_hbm.at[:, :, own], normed),
         net.load(wout_hbm, wout_all.at[yi]),
         net.load(cot_hbm, cot.at[span(z * 2 + i, HALF)]),
     ]
@@ -515,7 +516,7 @@
                 y[rows8(t), :] = total
                 return tuple(new)
 
-            hs = lax.fori_loop(0, CHUNK, body, tuple(state[n] for n in range(n0, n0 + NSTEP)), unroll=2)
+            hs = lax.fori_loop(0, CHUNK, body, tuple(state[n] for n in range(n0, n0 + NSTEP)), unroll=CHUNK)
             for m in range(NSTEP):
                 state[n0 + m] = hs[m]
         return carry
@@ -613,7 +614,7 @@
                 tuple(state[n] for n in range(n0, n0 + NSTEP)),
                 tuple(acc_ref[n] for n in range(n0, n0 + NSTEP)),
             )
-            lams, accs = lax.fori_loop(0, CHUNK, body, first, unroll=2)
+            lams, accs = lax.fori_loop(0, CHUNK, body, first, unroll=CHUNK)
             for m in range(NSTEP):
                 state[n0 + m] = lams[m]
                 acc_ref[n0 + m] = accs[m]
@@ -677,8 +678,7 @@
     mixed_sum[...] = (total + tokens[span(gh, HALF), :].astype(f32)).astype(bf16)
     mixed_home = net.copy(mixed_sum, mixed, net.over_x())
     gate_copy.wait_recv()
-    own = pl.ds(pl.multiple_of(s * (width // 2), 128), width // 2)
-    part_z = mm_tn(gate_both[0], normed[0, :, own]) + mm_tn(gate_both[1], normed[1, :, own])
+    part_z = mm_tn(gate_both[0], normed[0]) + mm_tn(gate_both[1], normed[1])
     for r in range(reps):
         wz_low[r] = part_z[r * cols : (r + 1) * cols].astype(bf16)
     wz_copies = [
@@ -729,7 +729,7 @@
         V((reps, TP, reps, piece, cols), bf16),
         V((width, ch), bf16),
         V((half, width), bf16),
-        V((2, half, width), bf16),
+        V((2, half, width // 2), bf16),
         V((2, STATE * 128, 128), bf16),
         V((PACK, STATE, 8, ch), f32),
         V((rows, 128), f32),
@@ -747,7 +747,6 @@
         V((ZS, HALF, width), bf16),
         V((ZS - 1, HALF, width), bf16),
         V((HALF, width), bf16),
-        V((rows, ch), f32),
         V((half, ch), bf16),
         V((half, ch), bf16),
         V((size, ch), f32),

time: 209 us -> 191 us (0.914)
  Pallas kernels: 208 us -> 189 us
    pallas_call x3, Pallas kernels: 204 us -> 186 us  [fused(): pl.pallas_call(kernel, out_shape=tuple((o for o, _ in outs)), in_specs=[p...]
where the time goes in v3:
time: 191 us; the launch traced here: 190 us
  Pallas kernels  189 us (99%)
    pallas_call x3, Pallas kernels, fused(): pl.pallas_call(kernel, out_shape=tuple((o for o, _ in outs)), in_specs=[p...  186 us

profile of v3, /device:TPU:0, one launch (start us, length us, event | category | flops | bytes accessed | tf_op | source)
XLA Modules:
  0.0 190.3 jit_solution(8828327226456248916)
XLA Ops:
  0.6 62.2 %shard_map.237 = (bf16[2,512,1536]{2,1,0:T(8,128)(2,1)}, f32[1072,384]{1,0:T(8,128)}, f32[1024,384]{1,0:T(8,128)}, f32[1024,384]{1,0:T(8,128)}, f32[512,384]{1,0...) custom-call(s32[2,2]{1,0:T(2,128)} %grids.1, ...), custom_call_target="tpu_custom_call" | custom-call | tf_op jit(solution)/shard_map/pallas_call | solution.py:207
  62.9 75.6 %shard_map.238 = (f32[1024,384]{1,0:T(8,128)}, bf16[1024,128]{1,0:T(8,128)(2,1)}, bf16[2,512,384]{2,1,0:T(8,128)(2,1)}, bf16[64,1536]{1,0:T(8,128)(2,1)}, f32[12...) custom-call(bf16[1024,128]{1,0:T(8,128)(2,1)} %get-tuple-element.58.proj_low, ...), custom_call_target="tpu_custom_call" | custom-call | tf_op jit(solution)/shard_map/pallas_call | solution.py:207
  138.5 48.4 %shard_map.239 = (f32[64,1536]{1,0:T(8,128)}, f32[1,1536]{1,0:T(1,128)}, f32[192,768]{1,0:T(8,128)}, f32[4,192]{1,0:T(4,128)}, f32[1,192]{1,0:T(1,128)}, /*index...) custom-call(f32[1024,384]{1,0:T(8,128)} %get-tuple-element.66.grad_values, ...), custom_call_target="tpu_custom_call" | custom-call | tf_op jit(solution)/shard_map/pallas_call | solution.py:207
  186.9 3.2 %shard_map.240 = (bf16[64,1536]{1,0:T(8,128)(2,1)}, f32[64,1536]{1,0:T(8,128)}, f32[192,768]{1,0:T(8,128)}, f32[192,768]{1,0:T(8,128)}, f32[96,1536]{1,0:T(8,128...) custom-call(s32[1]{0:T(128)} %bitcast.index, ...), custom_call_target="tpu_custom_call" | custom-call | tf_op jit(solution)/shard_map/pallas_call | solution.py:1015

commit v4 on v3

v4 whole, which is shorter than its diff:
```python
from functools import partial

import jax
import jax.numpy as jnp
from jax import lax
from jax.experimental import pallas as pl
from jax.experimental.pallas import tpu as pltpu
from jax.sharding import PartitionSpec as P

f32 = jnp.float32
bf16 = jnp.bfloat16
EPS = 1e-05
DT_RANK = 96
STATE = 16
TAPS = 4
ZS = 4
TP = 8
PACK = 128
HALF = 64
CHUNK = 16
NSTEP = 4
LOG2E = 1.4426950408889634
LN2 = 0.6931471805599453
BIG = 1e9
PAD = 24
TAP_ROW, BIAS_ROW, STEP_ROW, SKIP_ROW, DECAY_ROW, SMALL_ROWS = 96, 100, 101, 102, 103, 128


def mm(left, right):
    return jnp.dot(left, right, preferred_element_type=f32)


def mm_nt(left, right):
    return lax.dot_general(left, right, (((1,), (1,)), ((), ())), preferred_element_type=f32)


def mm_tn(left, right):
    return lax.dot_general(left, right, (((0,), (0,)), ((), ())), preferred_element_type=f32)


def segment_of(t, ends):
    t = t.astype(f32) if hasattr(t, "astype") else float(t)
    return (t >= ends[0]).astype(f32) + (t >= ends[1]).astype(f32)


def rows8(t):
    return pl.ds(pl.multiple_of(t * 8, 8), 8)


def span(start, size):
    return pl.ds(pl.multiple_of(start * size, size), size)


def sigmoid(v):
    return 1.0 / (1.0 + jnp.exp(-v))


def softplus(v):
    return jnp.maximum(v, 0.0) + jnp.log1p(jnp.exp(-jnp.abs(v)))


def wide(mask, ch):
    return jnp.concatenate([mask] * (ch // 128), axis=1)


def tiles(v):
    total = v[:, 0:128]
    for at in range(128, v.shape[1], 128):
        total = total + v[:, at : at + 128]
    return total


class Copy:
    def __init__(self, copy):
        self.copy, self.sent, self.got = copy, False, False
        copy.start()

    def wait_send(self):
        if not self.sent:
            self.copy.wait_send()
            self.sent = True

    def wait_recv(self):
        if not self.got:
            self.copy.wait_recv()
            self.got = True


class Net:
    def __init__(self, reps, send, recv, local):
        self.reps, self.send, self.recv, self.local = reps, send, recv, local
        self.s = lax.axis_index("dir")
        p = lax.axis_index("dp")
        self.i = lax.rem(p, 2)
        self.y = lax.rem(p // 2, reps)
        self.z = p // (2 * reps)
        self.used = 0
        self.moved = 0
        self.copies = []
        self.saves = []

    def place(self, s, z, y, i):
        return (s, (z * self.reps + y) * 2 + i)

    def flip(self, m):
        if m == 1:
            return self.z + 1 - 2 * lax.rem(self.z, 2)
        if m == 2:
            return lax.rem(self.z + 2, ZS)
        return ZS - 1 - self.z

    def over_x(self):
        return self.place(1 - self.s, self.z, self.y, self.i)

    def sibling(self):
        return self.place(self.s, self.z, self.y, 1 - self.i)

    def along_z(self, m):
        return self.place(self.s, self.flip(m), self.y, self.i)

    def shared(self, m):
        z = self.flip(m // 2) if m // 2 else self.z
        i = 1 - self.i if m % 2 else self.i
        return z, i

    def to_shared(self, m):
        z, i = self.shared(m)
        return self.place(self.s, z, self.y, i)

    def y_at(self, d):
        return lax.rem(self.y + d, self.reps)

    def along_y(self, d):
        return self.place(self.s, self.z, self.y_at(d), self.i)

    def greet(self):
        self.peers = [self.over_x()] + [self.to_shared(m) for m in range(1, TP)]
        self.peers += [self.along_y(d) for d in range(1, self.reps)]
        barrier = pltpu.get_barrier_semaphore()
        for peer in self.peers:
            pl.semaphore_signal(barrier, inc=1, device_id=peer, device_id_type=pl.DeviceIdType.MESH)

    def met(self):
        pl.semaphore_wait(pltpu.get_barrier_semaphore(), len(self.peers))

    def copy(self, source, target, peer):
        k = self.used
        self.used += 1
        c = Copy(
            pltpu.make_async_remote_copy(
                src_ref=source,
                dst_ref=target,
                send_sem=self.send.at[k],
                recv_sem=self.recv.at[k],
                device_id=peer,
                device_id_type=pl.DeviceIdType.MESH,
            )
        )
        self.copies.append(c)
        return c

    def load(self, source, target):
        c = pltpu.make_async_copy(source, target, self.local.at[self.moved])
        self.moved += 1
        c.start()
        return c

    def save(self, source, target):
        self.saves.append(self.load(source, target))

    def finish(self):
        for c in self.copies:
            c.wait_recv()
            c.wait_send()
        for c in self.saves:
            c.wait()


class Reduce:
    def __init__(self, net, part, base, size, fold, out_low, in_low, total):
        self.net, self.part, self.base = net, part, base
        self.fold, self.out_low, self.in_low, self.total = fold, out_low, in_low, total
        self.rows = size // 2
        self.block = self.rows // ZS
        self.first = net.copy(part.at[self.at(1 - net.i, self.rows)], fold, net.sibling())

    def at(self, n, size):
        return pl.ds(pl.multiple_of(self.base + n * size, size), size)

    def across_z(self):
        net, fold = self.net, self.fold
        self.first.wait_recv()
        fold[...] = self.part[self.at(net.i, self.rows), :] + fold[...]
        self.out_low[...] = fold[...].astype(bf16).reshape(ZS, self.block, 128)
        self.cs = [
            net.copy(self.out_low.at[net.flip(m)], self.in_low.at[m - 1], net.along_z(m))
            for m in range(1, ZS)
        ]

    def give(self):
        net, total = self.net, self.total
        mine = self.at(net.i * ZS + net.z, self.block)
        value = self.fold[span(net.z, self.block), :]
        for m in range(1, ZS):
            self.cs[m - 1].wait_recv()
            value = value + self.in_low[m - 1].astype(f32)
        total[mine, :] = value.astype(bf16)
        self.cs = [net.copy(total.at[mine], total.at[mine], net.along_z(m)) for m in range(1, ZS)]
        self.ds = [net.copy(total.at[mine], total.at[mine], net.sibling())]

    def end(self):
        net, total = self.net, self.total
        for m in range(1, ZS):
            self.cs[m - 1].wait_recv()
            there = self.at(net.i * ZS + net.flip(m), self.block)
            self.ds.append(net.copy(total.at[there], total.at[there], net.sibling()))
        for d in self.ds:
            d.wait_recv()


REDUCE_ROWS = TP * HALF
REDUCE_SCRATCH = (
    pltpu.VMEM((REDUCE_ROWS // 2, 128), f32),
    pltpu.VMEM((ZS, REDUCE_ROWS // 2 // ZS, 128), bf16),
    pltpu.VMEM((ZS - 1, REDUCE_ROWS // 2 // ZS, 128), bf16),
)


def fused(kernel, name_id, copies, moves, outs, args, scratch):
    return pl.pallas_call(
        kernel,
        out_shape=tuple(o for o, _ in outs),
        in_specs=[pl.BlockSpec(memory_space=m) for _, m in args],
        out_specs=tuple(pl.BlockSpec(memory_space=m) for _, m in outs),
        scratch_shapes=list(scratch)
        + [pltpu.SemaphoreType.DMA((n,)) for n in (copies, copies, moves)],
        compiler_params=pltpu.CompilerParams(
            collective_id=name_id, has_side_effects=True, vmem_limit_bytes=63 << 20
        ),
    )(*(a for a, _ in args))


def block_kernel(reps, *refs):
    refs = list(refs)

    def take_refs(n):
        out = refs[:n]
        del refs[:n]
        return out

    (
        grids, gain_own, wstep_own, taps_own, bias_own, step_own, skip_own, decay_own, wstate_own, wout_own,
        cot_own, tokens, wx_own, wz_own,
    ) = take_refs(14)
    (
        mixed, grad_tokens, wx_mine, wx_theirs, wz_mine, wz_theirs, out_mine, out_theirs, rows_mine,
        rows_theirs, state_mine, state_theirs, grad_gain,
    ) = take_refs(13)
    (
        meta_all, gain, ends_ref, wx_all, wx, wz_all, wz, small_all, small, wstate_all, wstate,
        wout_send, wout_in, wout_all, wout,
    ) = take_refs(15)
    (tok, normed, raw, conv_in, conv_pre, conv_out, gate_in, part, proj_low, proj) = take_refs(10)
    (
        hprev, step, decay_step, u, state, acc_ref, rate_ref, s1, s2, pb, pc, ones, bias_acc, skip_acc, g,
    ) = take_refs(15)
    (y_send, y_in, g_send, g_in, gated, gate_both, cot, mixed_core, mixed_low, mixed_z, mixed_sum, tok_last) = take_refs(12)
    (out_send, out_y, out_low, out_x_in, out_all, wz_low, part_back, grad_proj, sums, gx, gx_in) = take_refs(11)
    (wx_low, rows_grad, rows_part, state_part, gain_acc, gain_in) = take_refs(6)
    reduces = [take_refs(3) for _ in range(4)]
    send, recv, local_sems = refs
    net = Net(reps, send, recv, local_sems)
    net.greet()
    s, z, yi, i = net.s, net.z, net.y, net.i
    sgn = 1 - 2 * s
    gh = 1 - s
    j = z * 2 + i
    cols, width = wx_own.shape
    ch = reps * cols
    piece = wout_own.shape[0]
    half = TP * HALF
    rounds = HALF // CHUNK
    size = CHUNK * 8
    share = piece % 32 == 0
    hp = piece // 2 if share else piece
    own_part = pl.ds(pl.multiple_of(s * hp, hp), hp) if share else pl.ds(0, piece)
    half_cols = pl.ds(pl.multiple_of(s * (width // 2), 128), width // 2)

    own_loads = [net.load(tokens.at[pl.ds(h * HALF, HALF)], tok.at[h, z, i]) for h in range(2)]
    own_loads += [net.load(wx_own, wx_all.at[yi]), net.load(wz_own, wz_all.at[yi])]
    own_loads += [net.load(tokens.at[pl.ds(pl.multiple_of(gh * HALF, HALF), HALF)], tok_last)]
    first_end = (grids[0, 0] * grids[0, 1]).astype(f32)
    second_end = first_end + (grids[1, 0] * grids[1, 1]).astype(f32)
    row = lax.broadcasted_iota(jnp.int32, (16, 128), 0)
    gain_row = jnp.concatenate([gain_own[...].astype(f32), jnp.zeros((1, 128 - piece), f32)], axis=1)
    meta = jnp.where(row == 0, gain_row, jnp.where(row == 1, first_end, second_end))
    meta_all[yi, j] = meta.astype(bf16)
    small_rows = [ref[...].astype(f32) for ref in (wstep_own, taps_own, bias_own, step_own, skip_own, decay_own)]
    small_rows.append(jnp.zeros((SMALL_ROWS - DECAY_ROW - STATE, cols), f32))
    small_all[yi] = jnp.concatenate(small_rows, axis=0).astype(bf16)
    wstate_all[yi] = wstate_own[...]
    net.met()
    own_first = tokens.at[pl.ds(pl.multiple_of(s * HALF, HALF), HALF)]
    own_last = tokens.at[pl.ds(pl.multiple_of(gh * HALF, HALF), HALF)]
    from_z = [net.copy(own_first, tok.at[s, z, i], net.along_z(m)) for m in range(1, ZS)]
    core_first = [net.copy(own_first, tok.at[s, z, i], net.sibling())]
    core_last = [net.copy(own_last, tok.at[gh, z, i], net.sibling())]
    metas = [net.copy(meta_all.at[yi, j], meta_all.at[yi, j], net.to_shared(m)) for m in range(1, TP)]
    first_y = []
    for d in range(1, reps):
        first_y.append(net.copy(wx_own, wx_all.at[yi], net.along_y(d)))
        for ref in (small_all, wstate_all):
            first_y.append(net.copy(ref.at[yi], ref.at[yi], net.along_y(d)))
    cot_mine = span(j, HALF)
    cot_x = net.copy(cot_own, cot.at[cot_mine], net.over_x())
    for c in metas:
        c.wait_recv()
    meta_y = [net.copy(meta_all.at[yi], meta_all.at[yi], net.along_y(d)) for d in range(1, reps)]
    late_y = [net.copy(wz_own, wz_all.at[yi], net.along_y(d)) for d in range(1, reps)]

    for ref in (conv_in, conv_pre):
        ref[0:PAD, :] = jnp.zeros((PAD, ch), f32)
        ref[PAD + 8 * PACK :, :] = jnp.zeros((PAD, ch), f32)
    for b in range(TP):
        both = meta_all[yi, b].astype(f32)
        ends_ref[0, b : b + 1, :] = both[1:2, :]
        ends_ref[1, b : b + 1, :] = both[2:3, :]
    for p in range(TP * reps):
        zp, yp, ip = p // (2 * reps), (p // 2) % reps, p % 2
        wout_send[zp * 2 + ip, :, yp * cols : (yp + 1) * cols] = wout_own[:, p * cols : (p + 1) * cols]
    wout_in[j, own_part] = wout_send[j, own_part]
    source = lax.broadcasted_iota(jnp.int32, (STATE * 128, 128), 0) // 128
    target = lax.broadcasted_iota(jnp.int32, (STATE * 128, 128), 1)
    ones[...] = (target == DT_RANK + source).astype(f32).astype(bf16)
    rows_grad[...] = jnp.zeros_like(rows_grad)
    state[...] = jnp.zeros_like(state)
    for c in own_loads:
        c.wait()

    from_x = []
    for m in range(1, ZS):
        from_z[m - 1].wait_recv()
        there = tok.at[s, net.flip(m), i]
        core_first.append(net.copy(there, there, net.sibling()))
        from_x.append(net.copy(there, there, net.over_x()))
    wout_z = []
    for m in range(1, TP):
        zm, im = net.shared(m)
        wout_z.append(net.copy(wout_send.at[zm * 2 + im, own_part], wout_in.at[j, own_part], net.to_shared(m)))
    cot_x.wait_recv()
    cot_z = [net.copy(cot.at[cot_mine], cot.at[cot_mine], net.along_z(m)) for m in range(1, ZS)]
    cot_core = [net.copy(cot.at[cot_mine], cot.at[cot_mine], net.sibling())]
    for c in meta_y + first_y:
        c.wait_recv()
    for p in range(TP * reps):
        zp, yp, ip = p // (2 * reps), (p // 2) % reps, p % 2
        gain[:, p * piece : (p + 1) * piece] = meta_all[yp, zp * 2 + ip].astype(f32)[0:1, 0:piece]
    for r in range(reps):
        wx[r * cols : (r + 1) * cols, :] = wx_all[r]
        small[:, r * cols : (r + 1) * cols] = small_all[r]
        wstate[r * cols : (r + 1) * cols, :] = wstate_all[r]
    for c in core_first:
        c.wait_recv()

    ends = (ends_ref[0], ends_ref[1])
    vectors = small[DT_RANK : DT_RANK + 16, :].astype(f32)
    taps = vectors[0 : TAPS + 1, :]
    step_bias = vectors[STEP_ROW - DT_RANK : STEP_ROW - DT_RANK + 1, :]
    skip = vectors[SKIP_ROW - DT_RANK : SKIP_ROW - DT_RANK + 1, :]

    def take(h):
        def one(q, carry):
            rows = span(q, PACK)
            x = tok[h, q].astype(f32).reshape(PACK, width)
            inv = lax.rsqrt(jnp.mean(x * x, axis=1, keepdims=True) + EPS)
            low = (x * inv * gain[...]).astype(bf16)
            normed[h, rows, :] = low
            raw[rows, :] = mm_nt(low, wx[...])
            return carry

        lax.fori_loop(0, ZS, one, 0)
        x = jnp.swapaxes(raw[...].reshape(8, HALF, ch), 0, 1).reshape(half, ch)
        conv_in[pl.ds(pl.multiple_of(PAD + h * half, 8), half), :] = x

    def convolve(h, sums):
        def one(k, carry):
            t = h * HALF + k
            seg = segment_of(t, ends)
            total = taps[4:5, :] + taps[3:4, :] * conv_in[rows8(t + 3), :]
            for n in range(1, TAPS):
                there = t - n * sgn
                same = wide((segment_of(there, ends) == seg).astype(f32), ch)
                total = total + taps[3 - n : 4 - n, :] * (conv_in[rows8(there + 3), :] * same)
            conv_pre[rows8(t + 3), :] = total
            act = total * sigmoid(total)
            conv_out[rows8(t), :] = act.astype(bf16).astype(f32)
            return carry

        lax.fori_loop(0, HALF, one, 0, unroll=4)
        rows = span(h, half)
        part[rows, :] = mm(conv_out[rows, :].astype(bf16), wstate[...])
        return Reduce(net, part, h * half, half, *sums, proj_low)

    take(s)
    sum_first = convolve(s, reduces[0])
    for m in range(1, ZS):
        from_x[m - 1].wait_recv()
        there = tok.at[gh, net.flip(m), i]
        core_last.append(net.copy(there, there, net.sibling()))
    sum_first.across_z()
    for c in wout_z:
        c.wait_recv()
    wout_x = [net.copy(wout_in.at[:, own_part], wout_in.at[:, own_part], net.over_x())] if share else []
    for c in core_last:
        c.wait_recv()
    take(gh)
    sum_first.give()
    sum_last = convolve(gh, reduces[1])
    for c in late_y:
        c.wait_recv()
    for r in range(reps):
        wz[r * cols : (r + 1) * cols, :] = wz_all[r]
    sum_first.end()
    first_rows = span(s, half)
    last_rows = span(gh, half)
    proj[first_rows, :] = proj_low[first_rows, :].astype(f32)

    wstep = jnp.where(lax.broadcasted_iota(jnp.int32, (128, ch), 0) < DT_RANK, small[...], 0.0).astype(bf16)
    rate_ref[...] = -LOG2E * jnp.exp(small[DT_RANK:, :].astype(f32)[DECAY_ROW - DT_RANK : DECAY_ROW - DT_RANK + STATE, :])
    y = g

    def prepare(block):
        rows = span(block, size)
        pre = mm(proj_low[rows, :], wstep) + step_bias
        step_all = softplus(pre)
        values = conv_out[rows, :]
        step[...] = step_all
        u[...] = step_all * values
        for k in range(CHUNK):
            t = block * CHUNK + k
            fresh = segment_of(t, ends) != segment_of(t - sgn, ends)
            decay_step[8 * k : 8 * k + 8, :] = jnp.where(
                wide(fresh, ch), BIG, step_all[8 * k : 8 * k + 8, :]
            )
        return rows, pre, values

    def rates(n0):
        return [jnp.broadcast_to(rate_ref[n : n + 1, :], (8, ch)) for n in range(n0, n0 + NSTEP)]

    def forward(c, carry):
        block = c + s * (2 * rounds - 1 - 2 * c)
        rows, _, values = prepare(block)
        y[rows, :] = skip * values
        for n0 in range(0, STATE, NSTEP):
            rate = rates(n0)

            def body(k, hs):
                r = s * (CHUNK - 1 - k) + (1 - s) * k
                t = block * CHUNK + r
                pv = proj[rows8(t), :]
                st = decay_step[rows8(r), :]
                uv = u[rows8(r), :]
                total = y[rows8(t), :]
                new = []
                for m in range(NSTEP):
                    n = n0 + m
                    if m % 2 == 0:
                        hprev[t, n // 2] = jnp.concatenate([hs[m], hs[m + 1]], axis=0).astype(bf16)
                    h = jnp.exp2(st * rate[m]) * hs[m] + uv * pv[:, DT_RANK + n : DT_RANK + n + 1]
                    total = total + h * pv[:, DT_RANK + STATE + n : DT_RANK + STATE + n + 1]
                    new.append(h)
                y[rows8(t), :] = total
                return tuple(new)

            hs = lax.fori_loop(0, CHUNK, body, tuple(state[n] for n in range(n0, n0 + NSTEP)), unroll=CHUNK)
            for m in range(NSTEP):
                state[n0 + m] = hs[m]
        return carry

    sum_last.across_z()
    for c in wout_x:
        c.wait_recv()
    wout_y = [net.copy(wout_in, wout_all.at[yi], net.along_y(d)) for d in range(1, reps)]
    wout_all[yi] = wout_in[...]
    lax.fori_loop(0, rounds // 2, forward, 0)
    sum_last.give()
    lax.fori_loop(rounds // 2, rounds, forward, 0)
    y_send[...] = y[first_rows, :].astype(bf16)
    y_copy = net.copy(y_send, y_in, net.over_x())
    sum_last.end()
    proj[last_rows, :] = proj_low[last_rows, :].astype(f32)
    gate_in[...] = mm_nt(normed[gh], wz[...])
    lax.fori_loop(rounds, 2 * rounds - 1, forward, 0)
    for m in range(1, ZS):
        cot_z[m - 1].wait_recv()
        rows = span(net.flip(m) * 2 + i, HALF)
        cot_core.append(net.copy(cot.at[rows], cot.at[rows], net.sibling()))
    lax.fori_loop(2 * rounds - 1, 2 * rounds, forward, 0)
    for c in wout_y:
        c.wait_recv()
    for p in range(TP * reps):
        zp, yp, ip = p // (2 * reps), (p // 2) % reps, p % 2
        wout[p * piece : (p + 1) * piece, :] = wout_all[yp, zp * 2 + ip]
    for c in cot_core:
        c.wait_recv()
    y_copy.wait_recv()

    summed = y[last_rows, :] + y_in[...].astype(f32)
    raw[...] = jnp.swapaxes(summed.reshape(HALF, 8, ch), 0, 1).reshape(half, ch)

    def gate_rows(q, carry):
        rows = span(q, PACK)
        gate = gate_in[rows, :]
        sig = sigmoid(gate)
        act = gate * sig
        summed = raw[rows, :]
        grad_gated = mm(cot[rows, :], wout[...])
        gate_both[gh, rows, :] = (grad_gated * summed * sig * (1.0 + gate * (1.0 - sig))).astype(bf16)
        gate_in[rows, :] = grad_gated * act
        low = (summed * act).astype(bf16)
        gated[rows, :] = low
        return carry

    lax.fori_loop(0, ZS, gate_rows, 0)
    back = jnp.swapaxes(gate_in[...].reshape(8, HALF, ch), 0, 1).reshape(half, ch)
    g[last_rows, :] = back
    g_send[...] = back.astype(bf16)
    g_copy = net.copy(g_send, g_in, net.over_x())
    gate_copy = net.copy(gate_both.at[gh], gate_both.at[gh], net.over_x())

    for c in core_last:
        c.wait_send()

    def mixed_rows(q, carry):
        tok[gh, q] = mm_nt(gated[span(q, PACK), :], wout[...]).astype(bf16).reshape(2, HALF, width)
        return carry

    lax.fori_loop(0, ZS, mixed_rows, 0)
    mixed_copy = net.copy(tok.at[gh, :, 1 - i], mixed_core, net.sibling())
    quarter = width // ZS
    for q in range(ZS):
        value = mm_tn(cot[:, q * quarter : (q + 1) * quarter], gated[...]).astype(bf16)
        for r in range(reps):
            out_send[r, q * 2 * piece : (q + 1) * 2 * piece, :] = value[r * 2 * piece : (r + 1) * 2 * piece, :]
    out_copies = [
        net.copy(out_send.at[net.y_at(d)], out_y.at[d - 1], net.along_y(d)) for d in range(1, reps)
    ]

    state[...] = jnp.zeros_like(state)
    acc_ref[...] = jnp.zeros_like(acc_ref)
    bias_acc[...] = jnp.zeros_like(bias_acc)
    skip_acc[...] = jnp.zeros_like(skip_acc)

    def backward(c, carry):
        block = (1 - s) * (2 * rounds - 1 - c) + s * c
        rows, pre, values = prepare(block)
        s1[...] = jnp.zeros_like(s1)
        s2[...] = jnp.zeros_like(s2)
        for n0 in range(0, STATE, NSTEP):
            rate = rates(n0)

            def body(k, both):
                lams, accs = both
                r = s * k + (1 - s) * (CHUNK - 1 - k)
                t = block * CHUNK + r
                here = rows8(r)
                pv = proj[rows8(t), :]
                gv = g[rows8(t), :]
                uv = u[here, :]
                stv = step[here, :]
                st = decay_step[here, :]
                one = s1[here, :]
                two = s2[here, :]
                new_lams, new_accs = [], []
                for m in range(NSTEP):
                    n = n0 + m
                    if m % 2 == 0:
                        pair = hprev[t, n // 2].astype(f32)
                    a = jnp.exp2(st * rate[m])
                    ah = a * pair[8 * (m % 2) : 8 * (m % 2) + 8]
                    lam = gv * pv[:, DT_RANK + STATE + n : DT_RANK + STATE + n + 1] + lams[m]
                    w = lam * ah
                    new_lams.append(a * lam)
                    two = two + rate[m] * w
                    new_accs.append(accs[m] + stv * w)
                    one = one + lam * pv[:, DT_RANK + n : DT_RANK + n + 1]
                    pb[here, 128 * n : 128 * n + 128] = tiles(lam * uv)
                    pc[here, 128 * n : 128 * n + 128] = tiles(gv * ah)
                s1[here, :] = one
                s2[here, :] = two
                return tuple(new_lams), tuple(new_accs)

            first = (
                tuple(state[n] for n in range(n0, n0 + NSTEP)),
                tuple(acc_ref[n] for n in range(n0, n0 + NSTEP)),
            )
            lams, accs = lax.fori_loop(0, CHUNK, body, first, unroll=CHUNK)
            for m in range(NSTEP):
                state[n0 + m] = lams[m]
                acc_ref[n0 + m] = accs[m]
        gv = g[rows, :]
        one = s1[...]
        q = (LN2 * s2[...] + values * one) * sigmoid(pre)
        q_low = q.astype(bf16)
        bias_acc[...] += jnp.sum(q.reshape(CHUNK, 8, ch), axis=0)
        skip_acc[...] += jnp.sum((gv * values).reshape(CHUNK, 8, ch), axis=0)
        rows_grad[0:DT_RANK, :] += mm_tn(proj_low[rows, :], q_low)[0:DT_RANK, :]
        gu = jnp.sum(gv * u[...], axis=1, keepdims=True)
        lane = lax.broadcasted_iota(jnp.int32, (size, 128), 1)
        read_part = mm(pc[...].astype(bf16), ones[...]) + gu * jnp.where(
            lane < DT_RANK + STATE, proj[rows, :], 0.0
        )
        read_part = jnp.where(lane >= DT_RANK + STATE, pltpu.roll(read_part, STATE, 1), 0.0)
        part_back[rows, :] = mm_nt(q_low, wstep) + mm(pb[...].astype(bf16), ones[...]) + read_part
        g[rows, :] = gv * skip + step[...] * one
        return carry

    lax.fori_loop(0, 1, backward, 0)
    mixed_copy.wait_recv()
    for q in range(ZS):
        mixed_low[q] = (tok[gh, q, i].astype(f32) + mixed_core[q].astype(f32)).astype(bf16)
    mixed_zs = [net.copy(mixed_low.at[net.flip(m)], mixed_z.at[m - 1], net.along_z(m)) for m in range(1, ZS)]
    lax.fori_loop(1, 2, backward, 0)
    for c in out_copies:
        c.wait_recv()
    total = out_send[yi].astype(f32)
    for d in range(1, reps):
        total = total + out_y[d - 1].astype(f32)
    total = total.astype(bf16)
    for q in range(TP):
        out_low[q] = total[q * piece : (q + 1) * piece]
    if share:
        other_part = pl.ds(pl.multiple_of(gh * hp, hp), hp)
        out_x = net.copy(out_low.at[:, other_part], out_x_in, net.over_x())
    lax.fori_loop(2, rounds, backward, 0)
    back_last = Reduce(net, part_back, gh * half, half, *reduces[2], grad_proj)
    g_copy.wait_recv()
    g[first_rows, :] = g_in[...].astype(f32)
    lax.fori_loop(rounds, rounds + 1, backward, 0)
    back_last.across_z()
    lax.fori_loop(rounds + 1, rounds + 2, backward, 0)
    back_last.give()
    lax.fori_loop(rounds + 2, 2 * rounds, backward, 0)
    back_first = Reduce(net, part_back, s * half, half, *reduces[3], grad_proj)
    back_last.end()

    w = conv_pre
    sums[...] = jnp.zeros_like(sums)

    def pull(h):
        def one(b, carry):
            at = h * half + b * PACK
            rows = pl.ds(pl.multiple_of(PAD + at, 8), PACK)
            at = pl.ds(pl.multiple_of(at, PACK), PACK)
            c = conv_pre[rows, :]
            sig = sigmoid(c)
            w[rows, :] = (g[at, :] + mm_nt(grad_proj[at, :], wstate[...])) * (sig * (1.0 + c * (1.0 - sig)))
            return carry

        lax.fori_loop(0, half // PACK, one, 0)

    def convolve_back(h):
        def one(k, carry):
            t = h * HALF + k
            seg = segment_of(t, ends)
            here = w[rows8(t + 3), :]
            total = taps[3:4, :] * here
            new = [carry[3] + here * conv_in[rows8(t + 3), :], carry[4] + here]
            first = []
            for n in range(1, TAPS):
                back = t - n * sgn
                ahead = t + n * sgn
                same_back = wide((segment_of(back, ends) == seg).astype(f32), ch)
                same_ahead = wide((segment_of(ahead, ends) == seg).astype(f32), ch)
                first.insert(0, carry[3 - n] + here * (conv_in[rows8(back + 3), :] * same_back))
                total = total + taps[3 - n : 4 - n, :] * (w[rows8(ahead + 3), :] * same_ahead)
            raw[rows8(k), :] = total
            return tuple(first + new)

        carry = lax.fori_loop(0, HALF, one, tuple(sums[n] for n in range(TAPS + 1)), unroll=4)
        for n in range(TAPS + 1):
            sums[n] = carry[n]
        gx[h] = jnp.swapaxes(raw[...].reshape(HALF, 8, ch), 0, 1).reshape(half, ch).astype(bf16)
        return net.copy(gx.at[h], gx_in.at[h], net.over_x())

    pull(gh)
    back_first.across_z()
    gx_last = convolve_back(gh)
    for c in mixed_zs:
        c.wait_recv()
    total = tok[gh, z, i].astype(f32) + mixed_core[z].astype(f32)
    for m in range(1, ZS):
        total = total + mixed_z[m - 1].astype(f32)
    mixed_sum[...] = (total + tok_last[...].astype(f32)).astype(bf16)
    net.copy(mixed_sum, mixed, net.over_x())
    back_first.give()
    gate_copy.wait_recv()
    part_z = mm_tn(gate_both[0], normed[0, :, half_cols]) + mm_tn(gate_both[1], normed[1, :, half_cols])
    for r in range(reps):
        wz_low[r] = part_z[r * cols : (r + 1) * cols].astype(bf16)
    for d in range(1, reps):
        net.copy(wz_low.at[net.y_at(d)], wz_theirs.at[d - 1], net.along_y(d))
    net.save(wz_low.at[yi], wz_mine)
    back_first.end()
    out_half = out_low
    if share:
        out_x.wait_recv()
        out_half = out_x_in
        out_half[...] = (out_low[:, own_part].astype(f32) + out_x_in[...].astype(f32)).astype(bf16)
    out_all[j] = out_half[j]
    out_zs = []
    for m in range(1, TP):
        zm, im = net.shared(m)
        out_zs.append(net.copy(out_half.at[zm * 2 + im], out_all.at[j], net.to_shared(m)))
    pull(s)
    gx_first = convolve_back(s)

    def rows_of(q, carry):
        rows = span(q, PACK)
        value = (
            mm(gx[s, rows, :], wx[...]) + mm(gx_in[s, rows, :], wx[...]) + mm(gate_both[s, rows, :], wz[...])
        )
        tok[gh, q] = value.astype(bf16).reshape(2, HALF, width)
        return carry

    mixed_copy.wait_send()
    gx_last.wait_recv()
    lax.fori_loop(0, ZS, rows_of, 0)
    to_core = net.copy(tok.at[gh, :, 1 - i], mixed_core, net.sibling())
    for c in mixed_zs:
        c.wait_send()
    gain_acc[0] = jnp.zeros(gain_acc.shape[1:], f32)
    to_core.wait_recv()
    for q in range(ZS):
        mixed_low[q] = (tok[gh, q, i].astype(f32) + mixed_core[q].astype(f32)).astype(bf16)
    to_z = [net.copy(mixed_low.at[net.flip(m)], mixed_z.at[m - 1], net.along_z(m)) for m in range(1, ZS)]

    def gain_terms(q, carry):
        x = tok[s, q].astype(f32).reshape(PACK, width)
        inv = lax.rsqrt(jnp.mean(x * x, axis=1, keepdims=True) + EPS)
        terms = tok[gh, q].astype(f32).reshape(PACK, width) * (x * inv)
        gain_acc[0] += jnp.sum(terms.reshape(PACK // 8, 8, width), axis=0)
        return carry

    lax.fori_loop(0, ZS, gain_terms, 0)
    stages = [
        [net.sibling()],
        [net.over_x()],
        [net.along_y(d) for d in range(1, reps)],
        [net.along_z(1)],
        [net.along_z(2)],
    ]
    slot = [0]

    def gain_start(k):
        cs = []
        for peer in stages[k]:
            cs.append((slot[0], net.copy(gain_acc.at[k], gain_in.at[slot[0]], peer)))
            slot[0] += 1
        return cs

    def gain_end(k, cs):
        total = gain_acc[k]
        for at, c in cs:
            c.wait_recv()
            total = total + gain_in[at]
        gain_acc[k + 1] = total

    cs = gain_start(0)
    gx_first.wait_recv()
    part_x = mm_tn(gx[0], normed[0, :, half_cols]) + mm_tn(gx[1], normed[1, :, half_cols])
    part_x = part_x + mm_tn(gx_in[0], normed[0, :, half_cols]) + mm_tn(gx_in[1], normed[1, :, half_cols])
    for r in range(reps):
        wx_low[r] = part_x[r * cols : (r + 1) * cols].astype(bf16)
    for d in range(1, reps):
        net.copy(wx_low.at[net.y_at(d)], wx_theirs.at[d - 1], net.along_y(d))
    net.save(wx_low.at[yi], wx_mine)
    gain_end(0, cs)
    cs = gain_start(1)
    state_all = mm_tn(conv_out[...].astype(bf16), grad_proj[...])
    rows_grad[STEP_ROW : STEP_ROW + 1, :] = jnp.sum(bias_acc[...], axis=0, keepdims=True)
    rows_grad[SKIP_ROW : SKIP_ROW + 1, :] = jnp.sum(skip_acc[...], axis=0, keepdims=True)
    for n in range(STATE):
        rows_grad[DECAY_ROW + n : DECAY_ROW + n + 1, :] = (
            jnp.sum(acc_ref[n], axis=0, keepdims=True) * rate_ref[n : n + 1, :] * LN2
        )
    for n in range(TAPS + 1):
        rows_grad[TAP_ROW + n : TAP_ROW + n + 1, :] = jnp.sum(sums[n], axis=0, keepdims=True)
    for r in range(reps):
        state_part[r] = state_all[r * cols : (r + 1) * cols, :]
        rows_part[r] = rows_grad[:, r * cols : (r + 1) * cols]
    for d in range(1, reps):
        net.copy(state_part.at[net.y_at(d)], state_theirs.at[d - 1], net.along_y(d))
        net.copy(rows_part.at[net.y_at(d)], rows_theirs.at[d - 1], net.along_y(d))
    net.save(state_part.at[yi], state_mine)
    net.save(rows_part.at[yi], rows_mine)
    gain_end(1, cs)
    cs = gain_start(2)
    gain_end(2, cs)
    cs = gain_start(3)
    for c in out_zs:
        c.wait_recv()
    net.copy(out_all.at[pl.ds(gh * ZS, ZS)], out_theirs, net.over_x())
    net.save(out_all.at[pl.ds(s * ZS, ZS)], out_mine)
    x = tok[s, z, i].astype(f32)
    inv = lax.rsqrt(jnp.mean(x * x, axis=1, keepdims=True) + EPS)
    unit = x * inv
    gain_end(3, cs)
    cs = gain_start(4)
    grad = tok[gh, z, i].astype(f32) + mixed_core[z].astype(f32)
    for m in range(1, ZS):
        to_z[m - 1].wait_recv()
        grad = grad + mixed_z[m - 1].astype(f32)
    scaled = grad * gain[...]
    mean = jnp.mean(scaled * unit, axis=1, keepdims=True)
    grad_tokens[...] = inv * (scaled - unit * mean) + cot_own[...].astype(f32)
    gain_end(4, cs)
    grad_gain[...] = jnp.sum(gain_acc[5], axis=0, keepdims=True)
    net.finish()


def block(reps, grids, gain, wstep, taps, bias, step, skip, decay, wstate, wout, cot, tokens, wx, wz):
    cols, width = wx.shape
    ch = reps * cols
    rows = TP * PACK
    half = rows // 2
    piece = wout.shape[0]
    hp = piece // 2 if piece % 32 == 0 else piece
    size = CHUNK * 8
    sds = jax.ShapeDtypeStruct
    V, H = pltpu.VMEM, pl.ANY
    args = [(grids, pltpu.SMEM)]
    args += [(a, V) for a in (gain, wstep, taps, bias, step, skip, decay, wstate, wout, cot)]
    args += [(a, H) for a in (tokens, wx, wz)]
    outs = (
        (sds((HALF, width), bf16), H),
        (sds((HALF, width), f32), V),
        (sds((cols, width // 2), bf16), H),
        (sds((reps - 1, cols, width // 2), bf16), H),
        (sds((cols, width // 2), bf16), H),
        (sds((reps - 1, cols, width // 2), bf16), H),
        (sds((ZS, hp, ch), bf16), H),
        (sds((ZS, hp, ch), bf16), H),
        (sds((SMALL_ROWS, cols), f32), H),
        (sds((reps - 1, SMALL_ROWS, cols), f32), H),
        (sds((cols, 128), f32), H),
        (sds((reps - 1, cols, 128), f32), H),
        (sds((1, width), f32), V),
    )
    big = V((rows, ch), f32)
    padded = V((rows + 2 * PAD, ch), f32)
    part = V((rows, 128), f32)
    low = V((half, ch), bf16)
    round_rows = V((size, ch), f32)
    state = V((STATE, 8, ch), f32)
    scratch = (
        V((reps, TP, 16, 128), bf16),
        V((1, width), f32),
        V((2, 8, 128), f32),
        V((reps, cols, width), bf16),
        V((ch, width), bf16),
        V((reps, cols, width), bf16),
        V((ch, width), bf16),
        V((reps, SMALL_ROWS, cols), bf16),
        V((SMALL_ROWS, ch), bf16),
        V((reps, cols, 128), bf16),
        V((ch, 128), bf16),
        V((TP, piece, ch), bf16),
        V((TP, piece, ch), bf16),
        V((reps, TP, piece, ch), bf16),
        V((width, ch), bf16),
        V((2, ZS, 2, HALF, width), bf16),
        V((2, half, width), bf16),
        V((half, ch), f32),
        padded,
        padded,
        big,
        V((half, ch), f32),
        part,
        V((rows, 128), bf16),
        part,
        V((PACK, STATE // 2, 16, ch), bf16),
        round_rows,
        round_rows,
        round_rows,
        state,
        state,
        V((STATE, ch), f32),
        round_rows,
        round_rows,
        V((size, STATE * 128), f32),
        V((size, STATE * 128), f32),
        V((STATE * 128, 128), bf16),
        V((8, ch), f32),
        V((8, ch), f32),
        big,
        low,
        low,
        low,
        low,
        low,
        V((2, half, ch), bf16),
        V((half, width), bf16),
        V((ZS, HALF, width), bf16),
        V((ZS, HALF, width), bf16),
        V((ZS - 1, HALF, width), bf16),
        V((HALF, width), bf16),
        V((HALF, width), bf16),
        V((reps, TP * piece, ch), bf16),
        V((reps - 1, TP * piece, ch), bf16),
        V((TP, piece, ch), bf16),
        V((TP, hp, ch), bf16),
        V((TP, hp, ch), bf16),
        V((reps, cols, width // 2), bf16),
        part,
        V((rows, 128), bf16),
        V((TAPS + 1, 8, ch), f32),
        V((2, half, ch), bf16),
        V((2, half, ch), bf16),
        V((reps, cols, width // 2), bf16),
        V((SMALL_ROWS, ch), f32),
        V((reps, SMALL_ROWS, cols), f32),
        V((reps, cols, 128), f32),
        V((6, 8, width), f32),
        V((3 + reps, 8, width), f32),
    ) + REDUCE_SCRATCH * 4
    copies = 120 + 10 * (reps - 1)
    return fused(partial(block_kernel, reps), 1, copies, 12, outs, args, scratch)


def place_kernel(
    reps, index, mixed_in, tokens_in, wx_mine, wx_theirs, wz_mine, wz_theirs, out_mine, out_theirs,
    rows_mine, rows_theirs, state_mine, state_theirs, gain_in,
    mixed, grad_tokens, gain, wx, wz, wout, taps, bias, wstate, wstep, step, decay, skip,
):
    mixed[...] = mixed_in[...]
    grad_tokens[...] = tokens_in[...]
    width, n = gain_in.shape[1], gain.shape[1]
    moved = pltpu.roll(jnp.broadcast_to(gain_in[...], (8, width)), width - index[0] * n, 1)
    gain[...] = moved[0:1, 0:n]

    def total(mine, theirs):
        value = mine[...].astype(f32)
        for d in range(reps - 1):
            value = value + theirs[d].astype(f32)
        return value

    wx[...] = total(wx_mine, wx_theirs)
    wz[...] = total(wz_mine, wz_theirs)
    cols = wx.shape[0]
    hp = out_mine.shape[1]
    share = hp < wout.shape[0]
    s = index[1]
    for q in range(ZS):
        parts = [(out_mine[q].astype(f32), s), (out_theirs[q].astype(f32), 1 - s)]
        if not share:
            parts = [(parts[0][0] + parts[1][0], 0)]
        for value, place in parts:
            for r in range(reps):
                at = ((q // 2) * reps + r) * 2 + q % 2
                rows = pl.ds(pl.multiple_of(place * hp, hp), hp) if share else pl.ds(0, hp)
                wout[rows, at * cols : (at + 1) * cols] = value[:, r * cols : (r + 1) * cols]
    rows = total(rows_mine, rows_theirs)
    wstep[...] = rows[0:DT_RANK]
    taps[...] = rows[TAP_ROW : TAP_ROW + TAPS]
    bias[...] = rows[BIAS_ROW : BIAS_ROW + 1]
    step[...] = rows[STEP_ROW : STEP_ROW + 1]
    skip[...] = rows[SKIP_ROW : SKIP_ROW + 1]
    decay[...] = rows[DECAY_ROW : DECAY_ROW + STATE]
    wstate[...] = total(state_mine, state_theirs)


def place(reps, index, results):
    mixed, grad_tokens, wx = results[0], results[1], results[2]
    ch = results[6].shape[2]
    cols = wx.shape[0]
    width = mixed.shape[1]
    piece = width // (TP * reps)
    sds = jax.ShapeDtypeStruct
    V = pl.BlockSpec(memory_space=pltpu.VMEM)
    outs = (
        sds(mixed.shape, bf16),
        sds(grad_tokens.shape, f32),
        sds((1, width // (2 * TP * reps)), f32),
        sds(wx.shape, f32),
        sds(wx.shape, f32),
        sds((piece, ZS * ch), f32),
        sds((TAPS, cols), f32),
        sds((1, cols), f32),
        sds((cols, 128), f32),
        sds((DT_RANK, cols), f32),
        sds((1, cols), f32),
        sds((STATE, cols), f32),
        sds((1, cols), f32),
    )
    return pl.pallas_call(
        partial(place_kernel, reps),
        out_shape=outs,
        in_specs=[pl.BlockSpec(memory_space=pltpu.SMEM)] + [V] * len(results),
        out_specs=tuple([V] * len(outs)),
        compiler_params=pltpu.CompilerParams(vmem_limit_bytes=63 << 20),
    )(index, *results)


def local(
    reps, tokens, item_grids, norm_gain, proj_in_x, proj_in_z, proj_out, conv_weight, conv_bias,
    proj_state, proj_step, step_bias, decay_log, skip_gain, grad_out,
):
    width = tokens.shape[1]
    results = block(
        reps, item_grids, norm_gain[None], proj_step[0], conv_weight[0], conv_bias, step_bias, skip_gain,
        decay_log[0], proj_state[0], proj_out.T, grad_out.reshape(HALF, width), tokens, proj_in_x.T,
        proj_in_z.T,
    )
    s = lax.axis_index("dir")
    index = jnp.stack([s * lax.axis_size("dp") + lax.axis_index("dp"), s]).astype(jnp.int32)
    (
        mixed, grad_tokens, grad_gain, grad_wx, grad_wz, grad_wout, grad_taps, grad_bias, grad_wstate,
        grad_wstep, grad_step, grad_decay, grad_skip,
    ) = place(reps, index, results)
    return (
        mixed.reshape(1, 1, HALF, width),
        grad_tokens.reshape(1, 1, HALF, width),
        grad_gain[0],
        grad_wx.T,
        grad_wz.T,
        grad_wout.T,
        grad_taps[None],
        grad_bias,
        grad_wstate[None],
        grad_wstep[None],
        grad_step,
        grad_decay[None],
        grad_skip,
    )


def solution(mesh):
    reps = mesh.shape["dp"] // TP
    return jax.shard_map(
        partial(local, reps),
        mesh=mesh,
        in_specs=(
            P("dp", None),
            P("dp", None),
            P("dp"),
            P(None, "dp"),
            P(None, "dp"),
            P(None, "dp"),
            P("dir", None, "dp"),
            P("dir", "dp"),
            P("dir", "dp", None),
            P("dir", None, "dp"),
            P("dir", "dp"),
            P("dir", None, "dp"),
            P("dir", "dp"),
            P("dp", "dir", None, None),
        ),
        out_specs=(
            P("dp", "dir", None, None),
            P("dp", "dir", None, None),
            P(("dir", "dp")),
            P("dir", "dp"),
            P("dir", "dp"),
            P("dir", "dp"),
            P("dir", None, "dp"),
            P("dir", "dp"),
            P("dir", "dp", None),
            P("dir", None, "dp"),
            P("dir", "dp"),
            P("dir", None, "dp"),
            P("dir", "dp"),
        ),
        check_vma=False,
    )
```

time: 191 us -> 169 us (0.88)
  Pallas kernels: 189 us -> 168 us
    pallas_call x3 -> x1, Pallas kernels: 186 us -> 165 us  [fused(): pl.pallas_call(kernel, out_shape=tuple((o for o, _ in outs)), in_specs=[p...]
where the time goes in v4:
time: 169 us
  Pallas kernels  168 us (99%)
    pallas_call x1, Pallas kernels, fused(): pl.pallas_call(kernel, out_shape=tuple((o for o, _ in outs)), in_specs=[p...  165 us

profile of v4, /device:TPU:0, one launch (start us, length us, event | category | flops | bytes accessed | tf_op | source)
XLA Modules:
  0.0 169.3 jit_solution(5812096597561252856)
XLA Ops:
  0.6 0.6 pad_add_fusion.index
  1.2 164.6 %shard_map.237 = (bf16[64,1536]{1,0:T(8,128)(2,1)}, f32[64,1536]{1,0:T(8,128)}, bf16[192,768]{1,0:T(8,128)(2,1)}, bf16[1,192,768]{2,1,0:T(8,128)(2,1)}, bf16[192...) custom-call(s32[2,2]{1,0:T(2,128)} %refs_0_.1, ...), custom_call_target="tpu_custom_call" | custom-call | tf_op jit(solution)/shard_map/pallas_call | solution.py:230
  165.8 3.2 %shard_map.238 = (bf16[64,1536]{1,0:T(8,128)(2,1)}, f32[64,1536]{1,0:T(8,128)}, f32[1,48]{1,0:T(1,128)}, f32[192,768]{1,0:T(8,128)}, f32[192,768]{1,0:T(8,128)},...) custom-call(s32[2]{0:T(128)} %pad_add_fusion.index, ...), custom_call_target="tpu_custom_call" | custom-call | tf_op jit(solution)/shard_map/pallas_call | solution.py:996

commit v5 on v4

--- a/solution.py
+++ b/solution.py
@@ -159,6 +159,11 @@
         self.copies.append(c)
         return c
 
+    def gather_z(self, source, at):
+        c = ZGather(self, source, at)
+        self.copies.append(c)
+        return c
+
     def load(self, source, target):
         c = pltpu.make_async_copy(source, target, self.local.at[self.moved])
         self.moved += 1
@@ -174,6 +179,56 @@
             c.wait_send()
         for c in self.saves:
             c.wait()
+
+
+class ZGather:
+    def __init__(self, net, source, at):
+        self.net, self.at = net, at
+        self.near = [net.copy(source, at(net.z), net.along_z(m)) for m in (1, 2)]
+        self.inner = lax.rem(net.z + 1, ZS) >= 2
+        k = net.used
+        net.used += 2
+        self.direct = self.make(source, at(net.z), k, k, 3)
+        far = at(net.flip(2))
+        self.onward = self.make(far, far, k + 1, k, 1)
+        self.got = False
+
+        @pl.when(self.inner)
+        def _():
+            self.direct.start()
+
+    def make(self, source, target, out, arrival, m):
+        return pltpu.make_async_remote_copy(
+            src_ref=source,
+            dst_ref=target,
+            send_sem=self.net.send.at[out],
+            recv_sem=self.net.recv.at[arrival],
+            device_id=self.net.along_z(m),
+            device_id_type=pl.DeviceIdType.MESH,
+        )
+
+    def wait(self, m):
+        if m < 3:
+            self.near[m - 1].wait_recv()
+            if m == 2:
+
+                @pl.when(self.inner)
+                def _():
+                    self.onward.start()
+
+        elif not self.got:
+            self.direct.wait_recv()
+            self.got = True
+        return self.at(self.net.flip(m))
+
+    def wait_recv(self):
+        pass
+
+    def wait_send(self):
+        @pl.when(self.inner)
+        def _():
+            self.direct.wait_send()
+            self.onward.wait_send()
 
 
 class Reduce:
@@ -266,7 +321,7 @@
     ) = take_refs(15)
     (y_send, y_in, g_send, g_in, gated, gate_both, cot, mixed_core, mixed_low, mixed_z, mixed_sum, tok_last) = take_refs(12)
     (out_send, out_y, out_low, out_x_in, out_all, wz_low, part_back, grad_proj, sums, gx, gx_in) = take_refs(11)
-    (wx_low, rows_grad, rows_part, state_part, gain_acc, gain_in) = take_refs(6)
+    (wx_low, rows_grad, rows_part, state_part, rows_low, state_low, gain_acc, gain_in) = take_refs(8)
     reduces = [take_refs(3) for _ in range(4)]
     send, recv, local_sems = refs
     net = Net(reps, send, recv, local_sems)
@@ -302,7 +357,7 @@
     net.met()
     own_first = tokens.at[pl.ds(pl.multiple_of(s * HALF, HALF), HALF)]
     own_last = tokens.at[pl.ds(pl.multiple_of(gh * HALF, HALF), HALF)]
-    from_z = [net.copy(own_first, tok.at[s, z, i], net.along_z(m)) for m in range(1, ZS)]
+    from_z = net.gather_z(own_first, lambda zz: tok.at[s, zz, i])
     core_first = [net.copy(own_first, tok.at[s, z, i], net.sibling())]
     core_last = [net.copy(own_last, tok.at[gh, z, i], net.sibling())]
     metas = [net.copy(meta_all.at[yi, j], meta_all.at[yi, j], net.to_shared(m)) for m in range(1, TP)]
@@ -339,8 +394,7 @@
 
     from_x = []
     for m in range(1, ZS):
-        from_z[m - 1].wait_recv()
-        there = tok.at[s, net.flip(m), i]
+        there = from_z.wait(m)
         core_first.append(net.copy(there, there, net.sibling()))
         from_x.append(net.copy(there, there, net.over_x()))
     wout_z = []
@@ -348,7 +402,7 @@
         zm, im = net.shared(m)
         wout_z.append(net.copy(wout_send.at[zm * 2 + im, own_part], wout_in.at[j, own_part], net.to_shared(m)))
     cot_x.wait_recv()
-    cot_z = [net.copy(cot.at[cot_mine], cot.at[cot_mine], net.along_z(m)) for m in range(1, ZS)]
+    cot_z = net.gather_z(cot.at[cot_mine], lambda zz: cot.at[span(zz * 2 + i, HALF)])
     cot_core = [net.copy(cot.at[cot_mine], cot.at[cot_mine], net.sibling())]
     for c in meta_y + first_y:
         c.wait_recv()
@@ -403,23 +457,24 @@
 
     take(s)
     sum_first = convolve(s, reduces[0])
-    for m in range(1, ZS):
+
+    def last_tokens(m):
         from_x[m - 1].wait_recv()
         there = tok.at[gh, net.flip(m), i]
         core_last.append(net.copy(there, there, net.sibling()))
+
+    last_tokens(1)
     sum_first.across_z()
+    last_tokens(2)
+    last_tokens(3)
     for c in wout_z:
         c.wait_recv()
     wout_x = [net.copy(wout_in.at[:, own_part], wout_in.at[:, own_part], net.over_x())] if share else []
+    sum_first.give()
     for c in core_last:
         c.wait_recv()
     take(gh)
-    sum_first.give()
     sum_last = convolve(gh, reduces[1])
-    for c in late_y:
-        c.wait_recv()
-    for r in range(reps):
-        wz[r * cols : (r + 1) * cols, :] = wz_all[r]
     sum_first.end()
     first_rows = span(s, half)
     last_rows = span(gh, half)
@@ -484,25 +539,28 @@
     wout_all[yi] = wout_in[...]
     lax.fori_loop(0, rounds // 2, forward, 0)
     sum_last.give()
+    for m in (1, 2):
+        there = cot_z.wait(m)
+        cot_core.append(net.copy(there, there, net.sibling()))
     lax.fori_loop(rounds // 2, rounds, forward, 0)
     y_send[...] = y[first_rows, :].astype(bf16)
     y_copy = net.copy(y_send, y_in, net.over_x())
     sum_last.end()
     proj[last_rows, :] = proj_low[last_rows, :].astype(f32)
+    for c in late_y:
+        c.wait_recv()
+    for r in range(reps):
+        wz[r * cols : (r + 1) * cols, :] = wz_all[r]
     gate_in[...] = mm_nt(normed[gh], wz[...])
     lax.fori_loop(rounds, 2 * rounds - 1, forward, 0)
-    for m in range(1, ZS):
-        cot_z[m - 1].wait_recv()
-        rows = span(net.flip(m) * 2 + i, HALF)
-        cot_core.append(net.copy(cot.at[rows], cot.at[rows], net.sibling()))
+    there = cot_z.wait(3)
+    cot_core.append(net.copy(there, there, net.sibling()))
     lax.fori_loop(2 * rounds - 1, 2 * rounds, forward, 0)
     for c in wout_y:
         c.wait_recv()
     for p in range(TP * reps):
         zp, yp, ip = p // (2 * reps), (p // 2) % reps, p % 2
         wout[p * piece : (p + 1) * piece, :] = wout_all[yp, zp * 2 + ip]
-    for c in cot_core:
-        c.wait_recv()
     y_copy.wait_recv()
 
     summed = y[last_rows, :] + y_in[...].astype(f32)
@@ -511,40 +569,36 @@
     def gate_rows(q, carry):
         rows = span(q, PACK)
         gate = gate_in[rows, :]
+        low = (raw[rows, :] * (gate * sigmoid(gate))).astype(bf16)
+        gated[rows, :] = low
+        tok[gh, q] = mm_nt(low, wout[...]).astype(bf16).reshape(2, HALF, width)
+        return carry
+
+    def grad_rows(q, carry):
+        rows = span(q, PACK)
+        gate = gate_in[rows, :]
         sig = sigmoid(gate)
-        act = gate * sig
-        summed = raw[rows, :]
         grad_gated = mm(cot[rows, :], wout[...])
-        gate_both[gh, rows, :] = (grad_gated * summed * sig * (1.0 + gate * (1.0 - sig))).astype(bf16)
-        gate_in[rows, :] = grad_gated * act
-        low = (summed * act).astype(bf16)
-        gated[rows, :] = low
+        gate_both[gh, rows, :] = (grad_gated * raw[rows, :] * sig * (1.0 + gate * (1.0 - sig))).astype(bf16)
+        gate_in[rows, :] = grad_gated * (gate * sig)
         return carry
 
+    for c in core_last:
+        c.wait_send()
     lax.fori_loop(0, ZS, gate_rows, 0)
+    mixed_copy = net.copy(tok.at[gh, :, 1 - i], mixed_core, net.sibling())
+    for c in cot_core:
+        c.wait_recv()
+    lax.fori_loop(0, ZS, grad_rows, 0)
     back = jnp.swapaxes(gate_in[...].reshape(8, HALF, ch), 0, 1).reshape(half, ch)
     g[last_rows, :] = back
     g_send[...] = back.astype(bf16)
     g_copy = net.copy(g_send, g_in, net.over_x())
     gate_copy = net.copy(gate_both.at[gh], gate_both.at[gh], net.over_x())
-
-    for c in core_last:
-        c.wait_send()
-
-    def mixed_rows(q, carry):
-        tok[gh, q] = mm_nt(gated[span(q, PACK), :], wout[...]).astype(bf16).reshape(2, HALF, width)
-        return carry
-
-    lax.fori_loop(0, ZS, mixed_rows, 0)
-    mixed_copy = net.copy(tok.at[gh, :, 1 - i], mixed_core, net.sibling())
-    quarter = width // ZS
+    mixed_copy.wait_recv()
     for q in range(ZS):
-        value = mm_tn(cot[:, q * quarter : (q + 1) * quarter], gated[...]).astype(bf16)
-        for r in range(reps):
-            out_send[r, q * 2 * piece : (q + 1) * 2 * piece, :] = value[r * 2 * piece : (r + 1) * 2 * piece, :]
-    out_copies = [
-        net.copy(out_send.at[net.y_at(d)], out_y.at[d - 1], net.along_y(d)) for d in range(1, reps)
-    ]
+        mixed_low[q] = (tok[gh, q, i].astype(f32) + mixed_core[q].astype(f32)).astype(bf16)
+    mixed_zs = [net.copy(mixed_low.at[net.flip(m)], mixed_z.at[m - 1], net.along_z(m)) for m in range(1, ZS)]
 
     state[...] = jnp.zeros_like(state)
     acc_ref[...] = jnp.zeros_like(acc_ref)
@@ -616,11 +670,19 @@
         return carry
 
     lax.fori_loop(0, 1, backward, 0)
-    mixed_copy.wait_recv()
+    quarter = width // ZS
     for q in range(ZS):
-        mixed_low[q] = (tok[gh, q, i].astype(f32) + mixed_core[q].astype(f32)).astype(bf16)
-    mixed_zs = [net.copy(mixed_low.at[net.flip(m)], mixed_z.at[m - 1], net.along_z(m)) for m in range(1, ZS)]
-    lax.fori_loop(1, 2, backward, 0)
+        value = mm_tn(cot[:, q * quarter : (q + 1) * quarter], gated[...]).astype(bf16)
+        for r in range(reps):
+            out_send[r, q * 2 * piece : (q + 1) * 2 * piece, :] = value[r * 2 * piece : (r + 1) * 2 * piece, :]
+    out_copies = [
+        net.copy(out_send.at[net.y_at(d)], out_y.at[d - 1], net.along_y(d)) for d in range(1, reps)
+    ]
+    lax.fori_loop(1, rounds, backward, 0)
+    back_last = Reduce(net, part_back, gh * half, half, *reduces[2], grad_proj)
+    g_copy.wait_recv()
+    g[first_rows, :] = g_in[...].astype(f32)
+    lax.fori_loop(rounds, rounds + 1, backward, 0)
     for c in out_copies:
         c.wait_recv()
     total = out_send[yi].astype(f32)
@@ -632,15 +694,10 @@
     if share:
         other_part = pl.ds(pl.multiple_of(gh * hp, hp), hp)
         out_x = net.copy(out_low.at[:, other_part], out_x_in, net.over_x())
-    lax.fori_loop(2, rounds, backward, 0)
-    back_last = Reduce(net, part_back, gh * half, half, *reduces[2], grad_proj)
-    g_copy.wait_recv()
-    g[first_rows, :] = g_in[...].astype(f32)
-    lax.fori_loop(rounds, rounds + 1, backward, 0)
     back_last.across_z()
-    lax.fori_loop(rounds + 1, rounds + 2, backward, 0)
+    lax.fori_loop(rounds + 1, 2 * rounds - 1, backward, 0)
     back_last.give()
-    lax.fori_loop(rounds + 2, 2 * rounds, backward, 0)
+    lax.fori_loop(2 * rounds - 1, 2 * rounds, backward, 0)
     back_first = Reduce(net, part_back, s * half, half, *reduces[3], grad_proj)
     back_last.end()
 
@@ -729,24 +786,17 @@
     to_core = net.copy(tok.at[gh, :, 1 - i], mixed_core, net.sibling())
     for c in mixed_zs:
         c.wait_send()
-    gain_acc[0] = jnp.zeros(gain_acc.shape[1:], f32)
-    to_core.wait_recv()
-    for q in range(ZS):
-        mixed_low[q] = (tok[gh, q, i].astype(f32) + mixed_core[q].astype(f32)).astype(bf16)
-    to_z = [net.copy(mixed_low.at[net.flip(m)], mixed_z.at[m - 1], net.along_z(m)) for m in range(1, ZS)]
-
     def gain_terms(q, carry):
         x = tok[s, q].astype(f32).reshape(PACK, width)
         inv = lax.rsqrt(jnp.mean(x * x, axis=1, keepdims=True) + EPS)
         terms = tok[gh, q].astype(f32).reshape(PACK, width) * (x * inv)
-        gain_acc[0] += jnp.sum(terms.reshape(PACK // 8, 8, width), axis=0)
-        return carry
-
-    lax.fori_loop(0, ZS, gain_terms, 0)
+        return carry + jnp.sum(terms.reshape(PACK // 8, 8, width), axis=0)
+
+    gain_acc[0] = jnp.sum(lax.fori_loop(0, ZS, gain_terms, jnp.zeros((8, width), f32)), axis=0, keepdims=True)
     stages = [
+        [net.along_y(d) for d in range(1, reps)],
         [net.sibling()],
         [net.over_x()],
-        [net.along_y(d) for d in range(1, reps)],
         [net.along_z(1)],
         [net.along_z(2)],
     ]
@@ -767,16 +817,10 @@
         gain_acc[k + 1] = total
 
     cs = gain_start(0)
-    gx_first.wait_recv()
-    part_x = mm_tn(gx[0], normed[0, :, half_cols]) + mm_tn(gx[1], normed[1, :, half_cols])
-    part_x = part_x + mm_tn(gx_in[0], normed[0, :, half_cols]) + mm_tn(gx_in[1], normed[1, :, half_cols])
-    for r in range(reps):
-        wx_low[r] = part_x[r * cols : (r + 1) * cols].astype(bf16)
-    for d in range(1, reps):
-        net.copy(wx_low.at[net.y_at(d)], wx_theirs.at[d - 1], net.along_y(d))
-    net.save(wx_low.at[yi], wx_mine)
-    gain_end(0, cs)
-    cs = gain_start(1)
+    to_core.wait_recv()
+    for q in range(ZS):
+        mixed_low[q] = (tok[gh, q, i].astype(f32) + mixed_core[q].astype(f32)).astype(bf16)
+    to_z = [net.copy(mixed_low.at[net.flip(m)], mixed_z.at[m - 1], net.along_z(m)) for m in range(1, ZS)]
     state_all = mm_tn(conv_out[...].astype(bf16), grad_proj[...])
     rows_grad[STEP_ROW : STEP_ROW + 1, :] = jnp.sum(bias_acc[...], axis=0, keepdims=True)
     rows_grad[SKIP_ROW : SKIP_ROW + 1, :] = jnp.sum(skip_acc[...], axis=0, keepdims=True)
@@ -789,19 +833,32 @@
     for r in range(reps):
         state_part[r] = state_all[r * cols : (r + 1) * cols, :]
         rows_part[r] = rows_grad[:, r * cols : (r + 1) * cols]
+    for r in range(reps):
+        state_low[r] = state_part[r].astype(bf16)
+        rows_low[r] = rows_part[r].astype(bf16)
     for d in range(1, reps):
-        net.copy(state_part.at[net.y_at(d)], state_theirs.at[d - 1], net.along_y(d))
-        net.copy(rows_part.at[net.y_at(d)], rows_theirs.at[d - 1], net.along_y(d))
+        net.copy(state_low.at[net.y_at(d)], state_theirs.at[d - 1], net.along_y(d))
+        net.copy(rows_low.at[net.y_at(d)], rows_theirs.at[d - 1], net.along_y(d))
     net.save(state_part.at[yi], state_mine)
     net.save(rows_part.at[yi], rows_mine)
+    gain_end(0, cs)
+    cs = gain_start(1)
+    gx_first.wait_recv()
+    part_x = mm_tn(gx[0], normed[0, :, half_cols]) + mm_tn(gx[1], normed[1, :, half_cols])
+    part_x = part_x + mm_tn(gx_in[0], normed[0, :, half_cols]) + mm_tn(gx_in[1], normed[1, :, half_cols])
+    for r in range(reps):
+        wx_low[r] = part_x[r * cols : (r + 1) * cols].astype(bf16)
+    for d in range(1, reps):
+        net.copy(wx_low.at[net.y_at(d)], wx_theirs.at[d - 1], net.along_y(d))
+    net.save(wx_low.at[yi], wx_mine)
     gain_end(1, cs)
     cs = gain_start(2)
-    gain_end(2, cs)
-    cs = gain_start(3)
     for c in out_zs:
         c.wait_recv()
     net.copy(out_all.at[pl.ds(gh * ZS, ZS)], out_theirs, net.over_x())
     net.save(out_all.at[pl.ds(s * ZS, ZS)], out_mine)
+    gain_end(2, cs)
+    cs = gain_start(3)
     x = tok[s, z, i].astype(f32)
     inv = lax.rsqrt(jnp.mean(x * x, axis=1, keepdims=True) + EPS)
     unit = x * inv
@@ -815,7 +872,7 @@
     mean = jnp.mean(scaled * unit, axis=1, keepdims=True)
     grad_tokens[...] = inv * (scaled - unit * mean) + cot_own[...].astype(f32)
     gain_end(4, cs)
-    grad_gain[...] = jnp.sum(gain_acc[5], axis=0, keepdims=True)
+    grad_gain[...] = gain_acc[5]
     net.finish()
 
 
@@ -842,9 +899,9 @@
         (sds((ZS, hp, ch), bf16), H),
         (sds((ZS, hp, ch), bf16), H),
         (sds((SMALL_ROWS, cols), f32), H),
-        (sds((reps - 1, SMALL_ROWS, cols), f32), H),
+        (sds((reps - 1, SMALL_ROWS, cols), bf16), H),
         (sds((cols, 128), f32), H),
-        (sds((reps - 1, cols, 128), f32), H),
+        (sds((reps - 1, cols, 128), bf16), H),
         (sds((1, width), f32), V),
     )
     big = V((rows, ch), f32)
@@ -921,8 +978,10 @@
         V((SMALL_ROWS, ch), f32),
         V((reps, SMALL_ROWS, cols), f32),
         V((reps, cols, 128), f32),
-        V((6, 8, width), f32),
-        V((3 + reps, 8, width), f32),
+        V((reps, SMALL_ROWS, cols), bf16),
+        V((reps, cols, 128), bf16),
+        V((6, 1, width), f32),
+        V((3 + reps, 1, width), f32),
     ) + REDUCE_SCRATCH * 4
     copies = 120 + 10 * (reps - 1)
     return fused(partial(block_kernel, reps), 1, copies, 12, outs, args, scratch)

time: 169 us -> 152 us (0.90)
  Pallas kernels: 168 us -> 150 us
    pallas_call x1, Pallas kernels: 165 us -> 147 us  [fused(): pl.pallas_call(kernel, out_shape=tuple((o for o, _ in outs)), in_specs=[p...]
where the time goes in v5:
time: 152 us
  Pallas kernels  150 us (99%)
    pallas_call x1, Pallas kernels, fused(): pl.pallas_call(kernel, out_shape=tuple((o for o, _ in outs)), in_specs=[p...  147 us
    pallas_call x1, Pallas kernels, place(): pl.pallas_call(partial(place_kernel, reps), out_shape=outs, in_specs=[pl....  3.19 us

profile of v5, /device:TPU:0, one launch (start us, length us, event | category | flops | bytes accessed | tf_op | source)
XLA Modules:
  0.0 151.6 jit_solution(14015626446757926298)
XLA Ops:
  0.6 0.7 pad_add_fusion.index
  1.3 146.9 %shard_map.237 = (bf16[64,1536]{1,0:T(8,128)(2,1)}, f32[64,1536]{1,0:T(8,128)}, bf16[192,768]{1,0:T(8,128)(2,1)}, bf16[1,192,768]{2,1,0:T(8,128)(2,1)}, bf16[192...) custom-call(s32[2,2]{1,0:T(2,128)} %refs_0_.1, ...), custom_call_target="tpu_custom_call" | custom-call | tf_op jit(solution)/shard_map/pallas_call | solution.py:285
  148.2 3.2 %shard_map.238 = (bf16[64,1536]{1,0:T(8,128)(2,1)}, f32[64,1536]{1,0:T(8,128)}, f32[1,48]{1,0:T(1,128)}, f32[192,768]{1,0:T(8,128)}, f32[192,768]{1,0:T(8,128)},...) custom-call(s32[2]{0:T(128)} %pad_add_fusion.index, ...), custom_call_target="tpu_custom_call" | custom-call | tf_op jit(solution)/shard_map/pallas_call | solution.py:1055

commit v6 on v5

--- a/solution.py
+++ b/solution.py
@@ -304,8 +304,8 @@
         return out
 
     (
-        grids, gain_own, wstep_own, taps_own, bias_own, step_own, skip_own, decay_own, wstate_own, wout_own,
-        cot_own, tokens, wx_own, wz_own,
+        grids, gain_own, wstep_own, taps_own, bias_own, step_own, skip_own, decay_own, wstate_own, wout_hbm,
+        cot_hbm, tokens, wx_own, wz_own,
     ) = take_refs(14)
     (
         mixed, grad_tokens, wx_mine, wx_theirs, wz_mine, wz_theirs, out_mine, out_theirs, rows_mine,
@@ -319,7 +319,7 @@
     (
         hprev, step, decay_step, u, state, acc_ref, rate_ref, s1, s2, pb, pc, ones, bias_acc, skip_acc, g,
     ) = take_refs(15)
-    (y_send, y_in, g_send, g_in, gated, gate_both, cot, mixed_core, mixed_low, mixed_z, mixed_sum, tok_last) = take_refs(12)
+    (y_send, y_in, g_send, g_in, gated, gate_both, cot, mixed_core, mixed_low, mixed_z, mixed_sum, tok_last, wout_own, cot_own) = take_refs(14)
     (out_send, out_y, out_low, out_x_in, out_all, wz_low, part_back, grad_proj, sums, gx, gx_in) = take_refs(11)
     (wx_low, rows_grad, rows_part, state_part, rows_low, state_low, gain_acc, gain_in) = take_refs(8)
     reduces = [take_refs(3) for _ in range(4)]
@@ -332,7 +332,7 @@
     j = z * 2 + i
     cols, width = wx_own.shape
     ch = reps * cols
-    piece = wout_own.shape[0]
+    piece = wout_hbm.shape[0]
     half = TP * HALF
     rounds = HALF // CHUNK
     size = CHUNK * 8
@@ -343,6 +343,7 @@
 
     own_loads = [net.load(tokens.at[pl.ds(h * HALF, HALF)], tok.at[h, z, i]) for h in range(2)]
     own_loads += [net.load(wx_own, wx_all.at[yi]), net.load(wz_own, wz_all.at[yi])]
+    own_loads += [net.load(wout_hbm, wout_own), net.load(cot_hbm, cot_own)]
     own_loads += [net.load(tokens.at[pl.ds(pl.multiple_of(gh * HALF, HALF), HALF)], tok_last)]
     first_end = (grids[0, 0] * grids[0, 1]).astype(f32)
     second_end = first_end + (grids[1, 0] * grids[1, 1]).astype(f32)
@@ -367,7 +368,7 @@
         for ref in (small_all, wstate_all):
             first_y.append(net.copy(ref.at[yi], ref.at[yi], net.along_y(d)))
     cot_mine = span(j, HALF)
-    cot_x = net.copy(cot_own, cot.at[cot_mine], net.over_x())
+    cot_x = net.copy(cot_hbm, cot.at[cot_mine], net.over_x())
     for c in metas:
         c.wait_recv()
     meta_y = [net.copy(meta_all.at[yi], meta_all.at[yi], net.along_y(d)) for d in range(1, reps)]
@@ -380,10 +381,6 @@
         both = meta_all[yi, b].astype(f32)
         ends_ref[0, b : b + 1, :] = both[1:2, :]
         ends_ref[1, b : b + 1, :] = both[2:3, :]
-    for p in range(TP * reps):
-        zp, yp, ip = p // (2 * reps), (p // 2) % reps, p % 2
-        wout_send[zp * 2 + ip, :, yp * cols : (yp + 1) * cols] = wout_own[:, p * cols : (p + 1) * cols]
-    wout_in[j, own_part] = wout_send[j, own_part]
     source = lax.broadcasted_iota(jnp.int32, (STATE * 128, 128), 0) // 128
     target = lax.broadcasted_iota(jnp.int32, (STATE * 128, 128), 1)
     ones[...] = (target == DT_RANK + source).astype(f32).astype(bf16)
@@ -391,6 +388,10 @@
     state[...] = jnp.zeros_like(state)
     for c in own_loads:
         c.wait()
+    for p in range(TP * reps):
+        zp, yp, ip = p // (2 * reps), (p // 2) % reps, p % 2
+        wout_send[zp * 2 + ip, :, yp * cols : (yp + 1) * cols] = wout_own[:, p * cols : (p + 1) * cols]
+    wout_in[j, own_part] = wout_send[j, own_part]
 
     from_x = []
     for m in range(1, ZS):
@@ -402,7 +403,16 @@
         zm, im = net.shared(m)
         wout_z.append(net.copy(wout_send.at[zm * 2 + im, own_part], wout_in.at[j, own_part], net.to_shared(m)))
     cot_x.wait_recv()
-    cot_z = net.gather_z(cot.at[cot_mine], lambda zz: cot.at[span(zz * 2 + i, HALF)])
+
+    def gather_cot(part):
+        rows = lambda zz: cot.at[span((zz * 2 + i) * 2 + part, HALF // 2)]
+        return net.gather_z(rows(z), rows)
+
+    def pass_cot(part, m):
+        there = cot_zs[part].wait(m)
+        cot_core.append(net.copy(there, there, net.sibling()))
+
+    cot_zs = [gather_cot(0)]
     cot_core = [net.copy(cot.at[cot_mine], cot.at[cot_mine], net.sibling())]
     for c in meta_y + first_y:
         c.wait_recv()
@@ -471,6 +481,9 @@
         c.wait_recv()
     wout_x = [net.copy(wout_in.at[:, own_part], wout_in.at[:, own_part], net.over_x())] if share else []
     sum_first.give()
+    cot_zs.append(gather_cot(1))
+    pass_cot(0, 1)
+    pass_cot(0, 2)
     for c in core_last:
         c.wait_recv()
     take(gh)
@@ -484,12 +497,13 @@
     rate_ref[...] = -LOG2E * jnp.exp(small[DT_RANK:, :].astype(f32)[DECAY_ROW - DT_RANK : DECAY_ROW - DT_RANK + STATE, :])
     y = g
 
-    def prepare(block):
+    def prepare(block, first):
         rows = span(block, size)
         pre = mm(proj_low[rows, :], wstep) + step_bias
-        step_all = softplus(pre)
+        if first:
+            step[rows, :] = softplus(pre)
+        step_all = step[rows, :]
         values = conv_out[rows, :]
-        step[...] = step_all
         u[...] = step_all * values
         for k in range(CHUNK):
             t = block * CHUNK + k
@@ -504,7 +518,7 @@
 
     def forward(c, carry):
         block = c + s * (2 * rounds - 1 - 2 * c)
-        rows, _, values = prepare(block)
+        rows, _, values = prepare(block, True)
         y[rows, :] = skip * values
         for n0 in range(0, STATE, NSTEP):
             rate = rates(n0)
@@ -532,6 +546,12 @@
                 state[n0 + m] = hs[m]
         return carry
 
+    def send_readout(n):
+        at = n + s * (rounds - 1 - 2 * n)
+        rows = span(at, size)
+        y_send[rows, :] = y[span(s * rounds + at, size), :].astype(bf16)
+        return net.copy(y_send.at[rows], y_in.at[rows], net.over_x())
+
     sum_last.across_z()
     for c in wout_x:
         c.wait_recv()
@@ -539,13 +559,13 @@
     wout_all[yi] = wout_in[...]
     lax.fori_loop(0, rounds // 2, forward, 0)
     sum_last.give()
-    for m in (1, 2):
-        there = cot_z.wait(m)
-        cot_core.append(net.copy(there, there, net.sibling()))
+    y_copies = [send_readout(n) for n in range(rounds // 2)]
     lax.fori_loop(rounds // 2, rounds, forward, 0)
-    y_send[...] = y[first_rows, :].astype(bf16)
-    y_copy = net.copy(y_send, y_in, net.over_x())
+    y_copies += [send_readout(n) for n in (rounds // 2, rounds - 1)]
+    pass_cot(0, 3)
     sum_last.end()
+    pass_cot(1, 1)
+    pass_cot(1, 2)
     proj[last_rows, :] = proj_low[last_rows, :].astype(f32)
     for c in late_y:
         c.wait_recv()
@@ -553,15 +573,14 @@
         wz[r * cols : (r + 1) * cols, :] = wz_all[r]
     gate_in[...] = mm_nt(normed[gh], wz[...])
     lax.fori_loop(rounds, 2 * rounds - 1, forward, 0)
-    there = cot_z.wait(3)
-    cot_core.append(net.copy(there, there, net.sibling()))
     lax.fori_loop(2 * rounds - 1, 2 * rounds, forward, 0)
     for c in wout_y:
         c.wait_recv()
     for p in range(TP * reps):
         zp, yp, ip = p // (2 * reps), (p // 2) % reps, p % 2
         wout[p * piece : (p + 1) * piece, :] = wout_all[yp, zp * 2 + ip]
-    y_copy.wait_recv()
+    for c in y_copies:
+        c.wait_recv()
 
     summed = y[last_rows, :] + y_in[...].astype(f32)
     raw[...] = jnp.swapaxes(summed.reshape(HALF, 8, ch), 0, 1).reshape(half, ch)
@@ -587,6 +606,7 @@
         c.wait_send()
     lax.fori_loop(0, ZS, gate_rows, 0)
     mixed_copy = net.copy(tok.at[gh, :, 1 - i], mixed_core, net.sibling())
+    pass_cot(1, 3)
     for c in cot_core:
         c.wait_recv()
     lax.fori_loop(0, ZS, grad_rows, 0)
@@ -607,7 +627,7 @@
 
     def backward(c, carry):
         block = (1 - s) * (2 * rounds - 1 - c) + s * c
-        rows, pre, values = prepare(block)
+        rows, pre, values = prepare(block, False)
         s1[...] = jnp.zeros_like(s1)
         s2[...] = jnp.zeros_like(s2)
         for n0 in range(0, STATE, NSTEP):
@@ -621,7 +641,7 @@
                 pv = proj[rows8(t), :]
                 gv = g[rows8(t), :]
                 uv = u[here, :]
-                stv = step[here, :]
+                stv = step[rows8(t), :]
                 st = decay_step[here, :]
                 one = s1[here, :]
                 two = s2[here, :]
@@ -666,7 +686,7 @@
         )
         read_part = jnp.where(lane >= DT_RANK + STATE, pltpu.roll(read_part, STATE, 1), 0.0)
         part_back[rows, :] = mm_nt(q_low, wstep) + mm(pb[...].astype(bf16), ones[...]) + read_part
-        g[rows, :] = gv * skip + step[...] * one
+        g[rows, :] = gv * skip + step[rows, :] * one
         return carry
 
     lax.fori_loop(0, 1, backward, 0)
@@ -751,14 +771,6 @@
     mixed_sum[...] = (total + tok_last[...].astype(f32)).astype(bf16)
     net.copy(mixed_sum, mixed, net.over_x())
     back_first.give()
-    gate_copy.wait_recv()
-    part_z = mm_tn(gate_both[0], normed[0, :, half_cols]) + mm_tn(gate_both[1], normed[1, :, half_cols])
-    for r in range(reps):
-        wz_low[r] = part_z[r * cols : (r + 1) * cols].astype(bf16)
-    for d in range(1, reps):
-        net.copy(wz_low.at[net.y_at(d)], wz_theirs.at[d - 1], net.along_y(d))
-    net.save(wz_low.at[yi], wz_mine)
-    back_first.end()
     out_half = out_low
     if share:
         out_x.wait_recv()
@@ -769,23 +781,44 @@
     for m in range(1, TP):
         zm, im = net.shared(m)
         out_zs.append(net.copy(out_half.at[zm * 2 + im], out_all.at[j], net.to_shared(m)))
+    gate_copy.wait_recv()
+    part_z = mm_tn(gate_both[0], normed[0, :, half_cols]) + mm_tn(gate_both[1], normed[1, :, half_cols])
+    for r in range(reps):
+        wz_low[r] = part_z[r * cols : (r + 1) * cols].astype(bf16)
+    for d in range(1, reps):
+        net.copy(wz_low.at[net.y_at(d)], wz_theirs.at[d - 1], net.along_y(d))
+    net.save(wz_low.at[yi], wz_mine)
+    back_first.end()
     pull(s)
     gx_first = convolve_back(s)
 
-    def rows_of(q, carry):
+    def rows_of(q):
         rows = span(q, PACK)
+        both = gx[s, rows, :].astype(f32) + gx_in[s, rows, :].astype(f32)
         value = (
-            mm(gx[s, rows, :], wx[...]) + mm(gx_in[s, rows, :], wx[...]) + mm(gate_both[s, rows, :], wz[...])
+            mm(both.astype(bf16), wx[...]) + mm(gate_both[s, rows, :], wz[...])
         )
         tok[gh, q] = value.astype(bf16).reshape(2, HALF, width)
-        return carry
+        return net.copy(tok.at[gh, q, 1 - i], mixed_core.at[q], net.sibling())
+
+    def send_on(m, c):
+        q = net.flip(m)
+        c.wait_recv()
+        mixed_low[q] = (tok[gh, q, i].astype(f32) + mixed_core[q].astype(f32)).astype(bf16)
+        to_z.append(net.copy(mixed_low.at[q], mixed_z.at[m - 1], net.along_z(m)))
 
     mixed_copy.wait_send()
-    gx_last.wait_recv()
-    lax.fori_loop(0, ZS, rows_of, 0)
-    to_core = net.copy(tok.at[gh, :, 1 - i], mixed_core, net.sibling())
     for c in mixed_zs:
         c.wait_send()
+    gx_last.wait_recv()
+    to_z = []
+    far = rows_of(net.flip(2))
+    middle = rows_of(net.flip(3))
+    send_on(2, far)
+    near = rows_of(net.flip(1))
+    send_on(3, middle)
+    to_core = rows_of(z)
+    send_on(1, near)
     def gain_terms(q, carry):
         x = tok[s, q].astype(f32).reshape(PACK, width)
         inv = lax.rsqrt(jnp.mean(x * x, axis=1, keepdims=True) + EPS)
@@ -817,10 +850,6 @@
         gain_acc[k + 1] = total
 
     cs = gain_start(0)
-    to_core.wait_recv()
-    for q in range(ZS):
-        mixed_low[q] = (tok[gh, q, i].astype(f32) + mixed_core[q].astype(f32)).astype(bf16)
-    to_z = [net.copy(mixed_low.at[net.flip(m)], mixed_z.at[m - 1], net.along_z(m)) for m in range(1, ZS)]
     state_all = mm_tn(conv_out[...].astype(bf16), grad_proj[...])
     rows_grad[STEP_ROW : STEP_ROW + 1, :] = jnp.sum(bias_acc[...], axis=0, keepdims=True)
     rows_grad[SKIP_ROW : SKIP_ROW + 1, :] = jnp.sum(skip_acc[...], axis=0, keepdims=True)
@@ -864,9 +893,11 @@
     unit = x * inv
     gain_end(3, cs)
     cs = gain_start(4)
+    to_core.wait_recv()
     grad = tok[gh, z, i].astype(f32) + mixed_core[z].astype(f32)
+    for c in to_z:
+        c.wait_recv()
     for m in range(1, ZS):
-        to_z[m - 1].wait_recv()
         grad = grad + mixed_z[m - 1].astype(f32)
     scaled = grad * gain[...]
     mean = jnp.mean(scaled * unit, axis=1, keepdims=True)
@@ -887,8 +918,8 @@
     sds = jax.ShapeDtypeStruct
     V, H = pltpu.VMEM, pl.ANY
     args = [(grids, pltpu.SMEM)]
-    args += [(a, V) for a in (gain, wstep, taps, bias, step, skip, decay, wstate, wout, cot)]
-    args += [(a, H) for a in (tokens, wx, wz)]
+    args += [(a, V) for a in (gain, wstep, taps, bias, step, skip, decay, wstate)]
+    args += [(a, H) for a in (wout, cot, tokens, wx, wz)]
     outs = (
         (sds((HALF, width), bf16), H),
         (sds((HALF, width), f32), V),
@@ -937,7 +968,7 @@
         V((rows, 128), bf16),
         part,
         V((PACK, STATE // 2, 16, ch), bf16),
-        round_rows,
+        big,
         round_rows,
         round_rows,
         state,
@@ -963,6 +994,8 @@
         V((ZS - 1, HALF, width), bf16),
         V((HALF, width), bf16),
         V((HALF, width), bf16),
+        V((piece, TP * ch), bf16),
+        V((HALF, width), bf16),
         V((reps, TP * piece, ch), bf16),
         V((reps - 1, TP * piece, ch), bf16),
         V((TP, piece, ch), bf16),
@@ -983,19 +1016,21 @@
         V((6, 1, width), f32),
         V((3 + reps, 1, width), f32),
     ) + REDUCE_SCRATCH * 4
-    copies = 120 + 10 * (reps - 1)
-    return fused(partial(block_kernel, reps), 1, copies, 12, outs, args, scratch)
+    copies = 160 + 12 * (reps - 1)
+    return fused(partial(block_kernel, reps), 1, copies, 16, outs, args, scratch)
 
 
 def place_kernel(
-    reps, index, mixed_in, tokens_in, wx_mine, wx_theirs, wz_mine, wz_theirs, out_mine, out_theirs,
+    reps, mixed_in, tokens_in, wx_mine, wx_theirs, wz_mine, wz_theirs, out_mine, out_theirs,
     rows_mine, rows_theirs, state_mine, state_theirs, gain_in,
     mixed, grad_tokens, gain, wx, wz, wout, taps, bias, wstate, wstep, step, decay, skip,
 ):
     mixed[...] = mixed_in[...]
     grad_tokens[...] = tokens_in[...]
     width, n = gain_in.shape[1], gain.shape[1]
-    moved = pltpu.roll(jnp.broadcast_to(gain_in[...], (8, width)), width - index[0] * n, 1)
+    s = lax.axis_index("dir")
+    index = s * (TP * reps) + lax.axis_index("dp")
+    moved = pltpu.roll(jnp.broadcast_to(gain_in[...], (8, width)), width - index * n, 1)
     gain[...] = moved[0:1, 0:n]
 
     def total(mine, theirs):
@@ -1009,7 +1044,6 @@
     cols = wx.shape[0]
     hp = out_mine.shape[1]
     share = hp < wout.shape[0]
-    s = index[1]
     for q in range(ZS):
         parts = [(out_mine[q].astype(f32), s), (out_theirs[q].astype(f32), 1 - s)]
         if not share:
@@ -1029,7 +1063,7 @@
     wstate[...] = total(state_mine, state_theirs)
 
 
-def place(reps, index, results):
+def place(reps, results):
     mixed, grad_tokens, wx = results[0], results[1], results[2]
     ch = results[6].shape[2]
     cols = wx.shape[0]
@@ -1055,10 +1089,10 @@
     return pl.pallas_call(
         partial(place_kernel, reps),
         out_shape=outs,
-        in_specs=[pl.BlockSpec(memory_space=pltpu.SMEM)] + [V] * len(results),
+        in_specs=[V] * len(results),
         out_specs=tuple([V] * len(outs)),
         compiler_params=pltpu.CompilerParams(vmem_limit_bytes=63 << 20),
-    )(index, *results)
+    )(*results)
 
 
 def local(
@@ -1071,12 +1105,10 @@
         decay_log[0], proj_state[0], proj_out.T, grad_out.reshape(HALF, width), tokens, proj_in_x.T,
         proj_in_z.T,
     )
-    s = lax.axis_index("dir")
-    index = jnp.stack([s * lax.axis_size("dp") + lax.axis_index("dp"), s]).astype(jnp.int32)
     (
         mixed, grad_tokens, grad_gain, grad_wx, grad_wz, grad_wout, grad_taps, grad_bias, grad_wstate,
         grad_wstep, grad_step, grad_decay, grad_skip,
-    ) = place(reps, index, results)
+    ) = place(reps, results)
     return (
         mixed.reshape(1, 1, HALF, width),
         grad_tokens.reshape(1, 1, HALF, width),

time: 152 us -> 144 us (0.947)
  Pallas kernels: 150 us -> 143 us
    pallas_call x1, Pallas kernels: 147 us -> 140 us  [fused(): pl.pallas_call(kernel, out_shape=tuple((o for o, _ in outs)), in_specs=[p...]
where the time goes in v6:
time: 144 us
  Pallas kernels  143 us (99%)
    pallas_call x1, Pallas kernels, fused(): pl.pallas_call(kernel, out_shape=tuple((o for o, _ in outs)), in_specs=[p...  140 us
    pallas_call x1, Pallas kernels, place(): pl.pallas_call(partial(place_kernel, reps), out_shape=outs, in_specs=[V]...  3.18 us

profile of v6, /device:TPU:0, one launch (start us, length us, event | category | flops | bytes accessed | tf_op | source)
XLA Modules:
  0.0 143.7 jit_solution(2716147284411811705)
XLA Ops:
  0.7 139.7 %shard_map.237 = (bf16[64,1536]{1,0:T(8,128)(2,1)}, f32[64,1536]{1,0:T(8,128)}, bf16[192,768]{1,0:T(8,128)(2,1)}, bf16[1,192,768]{2,1,0:T(8,128)(2,1)}, bf16[192...) custom-call(s32[2,2]{1,0:T(2,128)} %refs_0_.1, ...), custom_call_target="tpu_custom_call" | custom-call | tf_op jit(solution)/shard_map/pallas_call | solution.py:285
  140.3 3.2 %shard_map.238 = (bf16[64,1536]{1,0:T(8,128)(2,1)}, f32[64,1536]{1,0:T(8,128)}, f32[1,48]{1,0:T(1,128)}, f32[192,768]{1,0:T(8,128)}, f32[192,768]{1,0:T(8,128)},...) custom-call(bf16[64,1536]{1,0:T(8,128)(2,1)} %get-tuple-element.39.m, ...), custom_call_target="tpu_custom_call" | custom-call | tf_op jit(solution)/shard_map/pallas_call | solution.py:1089

commit v7 on v6

--- a/solution.py
+++ b/solution.py
@@ -476,12 +476,12 @@
     last_tokens(1)
     sum_first.across_z()
     last_tokens(2)
+    sum_first.give()
+    cot_zs.append(gather_cot(1))
     last_tokens(3)
     for c in wout_z:
         c.wait_recv()
     wout_x = [net.copy(wout_in.at[:, own_part], wout_in.at[:, own_part], net.over_x())] if share else []
-    sum_first.give()
-    cot_zs.append(gather_cot(1))
     pass_cot(0, 1)
     pass_cot(0, 2)
     for c in core_last:

time: 144 us -> 144 us (level)
  no operation moved by 1% of the time
where the time goes in v7:
time: 144 us
  Pallas kernels  143 us (99%)
    pallas_call x1, Pallas kernels, fused(): pl.pallas_call(kernel, out_shape=tuple((o for o, _ in outs)), in_specs=[p...  140 us
    pallas_call x1, Pallas kernels, place(): pl.pallas_call(partial(place_kernel, reps), out_shape=outs, in_specs=[V]...  3.18 us

profile of v7, /device:TPU:0, one launch (start us, length us, event | category | flops | bytes accessed | tf_op | source)
XLA Modules:
  0.0 144.2 jit_solution(5003775300528770051)
XLA Ops:
  0.7 140.1 %shard_map.237 = (bf16[64,1536]{1,0:T(8,128)(2,1)}, f32[64,1536]{1,0:T(8,128)}, bf16[192,768]{1,0:T(8,128)(2,1)}, bf16[1,192,768]{2,1,0:T(8,128)(2,1)}, bf16[192...) custom-call(s32[2,2]{1,0:T(2,128)} %refs_0_.1, ...), custom_call_target="tpu_custom_call" | custom-call | tf_op jit(solution)/shard_map/pallas_call | solution.py:285
  140.8 3.2 %shard_map.238 = (bf16[64,1536]{1,0:T(8,128)(2,1)}, f32[64,1536]{1,0:T(8,128)}, f32[1,48]{1,0:T(1,128)}, f32[192,768]{1,0:T(8,128)}, f32[192,768]{1,0:T(8,128)},...) custom-call(bf16[64,1536]{1,0:T(8,128)(2,1)} %get-tuple-element.39.m, ...), custom_call_target="tpu_custom_call" | custom-call | tf_op jit(solution)/shard_map/pallas_call | solution.py:1089
